TPU v7x, 512 devices: a whole 4x8x8 slice. The times are simulated.
512 devices in a mesh: expert: 64 (over y, z), tensor: 8 (over x, core).
Axes of the slice: x: 4, y: 8, z: 8, core: 2. Of those that a mesh axis runs over, the one named last changes fastest.
Arguments:
- grad_out: bfloat16 [4096, 6144], P('expert', 'tensor'), may hold values from -3 to 3
- routes: int32 [4096, 2], P('expert'), may hold values from 0 to 7, all different within a row; in each aligned block of 64 rows (0 to 63, 64 to 127, ...) at most 24 rows name the same one
- gates: bfloat16 [4096, 2], P('expert'), may hold values from 0.099609375 to 1
- w_down: bfloat16 [65536, 6144], P('expert', 'tensor'), may hold values from -0.0625 to 0.0625
- gate_pre: bfloat16 [1536, 65536], P(None, ('expert', 'tensor')), may hold values from -5 to 5
- up_pre: bfloat16 [1536, 65536], P(None, ('expert', 'tensor')), may hold values from -5 to 5
Outputs:
- w_down_grad: bfloat16 [65536, 6144], P('expert', 'tensor')
- gate_pre_grad: bfloat16 [1536, 65536], P(None, ('expert', 'tensor'))
- up_pre_grad: bfloat16 [1536, 65536], P(None, ('expert', 'tensor'))
- gate_grad: float32 [4096, 2], P('expert')
Inputs may be any that keep to these rules, and one draw needn't show every extreme that they name: `routes`: among the 64 tokens of one index of expert, no expert is named more than 24 times, a bound that some block reaches. The two experts of a token differ.
All inputs are finite; a program needn't handle non-finite values.
Results may differ from a plain program's by a relative error of at most 0.019.
Values may be sent and summed in bfloat16 or wider, within the bound.
No kernel may reach another device: no remote copies, remote signals or barrier semaphores. Data moves between devices by JAX's collectives and lax.ppermute only.
A program may use at most 64 MiB of HBM per device.

v0:
```python
import jax
import jax.numpy as jnp
from jax import lax
from jax.sharding import PartitionSpec as P

EXPERTS = 8
TOP = 2
CAP = 24


def per_device(grad_out, routes, gates, w_down, gate_pre, up_pre):
    replicas = lax.axis_size("expert") // EXPERTS
    col_width = grad_out.shape[1]
    flat_routes = routes.reshape(-1)
    matches = flat_routes[:, None] == jnp.arange(EXPERTS, dtype=jnp.int32)[None, :]
    ranking = jnp.sum(
        jnp.where(matches, jnp.cumsum(matches.astype(jnp.int32), axis=0) - 1, 0), axis=1
    )
    targets = jnp.arange(EXPERTS * CAP, dtype=jnp.int32)
    target_expert = targets // CAP
    target_rank = targets % CAP
    selector = (
        (flat_routes[None, :] == target_expert[:, None])
        & (ranking[None, :] == target_rank[:, None])
    ).astype(jnp.bfloat16)
    pair_rows = jnp.repeat(grad_out, TOP, axis=0)
    packed = jnp.dot(selector, pair_rows, preferred_element_type=jnp.float32).astype(jnp.bfloat16)
    packed_gates = jnp.dot(selector, gates.reshape(-1), preferred_element_type=jnp.float32).astype(
        jnp.bfloat16
    )
    send_rows = jnp.repeat(packed.reshape(EXPERTS, CAP, col_width), replicas, axis=0)
    send_gates = jnp.repeat(packed_gates.reshape(EXPERTS, CAP), replicas, axis=0)
    got_rows, got_gates = (
        lax.all_to_all(send_rows, "expert", split_axis=0, concat_axis=0, tiled=True),
        lax.all_to_all(send_gates, "expert", split_axis=0, concat_axis=0, tiled=True),
    )
    slot_count = got_rows.shape[0] * CAP
    slot_rows = got_rows.reshape(slot_count, col_width)
    slot_gates = got_gates.reshape(slot_count).astype(jnp.float32)
    hidden_grad = (
        lax.psum_scatter(
            lax.dot_general(
                w_down, slot_rows, (((1,), (1,)), ((), ())), preferred_element_type=jnp.float32
            ).astype(jnp.bfloat16),
            "tensor",
            scatter_dimension=0,
            tiled=True,
        )
        .astype(jnp.float32)
        .T
    )
    gate_act = gate_pre.astype(jnp.float32)
    up_act = up_pre.astype(jnp.float32)
    logistic = jax.nn.sigmoid(gate_act)
    swish_out = gate_act * logistic
    hidden = swish_out * up_act
    scale = slot_gates[:, None]
    gate_pre_grad = (
        scale * hidden_grad * up_act * logistic * (1.0 + gate_act * (1.0 - logistic))
    ).astype(jnp.bfloat16)
    up_pre_grad = (scale * hidden_grad * swish_out).astype(jnp.bfloat16)
    scaled_hidden = (scale * hidden).astype(jnp.bfloat16)
    w_down_grad = lax.dot_general(
        lax.all_gather(scaled_hidden, "tensor", axis=1, tiled=True),
        slot_rows,
        (((0,), (0,)), ((), ())),
        preferred_element_type=jnp.float32,
    ).astype(jnp.bfloat16)
    slot_dots = jnp.sum(hidden * hidden_grad, axis=1)
    selector_wide = selector.astype(jnp.float32)
    summed = lax.psum(slot_dots, "tensor")
    returned = lax.all_to_all(
        summed.reshape(-1, CAP), "expert", split_axis=0, concat_axis=0, tiled=True
    )
    totals = jnp.sum(returned.reshape(EXPERTS, replicas, CAP), axis=1).reshape(-1)
    gate_grad = jnp.dot(totals, selector_wide, precision=lax.Precision.HIGHEST)
    return (w_down_grad, gate_pre_grad, up_pre_grad, gate_grad.reshape(routes.shape))


def solution(mesh):
    return jax.shard_map(
        per_device,
        mesh=mesh,
        in_specs=(
            P("expert", "tensor"),
            P("expert", None),
            P("expert", None),
            P("expert", "tensor"),
            P(None, ("expert", "tensor")),
            P(None, ("expert", "tensor")),
        ),
        out_specs=(
            P("expert", "tensor"),
            P(None, ("expert", "tensor")),
            P(None, ("expert", "tensor")),
            P("expert", None),
        ),
        check_vma=False,
    )
```

profile of v0, /device:TPU:1, one launch (start us, length us, event | category | flops | bytes accessed | tf_op | source)
XLA Modules:
  0.0 199.7 jit_solution(11662699998940303306)
XLA Ops:
  7.2 0.9 copy.20
  8.1 0.1 eq.69
  8.4 0.2 reduce_window_sum.11
  8.5 0.2 select_reduce_fusion
  8.7 1.0 broadcast_in_dim.20
  9.8 0.3 convolution_convert_fusion.2
  10.1 0.2 broadcast_in_dim.21
  10.3 75.3 %all_to_all.23 = bf16[64,24,768]{2,1,0:T(8,128)(2,1)S(1)} all-to-all(bf16[64,24,768]{2,1,0:T(8,128)(2,1)S(1)} %bitcast.34), channel_id=1, replica_groups=mesh['expert'=64,'tensor'=8] {'expert'}, dimensions={0} | all-to-all | bytes 4718592 | tf_op jit(solution)/shard_map/all_to_all | solution.py:34
  85.5 1.4 copy-done.1
  86.9 4.1 %fusion = bf16[1024,1536]{0,1:T(8,128)(2,1)} fusion(bf16[1536,768]{1,0:T(8,128)(2,1)S(1)} %bitcast.35, bf16[1024,768]{1,0:T(8,128)(2,1)S(1)} %copy-done), kind=kOutput, calls=%fused_computation.1 | convolution fusion | flops 2417491968 | bytes 7077888 | tf_op jit(solution)/shard_map/dot_general | solution.py:42
  91.1 4.6 %copy.27 = bf16[1024,1536]{1,0:T(8,128)(2,1)} copy(bf16[1024,1536]{0,1:T(8,128)(2,1)} %fusion) | data formatting | bytes 6291456
  95.8 0.6 copy-done.4
  96.5 0.1 reshape.104
  96.6 0.2 fusion.13
  97.0 20.9 %all_to_all.24 = bf16[64,1,24]{2,1,0:T(2,128)(2,1)S(1)} all-to-all(bf16[64,1,24]{2,1,0:T(2,128)(2,1)S(1)} %copy.22), channel_id=1, replica_groups=mesh['expert'=64,'tensor'=8] {'expert'}, dimensions={0} | all-to-all | bytes 6144 | tf_op jit(solution)/shard_map/all_to_all | solution.py:35
  118.1 16.6 %reduce-scatter.4.cloned.1.call-done = bf16[128,1536]{1,0:T(8,128)(2,1)} async-done(((bf16[1024,1536]{1,0:T(8,128)(2,1)}), bf16[128,1536]{1,0:T(8,128)(2,1)}) %reduce-scatter.4.cloned.1.call-update) | async-done | bytes 393232
  134.7 1.2 copy.28
  136.0 1.7 fusion.10
  137.9 25.0 %psum.7 = f32[64,1,24]{2,0,1:T(8,128)} all-reduce(f32[64,1,24]{2,0,1:T(8,128)S(1)} %all_to_all.18), channel_id=1, replica_groups=mesh['expert'=64,'tensor'=8] {'tensor'}, use_global_device_ids=true, to_apply=%region_4.5 | all-reduce | flops 1536 | bytes 12288 | tf_op jit(solution)/shard_map/psum | solution.py:71
  162.9 11.7 %all-to-all-start.2 = ((f32[64,1,24]{2,1,0:T(1,128)}), f32[64,1,24]{2,1,0:T(1,128)S(1)}, u32[]{:S(2)}, u32[]{:S(2)}) async-start(f32[64,1,24]{2,1,0:T(1,128)} %bitcast.7), calls=%async_computation.2 | async-start | bytes 65536 | tf_op jit(solution)/shard_map/all_to_all | solution.py:72
  174.7 0.2 compare_and_fusion
  174.9 10.6 %all-to-all-done.2 = f32[64,1,24]{2,1,0:T(1,128)S(1)} async-done(((f32[64,1,24]{2,1,0:T(1,128)}), f32[64,1,24]{2,1,0:T(1,128)S(1)}, u32[]{:S(2)}, u32[]{:S(2)}) %all-to-all-start.2) | async-done | bytes 6176 | tf_op jit(solution)/shard_map/all_to_all | solution.py:72
  185.6 0.8 fusion.11
  186.4 6.4 %convolution_convert_fusion.1 = bf16[1024,768]{1,0:T(8,128)(2,1)} fusion(bf16[1536,1024]{1,0:T(8,128)(2,1)} %all-gather.2.cloned.1.call-done, bf16[1536,768]{1,0:T(8,128)(2,1)} %bitcast.36), kind=kOutput, calls=%fused_computation.2 | convolution fusion | flops 2416705536 | bytes 7077888 | tf_op jit(solution)/shard_map/dot_general | solution.py:63
  (27 shorter events, 1.0 us)
Async XLA Ops:
  7.2 79.8 %copy-start = (bf16[1024,768]{1,0:T(8,128)(2,1)S(1)}, bf16[1024,768]{1,0:T(8,128)(2,1)}, u32[]{:S(2)}) copy-start(bf16[1024,768]{1,0:T(8,128)(2,1)} %param.9) | copy-start | bytes 4718596
  7.2 127.5 %reduce-scatter.4.cloned.1.call-start = ((), (), s32[]{:S(2)}) async-start(), calls=%async_computation.5 | async-start | bytes 3538944
  85.5 1.4 copy-start.1
  95.7 0.7 copy-start.4
  95.7 40.3 %copy-start.2 = (bf16[1536,128]{1,0:T(8,128)(2,1)S(1)}, bf16[1536,128]{1,0:T(8,128)(2,1)}, u32[]{:S(2)}) copy-start(bf16[1536,128]{1,0:T(8,128)(2,1)} %param.11) | copy-start | bytes 1179652
  95.7 40.3 %copy-start.3 = (bf16[1536,128]{1,0:T(8,128)(2,1)S(1)}, bf16[1536,128]{1,0:T(8,128)(2,1)}, u32[]{:S(2)}) copy-start(bf16[1536,128]{1,0:T(8,128)(2,1)} %param.10) | copy-start | bytes 1179652
  95.7 90.6 %all-gather.2.cloned.1.call-start = ((), (), s32[]{:S(2)}) async-start(), calls=%async_computation.4 | async-start | bytes 3538944 | tf_op jit(solution)/shard_map/all_gather | solution.py:64
  162.9 22.6 %all-to-all-start.2 = ((f32[64,1,24]{2,1,0:T(1,128)}), f32[64,1,24]{2,1,0:T(1,128)S(1)}, u32[]{:S(2)}, u32[]{:S(2)}) async-start(f32[64,1,24]{2,1,0:T(1,128)} %bitcast.7), calls=%async_computation.2 | async-start | bytes 65536 | tf_op jit(solution)/shard_map/all_to_all | solution.py:72
Sparse Core Ops, SparseCore 0:
  95.9 38.8 reduce-scatter.3
  137.8 37.9 all-gather.1
where the time goes:
time: 202 us; the launch traced here: 200 us
  blocking collectives  121 us (60%)
  waiting for transfers between devices  27.2 us (13%)
  between operations  14.2 us (7%)
  matrix products  11.9 us (6%)
  starting transfers between devices  11.8 us (6%)
  local copies, waits for them, and re-layouts  10.9 us (5%)
  other arithmetic  2.43 us (1%)
    all_to_all x1, blocking collectives, per_device(): lax.all_to_all(send_rows, 'expert', split_axis=0, concat_axis=0, tiled=True)  75.3 us
    psum x1, blocking collectives, per_device(): summed = lax.psum(slot_dots, 'tensor')  25 us
    all_to_all x1, blocking collectives, per_device(): lax.all_to_all(send_gates, 'expert', split_axis=0, concat_axis=0, tiled=T...  20.9 us
    unnamed x3, waiting for transfers between devices  16.6 us
    all_to_all x1, starting transfers between devices, per_device(): lax.all_to_all(summed.reshape(-1, CAP), 'expert', split_axis=0, concat_ax...  11.7 us
    all_to_all x1, waiting for transfers between devices, per_device(): lax.all_to_all(summed.reshape(-1, CAP), 'expert', split_axis=0, concat_ax...  10.6 us
    unnamed x14, local copies, waits for them, and re-layouts  8.88 us
    dot_general x1, matrix products, per_device(): lax.dot_general(lax.all_gather(scaled_hidden, 'tensor', axis=1, tiled=Tru...  6.45 us
  transfers between devices with their start and end apart: 3, of which 2 were waited for; matrix products, arithmetic and copies ran while one was open for 1% of the time, Pallas kernels for 0%

commit v1 on v0

v1 whole, which is shorter than its diff:
```python
import jax
import jax.numpy as jnp
from jax import lax
from jax.sharding import Mesh
from jax.sharding import PartitionSpec as P

EXPERTS = 8
CAP = 24
BF = jnp.bfloat16
F32 = jnp.float32


def shift(x, axis, step):
    n = lax.axis_size(axis)
    return lax.ppermute(x, axis, [(i, (i + step) % n) for i in range(n)])


def swap(x, axis, mask):
    n = lax.axis_size(axis)
    return lax.ppermute(x, axis, [(i, i ^ mask) for i in range(n)])


def per_device(grad_out, routes, gates, w_down, gate_pre, up_pre):
    ny, nz = lax.axis_size("y"), lax.axis_size("z")
    nx, nc = lax.axis_size("x"), lax.axis_size("c")
    zi, xi, ci = lax.axis_index("z"), lax.axis_index("x"), lax.axis_index("c")
    tokens, width = grad_out.shape
    fb = gate_pre.shape[1]
    block = ny * CAP
    slots = nz * block

    routes_t = routes.T
    gates_t = gates.T.astype(F32)
    named = routes_t[:, None, :] == jnp.arange(EXPERTS, dtype=jnp.int32)[None, :, None]
    member = jnp.any(named, axis=0)
    weight = jnp.sum(jnp.where(named, gates_t[:, None, :], 0.0), axis=0)
    earlier = (
        jnp.arange(tokens, dtype=jnp.int32)[:, None] < jnp.arange(tokens, dtype=jnp.int32)[None, :]
    )
    rank = jnp.dot(member.astype(BF), earlier.astype(BF), preferred_element_type=F32).astype(jnp.int32)
    chosen = member[:, None, :] & (rank[:, None, :] == jnp.arange(CAP, dtype=jnp.int32)[None, :, None])
    selector = jnp.where(chosen, weight[:, None, :], 0.0).astype(BF).reshape(EXPERTS * CAP, tokens)
    packed = jnp.dot(selector, grad_out, preferred_element_type=F32).astype(BF)

    own = lax.all_to_all(
        packed.reshape(EXPERTS, CAP, width), "y", split_axis=0, concat_axis=0, tiled=True
    ).reshape(block, width)
    ahead, behind = [own], [own]
    for _ in range(nz // 2 - 1):
        behind.append(shift(behind[-1], "z", 1))
        ahead.append(shift(ahead[-1], "z", -1))
    half = block // 2
    far_low = shift(behind[-1][:half], "z", 1)
    far_high = shift(ahead[-1][half:], "z", -1)
    rows = jnp.concatenate(ahead + [far_low, far_high] + behind[:0:-1], axis=0)

    def ring_order(a):
        a = a.reshape(ny, nz, CAP, a.shape[1]).transpose(1, 0, 2, 3)
        return jnp.roll(a, -zi, axis=0).reshape(slots, a.shape[3])

    def slot_order(a):
        a = jnp.roll(a.reshape(nz, ny, CAP, a.shape[1]), zi, axis=0)
        return a.transpose(1, 0, 2, 3).reshape(slots, a.shape[3])

    gate_act = ring_order(gate_pre).astype(F32)
    up_act = ring_order(up_pre).astype(F32)
    logistic = jax.nn.sigmoid(gate_act)
    swish_out = gate_act * logistic
    hidden = lax.all_gather((swish_out * up_act).astype(BF), ("x", "c"), axis=1, tiled=True)

    def units(i, j):
        return lax.dynamic_slice_in_dim(w_down, ((xi ^ i) * nc + (ci ^ j)) * fb, fb, 0)

    w_other = jnp.concatenate([units(i, 1) for i in range(nx)], axis=0)
    w_own = jnp.concatenate([units(i, 0) for i in range(nx)], axis=0)

    def product(w):
        return lax.dot_general(rows, w, (((1,), (1,)), ((), ())), preferred_element_type=F32)

    got = swap(product(w_other).astype(BF), "c", 1)
    part = product(w_own) + got.astype(F32)
    hs = slots // 2
    pa, pb = part[:hs], part[hs:]

    def cols(a, i, n=1):
        return a[:, i * fb : (i + n) * fb]

    ga = swap(cols(pa, 1, 2).astype(BF), "x", 1).astype(F32)
    gb = swap(cols(pb, 2, 2).astype(BF), "x", 3).astype(F32)
    qa0, qa3 = cols(pa, 0) + cols(ga, 0), cols(pa, 3) + cols(ga, 1)
    qb0, qb1 = cols(pb, 0) + cols(gb, 1), cols(pb, 1) + cols(gb, 0)
    ga = swap(qa3.astype(BF), "x", 3).astype(F32)
    gb = swap(qb1.astype(BF), "x", 1).astype(F32)
    hidden_grad = jnp.concatenate([qa0 + ga, qb0 + gb], axis=0)

    gate_pre_grad = slot_order(
        (hidden_grad * up_act * logistic * (1.0 + gate_act * (1.0 - logistic))).astype(BF)
    )
    up_pre_grad = slot_order((hidden_grad * swish_out).astype(BF))

    w_down_grad = lax.dot_general(
        hidden, rows, (((0,), (0,)), ((), ())), preferred_element_type=F32
    ).astype(BF)

    outputs = jnp.dot(hidden, w_down, preferred_element_type=F32)
    dots = jnp.sum(rows.astype(F32) * outputs, axis=1)
    dots = lax.psum(dots, ("x", "c"))
    dots = jnp.roll(dots.reshape(nz, ny, CAP), zi, axis=0).transpose(1, 0, 2)
    back = lax.all_to_all(
        dots.reshape(ny * nz, CAP), ("y", "z"), split_axis=0, concat_axis=0, tiled=True
    )
    totals = jnp.sum(back.reshape(EXPERTS, nz, CAP), axis=1)
    by_token = jnp.sum(jnp.where(chosen, totals[:, :, None], 0.0), axis=1)
    gate_grad = jnp.sum(jnp.where(named, by_token[None], 0.0), axis=1) / gates_t
    return (w_down_grad, gate_pre_grad, up_pre_grad, gate_grad.T)


def solution(mesh):
    fine = Mesh(
        mesh.devices.reshape(EXPERTS, mesh.shape["expert"] // EXPERTS, mesh.shape["tensor"] // 2, 2),
        ("y", "z", "x", "c"),
    )
    e, t = ("y", "z"), ("x", "c")
    return jax.shard_map(
        per_device,
        mesh=fine,
        in_specs=(P(e, t), P(e, None), P(e, None), P(e, t), P(None, e + t), P(None, e + t)),
        out_specs=(P(e, t), P(None, e + t), P(None, e + t), P(e, None)),
        check_vma=False,
    )
```

time: 202 us -> 229 us (1.13)
  blocking collectives: 121 us -> 39.7 us
  starting transfers between devices: 11.8 us -> 67.5 us
  waiting for transfers between devices: 27.2 us -> 68.3 us
  other arithmetic: 2.43 us -> 8.28 us
  matrix products: 11.9 us -> 15.3 us
    all_to_all x2 -> x1, blocking collectives: 96.2 us -> 17.6 us  [per_device(): lax.all_to_all(packed.reshape(EXPERTS, CAP, width), 'y', split_axis=0, co...]
    ppermute x0 -> x13, starting transfers between devices: none -> 54.3 us  [the longest x8 32.7 us: shift(): return lax.ppermute(x, axis, [(i, (i + step) % n) for i in range(n)])]
    all_gather x1, waiting for transfers between devices: 0.01 us -> 36.8 us  [per_device(): lax.all_gather((swish_out * up_act).astype(BF), ('x', 'c'), axis=1, tiled...]
    ppermute x0 -> x13, waiting for transfers between devices: none -> 26.6 us  [the longest x8 13.5 us: shift(): return lax.ppermute(x, axis, [(i, (i + step) % n) for i in range(n)])]
    unnamed x3 -> x1, waiting for transfers between devices: 16.6 us -> 0.02 us
    unnamed x14 -> x28, local copies, waits for them, and re-layouts: 8.88 us -> 0.07 us
    all_to_all x1, waiting for transfers between devices: 10.6 us -> 4.93 us  [per_device(): lax.all_to_all(dots.reshape(ny * nz, CAP), ('y', 'z'), split_axis=0, conc...]
    concatenate x0 -> x1, local copies, waits for them, and re-layouts: none -> 3.88 us  [per_device(): rows = jnp.concatenate(ahead + [far_low, far_high] + behind[:0:-1], axis=0)]
  transfers between devices with their start and end apart: 3 -> 15, of which waited for: 2 -> 10; matrix products, arithmetic and copies ran while one was open for 1% -> 6% of each run, Pallas kernels for 0% -> 0%
where the time goes in v1:
time: 229 us; the launch traced here: 225 us
  waiting for transfers between devices  68.3 us (30%)
  starting transfers between devices  67.5 us (29%)
  blocking collectives  39.7 us (17%)
  matrix products  15.3 us (7%)
  between operations  14.6 us (6%)
  local copies, waits for them, and re-layouts  11.4 us (5%)
  other arithmetic  8.28 us (4%)
    all_gather x1, waiting for transfers between devices, per_device(): lax.all_gather((swish_out * up_act).astype(BF), ('x', 'c'), axis=1, tiled...  36.8 us
    ppermute x8, starting transfers between devices, shift(): return lax.ppermute(x, axis, [(i, (i + step) % n) for i in range(n)])  32.7 us
    psum x1, blocking collectives, per_device(): dots = lax.psum(dots, ('x', 'c'))  22.1 us
    ppermute x5, starting transfers between devices, swap(): return lax.ppermute(x, axis, [(i, i ^ mask) for i in range(n)])  21.6 us
    all_to_all x1, blocking collectives, per_device(): lax.all_to_all(packed.reshape(EXPERTS, CAP, width), 'y', split_axis=0, co...  17.6 us
    ppermute x8, waiting for transfers between devices, shift(): return lax.ppermute(x, axis, [(i, (i + step) % n) for i in range(n)])  13.5 us
    all_to_all x1, starting transfers between devices, per_device(): lax.all_to_all(dots.reshape(ny * nz, CAP), ('y', 'z'), split_axis=0, conc...  13.2 us
    ppermute x5, waiting for transfers between devices, swap(): return lax.ppermute(x, axis, [(i, i ^ mask) for i in range(n)])  13.2 us
  transfers between devices with their start and end apart: 15, of which 10 were waited for; matrix products, arithmetic and copies ran while one was open for 6% of the time, Pallas kernels for 0%

profile of v1, /device:TPU:1, one launch (start us, length us, event | category | flops | bytes accessed | tf_op | source)
XLA Modules:
  0.0 225.2 jit_solution(16699764163542331073)
XLA Ops:
  9.9 17.6 %all_to_all.14 = bf16[8,24,768]{2,1,0:T(8,128)(2,1)S(1)} all-to-all(bf16[8,24,768]{2,1,0:T(8,128)(2,1)S(1)} %bitcast.72), channel_id=1, replica_groups=mesh['y'=8,'z'=8,'x'=4,'c'=2] {'y'}, dimensions={0} | all-to-all | bytes 589824 | tf_op jit(solution)/shard_map/all_to_all | solution.py:45
  27.7 4.7 %collective-permute-start.3 = (bf16[192,768]{0,1:T(8,128)(2,1)S(1)}, bf16[192,768]{0,1:T(8,128)(2,1)S(1)}, u32[]{:S(2)}, u32[]{:S(2)}) collective-permute-start(bf16[192,768]{0,1:T(8,128)(2,1)S(1)} %copy.43), channel_id=1, source_target_pairs={{0,8},{8,16},{16,24},{24,32},{32,40},{40,48},{48,56},{56,0},{1,9},... | collective-permute-start | bytes 884744 | tf_op jit(solution)/shard_map/ppermute | solution.py:15
  32.4 8.6 %collective-permute-start = (bf16[192,768]{0,1:T(8,128)(2,1)S(1)}, bf16[192,768]{0,1:T(8,128)(2,1)S(1)}, u32[]{:S(2)}, u32[]{:S(2)}) collective-permute-start(bf16[192,768]{0,1:T(8,128)(2,1)S(1)} %copy.43), channel_id=1, source_target_pairs={{0,56},{8,0},{16,8},{24,16},{32,24},{40,32},{48,40},{56,48},{1,57}... | collective-permute-start | bytes 884744 | tf_op jit(solution)/shard_map/ppermute | solution.py:15
  41.0 4.8 %collective-permute-done.3 = bf16[192,768]{0,1:T(8,128)(2,1)S(1)} collective-permute-done((bf16[192,768]{0,1:T(8,128)(2,1)S(1)}, bf16[192,768]{0,1:T(8,128)(2,1)S(1)}, u32[]{:S(2)}, u32[]{:S(2)}) %collective-permute-start.3) | collective-permute-done | bytes 294944 | tf_op jit(solution)/shard_map/ppermute | solution.py:15
  47.7 4.6 %collective-permute-start.1 = (bf16[192,768]{0,1:T(8,128)(2,1)S(1)}, bf16[192,768]{0,1:T(8,128)(2,1)}, u32[]{:S(2)}, u32[]{:S(2)}) collective-permute-start(bf16[192,768]{0,1:T(8,128)(2,1)S(1)} %collective-permute-done), channel_id=1, source_target_pairs={{0,56},{8,0},{16,8},{24,16},{32,24},{40,32},{48,40},{56,48},{1,57}... | collective-permute-start | bytes 884744 | tf_op jit(solution)/shard_map/ppermute | solution.py:15
  52.3 3.9 %collective-permute-done.4 = bf16[192,768]{0,1:T(8,128)(2,1)} collective-permute-done((bf16[192,768]{0,1:T(8,128)(2,1)S(1)}, bf16[192,768]{0,1:T(8,128)(2,1)}, u32[]{:S(2)}, u32[]{:S(2)}) %collective-permute-start.4) | collective-permute-done | bytes 294944 | tf_op jit(solution)/shard_map/ppermute | solution.py:15
  58.2 4.6 %collective-permute-start.2 = (bf16[192,768]{0,1:T(8,128)(2,1)}, bf16[192,768]{0,1:T(8,128)(2,1)S(1)}, u32[]{:S(2)}, u32[]{:S(2)}) collective-permute-start(bf16[192,768]{0,1:T(8,128)(2,1)} %collective-permute-done.1), channel_id=1, source_target_pairs={{0,56},{8,0},{16,8},{24,16},{32,24},{40,32},{48,40},{56,48},{1,57}... | collective-permute-start | bytes 884744 | tf_op jit(solution)/shard_map/ppermute | solution.py:15
  62.8 3.4 %collective-permute-done.5 = bf16[192,768]{0,1:T(8,128)(2,1)S(1)} collective-permute-done((bf16[192,768]{0,1:T(8,128)(2,1)}, bf16[192,768]{0,1:T(8,128)(2,1)S(1)}, u32[]{:S(2)}, u32[]{:S(2)}) %collective-permute-start.5) | collective-permute-done | bytes 294944 | tf_op jit(solution)/shard_map/ppermute | solution.py:15
  68.3 4.6 %collective-permute-start.7 = (bf16[96,768]{0,1:T(8,128)(2,1)S(1)}, bf16[96,768]{0,1:T(8,128)(2,1)}, u32[]{:S(2)}, u32[]{:S(2)}) collective-permute-start(bf16[96,768]{0,1:T(8,128)(2,1)S(1)} %slice.59), channel_id=1, source_target_pairs={{0,56},{8,0},{16,8},{24,16},{32,24},{40,32},{48,40},{56,48},{1,57}... | collective-permute-start | bytes 442376 | tf_op jit(solution)/shard_map/ppermute | solution.py:15
  75.4 3.9 %concatenate.21 = bf16[1536,768]{0,1:T(8,128)(2,1)S(1)} concatenate(bf16[192,768]{0,1:T(8,128)(2,1)S(1)} %copy.43, bf16[192,768]{0,1:T(8,128)(2,1)} %copy-done.7, bf16[192,768]{0,1:T(8,128)(2,1)} %collective-permute-done.1, bf16[192,768]{0,1:T(8,128)(2,1)} %copy-done.4, bf16[96,768]{0,1:T(8,128)(2,1)S(1)} %collective-permute-done.6, bf16[96,768]{0,1:T(8,128)(2,1)} %collective-permute-done.7, ...), dimensions={0} | concatenate | bytes 4718592 | tf_op jit(solution)/shard_map/concatenate | solution.py:55
  79.4 2.7 %convolution_convert_fusion = bf16[1536,512]{1,0:T(8,128)(2,1)S(1)} fusion(bf16[1536,768]{0,1:T(8,128)(2,1)S(1)} %concatenate.21, bf16[128,768]{1,0:T(8,128)(2,1)} %get-tuple-element.20, bf16[128,768]{1,0:T(8,128)(2,1)} %get-tuple-element.14, bf16[128,768]{1,0:T(8,128)(2,1)} %get-tuple-element.15, bf16[128,768]{1,0:T(8,128)(2,1)} %get-tuple-element.16), kind=kOutput, calls=%fused_computation.2 | convolution fusion | flops 1211891712 | bytes 4718592 | tf_op jit(solution)/shard_map/dot_general | solution.py:78
  82.1 8.5 %collective-permute-start.8 = (bf16[1536,512]{1,0:T(8,128)(2,1)S(1)}, bf16[1536,512]{1,0:T(8,128)(2,1)S(1)}, u32[]{:S(2)}, u32[]{:S(2)}) collective-permute-start(bf16[1536,512]{1,0:T(8,128)(2,1)S(1)} %convolution_convert_fusion), channel_id=1, source_target_pairs={{0,1},{1,0},{2,3},{3,2},{4,5},{5,4},{6,7},{7,6},{8,9},{9,8},{10,11... | collective-permute-start | bytes 4718600 | tf_op jit(solution)/shard_map/ppermute | solution.py:20
  90.6 3.0 %collective-permute-done.8 = bf16[1536,512]{1,0:T(8,128)(2,1)S(1)} collective-permute-done((bf16[1536,512]{1,0:T(8,128)(2,1)S(1)}, bf16[1536,512]{1,0:T(8,128)(2,1)S(1)}, u32[]{:S(2)}, u32[]{:S(2)}) %collective-permute-start.8) | collective-permute-done | bytes 1572896 | tf_op jit(solution)/shard_map/ppermute | solution.py:20
  95.1 3.2 %collective-permute-start.9 = (bf16[768,256]{1,0:T(8,128)(2,1)S(1)}, bf16[768,256]{1,0:T(8,128)(2,1)S(1)}, u32[]{:S(2)}, u32[]{:S(2)}) collective-permute-start(bf16[768,256]{1,0:T(8,128)(2,1)S(1)} %get-tuple-element.11), channel_id=1, source_target_pairs={{0,2},{2,0},{4,6},{6,4},{1,3},{3,1},{5,7},{7,5},{8,10},{10,8},{12,... | collective-permute-start | bytes 1179656 | tf_op jit(solution)/shard_map/ppermute | solution.py:20
  98.4 3.7 %collective-permute-start.11 = (bf16[768,256]{1,0:T(8,128)(2,1)S(1)}, bf16[768,256]{1,0:T(8,128)(2,1)S(1)}, u32[]{:S(2)}, u32[]{:S(2)}) collective-permute-start(bf16[768,256]{1,0:T(8,128)(2,1)S(1)} %get-tuple-element.12), channel_id=1, source_target_pairs={{0,6},{2,4},{4,2},{6,0},{1,7},{3,5},{5,3},{7,1},{8,14},{10,12},{12... | collective-permute-start | bytes 1179656 | tf_op jit(solution)/shard_map/ppermute | solution.py:20
  102.0 5.3 %collective-permute-done.9 = bf16[768,256]{1,0:T(8,128)(2,1)S(1)} collective-permute-done((bf16[768,256]{1,0:T(8,128)(2,1)S(1)}, bf16[768,256]{1,0:T(8,128)(2,1)S(1)}, u32[]{:S(2)}, u32[]{:S(2)}) %collective-permute-start.9) | collective-permute-done | bytes 393248 | tf_op jit(solution)/shard_map/ppermute | solution.py:20
  107.5 4.3 %collective-permute-start.10 = (bf16[768,128]{1,0:T(8,128)(2,1)S(1)}, bf16[768,128]{1,0:T(8,128)(2,1)S(1)}, u32[]{:S(2)}, u32[]{:S(2)}) collective-permute-start(bf16[768,128]{1,0:T(8,128)(2,1)S(1)} %fusion.35), channel_id=1, source_target_pairs={{0,6},{2,4},{4,2},{6,0},{1,7},{3,5},{5,3},{7,1},{8,14},{10,12},{12... | collective-permute-start | bytes 589832 | tf_op jit(solution)/shard_map/ppermute | solution.py:20
  111.9 3.9 %collective-permute-done.10 = bf16[768,128]{1,0:T(8,128)(2,1)S(1)} collective-permute-done((bf16[768,128]{1,0:T(8,128)(2,1)S(1)}, bf16[768,128]{1,0:T(8,128)(2,1)S(1)}, u32[]{:S(2)}, u32[]{:S(2)}) %collective-permute-start.10) | collective-permute-done | bytes 196640 | tf_op jit(solution)/shard_map/ppermute | solution.py:20
  129.1 36.8 %all-gather.2.cloned.1.call-done = bf16[1536,1024]{1,0:T(8,128)(2,1)} async-done(((bf16[1536,128]{1,0:T(8,128)(2,1)}), bf16[1536,1024]{1,0:T(8,128)(2,1)}) %all-gather.2.cloned.1.call-update) | async-done | bytes 3145744 | tf_op jit(solution)/shard_map/all_gather | solution.py:69
  165.8 5.1 %multiply_reduce_fusion = f32[1536]{0:T(1024)S(1)} fusion(bf16[1536,768]{0,1:T(8,128)(2,1)S(1)} %concatenate.21, bf16[1536,1024]{1,0:T(8,128)(2,1)} %all-gather.2.cloned.1.call-done, bf16[1024,768]{1,0:T(8,128)(2,1)} %param.11), kind=kOutput, calls=%fused_computation | convolution fusion | flops 2419456512 | bytes 7084032 | tf_op jit(solution)/shard_map/dot_general | solution.py:105
  171.0 22.1 %psum.7 = f32[8,8,24]{2,1,0:T(8,128)S(1)} all-reduce(f32[8,8,24]{2,1,0:T(8,128)S(1)} %reshape.65), channel_id=1, replica_groups=mesh['y'=8,'z'=8,'x'=4,'c'=2] {'x','c'}, use_global_device_ids=true, to_apply=%region_3.5 | all-reduce | flops 1536 | bytes 12288 | tf_op jit(solution)/shard_map/psum | solution.py:107
  193.7 13.2 %all-to-all-start.1 = ((f32[64,1,24]{2,1,0:T(1,128)}), f32[64,1,24]{2,1,0:T(1,128)S(1)}, u32[]{:S(2)}, u32[]{:S(2)}) async-start(f32[64,1,24]{2,1,0:T(1,128)} %bitcast.20), calls=%async_computation.1 | async-start | bytes 65536 | tf_op jit(solution)/shard_map/all_to_all | solution.py:109
  207.0 5.7 %convolution_convert_fusion.1 = bf16[1024,768]{1,0:T(8,128)(2,1)} fusion(bf16[1536,1024]{1,0:T(8,128)(2,1)} %all-gather.2.cloned.1.call-done, bf16[1536,768]{0,1:T(8,128)(2,1)S(1)} %concatenate.21), kind=kOutput, calls=%fused_computation.3 | convolution fusion | flops 2416705536 | bytes 7077888 | tf_op jit(solution)/shard_map/dot_general | solution.py:101
  212.6 4.9 %all-to-all-done.1 = f32[64,1,24]{2,1,0:T(1,128)S(1)} async-done(((f32[64,1,24]{2,1,0:T(1,128)}), f32[64,1,24]{2,1,0:T(1,128)S(1)}, u32[]{:S(2)}, u32[]{:S(2)}) %all-to-all-start.1) | async-done | bytes 6176 | tf_op jit(solution)/shard_map/all_to_all | solution.py:109
  (76 shorter events, 27.7 us)
Async XLA Ops:
  7.2 65.7 %copy-start.1 = (bf16[1024,768]{1,0:T(8,128)(2,1)S(1)}, bf16[1024,768]{1,0:T(8,128)(2,1)}, u32[]{:S(2)}) copy-start(bf16[1024,768]{1,0:T(8,128)(2,1)} %param.11) | copy-start | bytes 4718596
  7.2 158.7 %all-gather.2.cloned.1.call-start = ((), (), s32[]{:S(2)}) async-start(), calls=%async_computation.2 | async-start | bytes 3538944 | tf_op jit(solution)/shard_map/all_gather | solution.py:69
  27.7 18.0 %collective-permute-start.3 = (bf16[192,768]{0,1:T(8,128)(2,1)S(1)}, bf16[192,768]{0,1:T(8,128)(2,1)S(1)}, u32[]{:S(2)}, u32[]{:S(2)}) collective-permute-start(bf16[192,768]{0,1:T(8,128)(2,1)S(1)} %copy.43), channel_id=1, source_target_pairs={{0,8},{8,16},{16,24},{24,32},{32,40},{40,48},{48,56},{56,0},{1,9},... | collective-permute-start | bytes 884744 | tf_op jit(solution)/shard_map/ppermute | solution.py:15
  32.4 15.3 %collective-permute-start = (bf16[192,768]{0,1:T(8,128)(2,1)S(1)}, bf16[192,768]{0,1:T(8,128)(2,1)S(1)}, u32[]{:S(2)}, u32[]{:S(2)}) collective-permute-start(bf16[192,768]{0,1:T(8,128)(2,1)S(1)} %copy.43), channel_id=1, source_target_pairs={{0,56},{8,0},{16,8},{24,16},{32,24},{40,32},{48,40},{56,48},{1,57}... | collective-permute-start | bytes 884744 | tf_op jit(solution)/shard_map/ppermute | solution.py:15
  45.8 12.4 %copy-start.6 = (bf16[192,768]{0,1:T(8,128)(2,1)}, bf16[192,768]{0,1:T(8,128)(2,1)S(1)}, u32[]{:S(2)}) copy-start(bf16[192,768]{0,1:T(8,128)(2,1)S(1)} %collective-permute-done.3) | copy-start | bytes 884740
  45.8 10.5 %collective-permute-start.4 = (bf16[192,768]{0,1:T(8,128)(2,1)S(1)}, bf16[192,768]{0,1:T(8,128)(2,1)}, u32[]{:S(2)}, u32[]{:S(2)}) collective-permute-start(bf16[192,768]{0,1:T(8,128)(2,1)S(1)} %collective-permute-done.3), channel_id=1, source_target_pairs={{0,8},{8,16},{16,24},{24,32},{32,40},{40,48},{48,56},{56,0},{1,9},... | collective-permute-start | bytes 884744 | tf_op jit(solution)/shard_map/ppermute | solution.py:15
  47.7 26.4 %copy-start.7 = (bf16[192,768]{0,1:T(8,128)(2,1)}, bf16[192,768]{0,1:T(8,128)(2,1)S(1)}, u32[]{:S(2)}) copy-start(bf16[192,768]{0,1:T(8,128)(2,1)S(1)} %collective-permute-done) | copy-start | bytes 884740
  47.7 10.4 %collective-permute-start.1 = (bf16[192,768]{0,1:T(8,128)(2,1)S(1)}, bf16[192,768]{0,1:T(8,128)(2,1)}, u32[]{:S(2)}, u32[]{:S(2)}) collective-permute-start(bf16[192,768]{0,1:T(8,128)(2,1)S(1)} %collective-permute-done), channel_id=1, source_target_pairs={{0,56},{8,0},{16,8},{24,16},{32,24},{40,32},{48,40},{56,48},{1,57}... | collective-permute-start | bytes 884744 | tf_op jit(solution)/shard_map/ppermute | solution.py:15
  56.2 9.9 %collective-permute-start.5 = (bf16[192,768]{0,1:T(8,128)(2,1)}, bf16[192,768]{0,1:T(8,128)(2,1)S(1)}, u32[]{:S(2)}, u32[]{:S(2)}) collective-permute-start(bf16[192,768]{0,1:T(8,128)(2,1)} %collective-permute-done.4), channel_id=1, source_target_pairs={{0,8},{8,16},{16,24},{24,32},{32,40},{40,48},{48,56},{56,0},{1,9},... | collective-permute-start | bytes 884744 | tf_op jit(solution)/shard_map/ppermute | solution.py:15
  58.2 9.9 %collective-permute-start.2 = (bf16[192,768]{0,1:T(8,128)(2,1)}, bf16[192,768]{0,1:T(8,128)(2,1)S(1)}, u32[]{:S(2)}, u32[]{:S(2)}) collective-permute-start(bf16[192,768]{0,1:T(8,128)(2,1)} %collective-permute-done.1), channel_id=1, source_target_pairs={{0,56},{8,0},{16,8},{24,16},{32,24},{40,32},{48,40},{56,48},{1,57}... | collective-permute-start | bytes 884744 | tf_op jit(solution)/shard_map/ppermute | solution.py:15
  66.2 7.9 %collective-permute-start.6 = (bf16[96,768]{0,1:T(8,128)(2,1)S(1)}, bf16[96,768]{0,1:T(8,128)(2,1)S(1)}, u32[]{:S(2)}, u32[]{:S(2)}) collective-permute-start(bf16[96,768]{0,1:T(8,128)(2,1)S(1)} %slice.58), channel_id=1, source_target_pairs={{0,8},{8,16},{16,24},{24,32},{32,40},{40,48},{48,56},{56,0},{1,9},... | collective-permute-start | bytes 442376 | tf_op jit(solution)/shard_map/ppermute | solution.py:15
  68.3 7.2 %collective-permute-start.7 = (bf16[96,768]{0,1:T(8,128)(2,1)S(1)}, bf16[96,768]{0,1:T(8,128)(2,1)}, u32[]{:S(2)}, u32[]{:S(2)}) collective-permute-start(bf16[96,768]{0,1:T(8,128)(2,1)S(1)} %slice.59), channel_id=1, source_target_pairs={{0,56},{8,0},{16,8},{24,16},{32,24},{40,32},{48,40},{56,48},{1,57}... | collective-permute-start | bytes 442376 | tf_op jit(solution)/shard_map/ppermute | solution.py:15
  79.3 14.3 %copy-start.8 = (bf16[128,768]{1,0:T(8,128)(2,1)S(1)}, bf16[128,768]{1,0:T(8,128)(2,1)}, u32[]{:S(2)}) copy-start(bf16[128,768]{1,0:T(8,128)(2,1)} %get-tuple-element.13) | copy-start | bytes 589828
  79.3 14.2 %copy-start.9 = (bf16[128,768]{1,0:T(8,128)(2,1)S(1)}, bf16[128,768]{1,0:T(8,128)(2,1)}, u32[]{:S(2)}) copy-start(bf16[128,768]{1,0:T(8,128)(2,1)} %get-tuple-element.17) | copy-start | bytes 589828
  79.3 14.2 %copy-start.10 = (bf16[128,768]{1,0:T(8,128)(2,1)S(1)}, bf16[128,768]{1,0:T(8,128)(2,1)}, u32[]{:S(2)}) copy-start(bf16[128,768]{1,0:T(8,128)(2,1)} %get-tuple-element.18) | copy-start | bytes 589828
  79.4 14.2 %copy-start.11 = (bf16[128,768]{1,0:T(8,128)(2,1)S(1)}, bf16[128,768]{1,0:T(8,128)(2,1)}, u32[]{:S(2)}) copy-start(bf16[128,768]{1,0:T(8,128)(2,1)} %get-tuple-element.19) | copy-start | bytes 589828
  82.1 11.5 %collective-permute-start.8 = (bf16[1536,512]{1,0:T(8,128)(2,1)S(1)}, bf16[1536,512]{1,0:T(8,128)(2,1)S(1)}, u32[]{:S(2)}, u32[]{:S(2)}) collective-permute-start(bf16[1536,512]{1,0:T(8,128)(2,1)S(1)} %convolution_convert_fusion), channel_id=1, source_target_pairs={{0,1},{1,0},{2,3},{3,2},{4,5},{5,4},{6,7},{7,6},{8,9},{9,8},{10,11... | collective-permute-start | bytes 4718600 | tf_op jit(solution)/shard_map/ppermute | solution.py:20
  95.1 20.7 %copy-start.5 = (f32[1536,512]{1,0:T(8,128)}, f32[1536,512]{1,0:T(8,128)S(1)}, u32[]{:S(2)}) copy-start(f32[1536,512]{1,0:T(8,128)S(1)} %get-tuple-element.22) | copy-start | bytes 9437188
  95.1 12.2 %collective-permute-start.9 = (bf16[768,256]{1,0:T(8,128)(2,1)S(1)}, bf16[768,256]{1,0:T(8,128)(2,1)S(1)}, u32[]{:S(2)}, u32[]{:S(2)}) collective-permute-start(bf16[768,256]{1,0:T(8,128)(2,1)S(1)} %get-tuple-element.11), channel_id=1, source_target_pairs={{0,2},{2,0},{4,6},{6,4},{1,3},{3,1},{5,7},{7,5},{8,10},{10,8},{12,... | collective-permute-start | bytes 1179656 | tf_op jit(solution)/shard_map/ppermute | solution.py:20
  98.4 13.5 %collective-permute-start.11 = (bf16[768,256]{1,0:T(8,128)(2,1)S(1)}, bf16[768,256]{1,0:T(8,128)(2,1)S(1)}, u32[]{:S(2)}, u32[]{:S(2)}) collective-permute-start(bf16[768,256]{1,0:T(8,128)(2,1)S(1)} %get-tuple-element.12), channel_id=1, source_target_pairs={{0,6},{2,4},{4,2},{6,0},{1,7},{3,5},{5,3},{7,1},{8,14},{10,12},{12... | collective-permute-start | bytes 1179656 | tf_op jit(solution)/shard_map/ppermute | solution.py:20
  107.5 8.3 %collective-permute-start.10 = (bf16[768,128]{1,0:T(8,128)(2,1)S(1)}, bf16[768,128]{1,0:T(8,128)(2,1)S(1)}, u32[]{:S(2)}, u32[]{:S(2)}) collective-permute-start(bf16[768,128]{1,0:T(8,128)(2,1)S(1)} %fusion.35), channel_id=1, source_target_pairs={{0,6},{2,4},{4,2},{6,0},{1,7},{3,5},{5,3},{7,1},{8,14},{10,12},{12... | collective-permute-start | bytes 589832 | tf_op jit(solution)/shard_map/ppermute | solution.py:20
  116.7 6.5 %collective-permute-start.12 = (bf16[768,128]{1,0:T(8,128)(2,1)S(1)}, bf16[768,128]{1,0:T(8,128)(2,1)}, u32[]{:S(2)}, u32[]{:S(2)}) collective-permute-start(bf16[768,128]{1,0:T(8,128)(2,1)S(1)} %get-tuple-element.10), channel_id=1, source_target_pairs={{0,2},{2,0},{4,6},{6,4},{1,3},{3,1},{5,7},{7,5},{8,10},{10,8},{12,... | collective-permute-start | bytes 589832 | tf_op jit(solution)/shard_map/ppermute | solution.py:20
  193.7 23.8 %all-to-all-start.1 = ((f32[64,1,24]{2,1,0:T(1,128)}), f32[64,1,24]{2,1,0:T(1,128)S(1)}, u32[]{:S(2)}, u32[]{:S(2)}) async-start(f32[64,1,24]{2,1,0:T(1,128)} %bitcast.20), calls=%async_computation.1 | async-start | bytes 65536 | tf_op jit(solution)/shard_map/all_to_all | solution.py:109
  206.9 10.8 %copy-start.13 = (bf16[64,2]{0,1:T(2,128)(2,1)S(1)}, bf16[64,2]{0,1:T(2,128)(2,1)}, u32[]{:S(2)}) copy-start(bf16[64,2]{0,1:T(2,128)(2,1)} %param.10) | copy-start | bytes 772
  (5 other events, 25.9 us)
Sparse Core Ops, SparseCore 0:
  127.3 38.4 all-gather.1

commit v2 on v1

v2 whole, which is shorter than its diff:
```python
import jax
import jax.numpy as jnp
from jax import lax
from jax.experimental import pallas as pl
from jax.experimental.pallas import tpu as pltpu
from jax.sharding import Mesh
from jax.sharding import PartitionSpec as P

EXPERTS = 8
CAP = 24
NZ = 8
NX = 4
BLOCK = EXPERTS * CAP
HALF = BLOCK // 2
SIZES = (HALF, BLOCK, BLOCK, BLOCK, HALF)
STARTS = (0, 96, 288, 480, 672)
MINE = 768
BF = jnp.bfloat16
F32 = jnp.float32
VM = pl.BlockSpec(memory_space=pltpu.VMEM)
SM = pl.BlockSpec(memory_space=pltpu.SMEM)


def call(body, outs, ins, cost):
    specs = [SM if a.dtype == jnp.int32 and a.shape == (40,) else VM for a in ins]
    return pl.pallas_call(
        body,
        out_shape=[jax.ShapeDtypeStruct(s, d) for s, d in outs],
        in_specs=specs,
        out_specs=[VM] * len(outs),
        compiler_params=pltpu.CompilerParams(vmem_limit_bytes=48 * 2**20),
        cost_estimate=pl.CostEstimate(flops=cost[0], bytes_accessed=cost[1], transcendentals=0),
    )(*ins)


def dot(a, b, da, db):
    return lax.dot_general(a, b, (((da,), (db,)), ((), ())), preferred_element_type=F32)


def pack_body(routes, gates, rows, out):
    tokens = rows.shape[0]
    expert = lax.broadcasted_iota(jnp.int32, (EXPERTS, tokens), 0)
    first, second = routes[0:1, :] == expert, routes[1:2, :] == expert
    weight = jnp.where(first, gates[0:1, :], 0.0) + jnp.where(second, gates[1:2, :], 0.0)
    member = jnp.where(first | second, 1.0, 0.0)
    at = lax.broadcasted_iota(jnp.int32, (tokens, tokens), 0)
    to = lax.broadcasted_iota(jnp.int32, (tokens, tokens), 1)
    earlier = jnp.where(at < to, 1.0, 0.0).astype(BF)
    rank = dot(member.astype(BF), earlier, 1, 0)
    rank = jnp.where(member > 0.0, rank, -1.0).astype(jnp.int32)
    place = lax.broadcasted_iota(jnp.int32, (CAP, tokens), 0)
    chosen = [
        jnp.where(rank[e : e + 1] == place, weight[e : e + 1], 0.0) for e in range(EXPERTS)
    ]
    out[...] = dot(jnp.concatenate(chosen, axis=0).astype(BF), rows[...], 1, 0).astype(BF)


def act_body(table, gate, up, mine, other, by_gate, by_up):
    for g in range(16):
        zs, half = table[g], table[16 + g]
        a = gate[pl.ds(half * 4, 4), zs].astype(F32).reshape(HALF, 128)
        b = up[pl.ds(half * 4, 4), zs].astype(F32).reshape(HALF, 128)
        sig = 1.0 / (1.0 + jnp.exp(-a))
        swish = a * sig
        at = pl.ds((g % 8) * HALF, HALF)
        (mine if g < 8 else other)[at, :] = (swish * b).astype(BF)
        by_gate[pl.ds(g * HALF, HALF), :] = b * sig * (1.0 + a * (1.0 - sig))
        by_up[pl.ds(g * HALF, HALF), :] = swish


def product_body(labels, table, r0, r1, r2, r3, r4, w_own, w_other, ha, hb, out, dots):
    ones = jnp.ones((8, 256), F32)
    core = table[36]
    first = pl.ds(pl.multiple_of(core * HALF, HALF), HALF)
    for piece, (ref, size, start) in enumerate(zip((r0, r1, r2, r3, r4), SIZES, STARTS)):
        rows = first if piece == 0 else pl.ds(0, size)
        own, other = ref[0, rows, :], ref[1, rows, :]
        total = None
        for i, h in enumerate((ha, hb)):
            at = pl.ds(pl.multiple_of(table[32 + labels[i]] * 256, 256), 256)
            part = dot(own, w_own[at, :], 1, 1) + dot(other, w_other[at, :], 1, 1)
            out[pl.ds(start, size), pl.ds(i * 256, 256)] = part.astype(out.dtype)
            term = part * h[pl.ds(start, size), :].astype(F32)
            total = term if total is None else total + term
        dots[:, pl.ds(start, size)] = lax.dot_general(
            ones, total, (((1,), (1,)), ((), ())), precision=lax.Precision.HIGHEST,
            preferred_element_type=F32,
        )


def weight_body(which, table, r0, r1, r2, r3, r4, h0, h1, h2, h3, *rest):
    out = rest[-1]
    core = table[36]
    first = pl.ds(pl.multiple_of(core * HALF, HALF), HALF)
    for label, h in enumerate((h0, h1, h2, h3)):
        total = None
        for piece, (ref, size, start) in enumerate(zip((r0, r1, r2, r3, r4), SIZES, STARTS)):
            rows = first if piece == 0 else pl.ds(0, size)
            term = dot(h[pl.ds(start, size), :], ref[which, rows, :], 0, 0)
            total = term if total is None else total + term
        at = pl.ds(pl.multiple_of(table[32 + label] * 256, 256), 256)
        if len(rest) == 2:
            total = total + rest[0][at, :].astype(F32)
        out[at, :] = total.astype(BF)


def grad_body(table, kept, got, by_gate, by_up, gate_out, up_out):
    for g in range(16):
        zs, half = table[g], table[16 + g]
        src = (kept if g < 8 else got)[pl.ds((g % 8) * HALF, HALF), :].astype(F32)
        at = pl.ds(g * HALF, HALF)
        gate_out[pl.ds(half * 4, 4), zs] = (src * by_gate[at, :]).reshape(4, CAP, 128).astype(BF)
        up_out[pl.ds(half * 4, 4), zs] = (src * by_up[at, :]).reshape(4, CAP, 128).astype(BF)


def per_device(grad_out, routes, gates, w_down, gate_pre, up_pre):
    zi, xi, ci = lax.axis_index("z"), lax.axis_index("x"), lax.axis_index("c")
    tokens, width = grad_out.shape
    ff = w_down.shape[0]

    sign = 2 * ci - 1
    m1, m2 = 1 + 2 * ci, 3 - 2 * ci
    steps = jnp.array([0, 1, 1, 2, 2, 3, 3, 4], jnp.int32)
    halves = jnp.array([0, 0, 1, 0, 1, 0, 1, 0], jnp.int32)
    ends = jnp.array([1, 0, 0, 0, 0, 0, 0, 1], jnp.int32)
    table = jnp.concatenate(
        [
            (zi + sign * steps) % NZ,
            (zi - sign * steps) % NZ,
            halves + ends * ci,
            halves + ends * (1 - ci),
            jnp.stack([xi, xi ^ m2, xi ^ m1, xi ^ 2, ci, ci, ci, ci]),
        ]
    ).astype(jnp.int32)

    def swap_core(x):
        return lax.ppermute(x, "c", [(0, 1), (1, 0)])

    def ring(x):
        return lax.ppermute(
            x, ("z", "c"), [(z * 2 + c, (z + 1 - 2 * c) % NZ * 2 + c) for z in range(NZ) for c in range(2)]
        )

    def swap_x(x, first):
        masks = (1, 3) if first else (3, 1)
        return lax.ppermute(
            x, ("x", "c"), [(i * 2 + c, (i ^ masks[c]) * 2 + c) for i in range(NX) for c in range(2)]
        )

    def pair(own, other):
        low, high = jnp.where(ci == 0, own, other), jnp.where(ci == 0, other, own)
        return jnp.concatenate([low, high], axis=1)

    routes_t, gates_t = routes.T, gates.T.astype(F32)
    (packed,) = call(
        pack_body, [((BLOCK, width), BF)], (routes_t, gates_t, grad_out), (2 * BLOCK * tokens * width, 400000)
    )
    own = lax.all_to_all(
        packed.reshape(EXPERTS, CAP, width), "y", split_axis=0, concat_axis=0, tiled=True
    ).reshape(BLOCK, width)
    w_other = swap_core(w_down)

    view = (EXPERTS, NZ, CAP, 128)
    mine, other, by_gate, by_up = call(
        act_body,
        [((MINE, 128), BF), ((MINE, 128), BF), ((2 * MINE, 128), F32), ((2 * MINE, 128), F32)],
        (table, gate_pre.reshape(view), up_pre.reshape(view)),
        (20 * 2 * MINE * 128, 3000000),
    )
    h0 = pair(mine, swap_core(other))
    h2 = swap_x(h0, True)
    h1 = swap_x(h0, False)
    h3 = swap_x(h2, False)

    r0 = jnp.stack([own, swap_core(own)])
    r1 = ring(r0)
    r2 = ring(r1)
    r3 = ring(r2)
    r4 = ring(lax.dynamic_slice_in_dim(r3, ci * HALF, HALF, 1))
    pieces = (r0, r1, r2, r3, r4)

    def product(labels, ha, hb, dtype):
        return call(
            lambda *refs: product_body(labels, *refs),
            [((MINE, 512), dtype), ((8, MINE), F32)],
            (table, *pieces, w_down, w_other, ha, hb),
            (2 * MINE * 512 * 2 * width, 6000000),
        )

    send, dots_a = product((2, 3), h2, h3, BF)
    keep, dots_b = product((0, 1), h0, h1, F32)
    part = keep + swap_x(send, True).astype(F32)
    whole = part[:, :256] + swap_x(part[:, 256:].astype(BF), False).astype(F32)
    low, high = whole[:, :128], whole[:, 128:]
    kept = jnp.where(ci == 0, low, high)
    got = swap_core(jnp.where(ci == 0, high, low).astype(BF))
    gate_pre_grad, up_pre_grad = call(
        grad_body, [(view, BF), (view, BF)], (table, kept, got, by_gate, by_up), (4 * MINE * 128, 3000000)
    )

    dots = (dots_a[0] + dots_b[0]).reshape(8, 4, CAP)
    zero = jnp.zeros((1, 4, CAP), F32)
    near = dots[1:7].reshape(3, EXPERTS, CAP)
    none = jnp.zeros_like(near)
    at0, at4 = dots[0:1], dots[7:8]

    def spread(c):
        ends = [jnp.concatenate([a, zero] if c == 0 else [zero, a], axis=1) for a in (at0, at4)]
        sides = (none, near[::-1]) if c == 0 else (near, none)
        return jnp.concatenate([ends[0], sides[0], ends[1], sides[1]], axis=0)

    by_source = jnp.roll(jnp.where(ci == 0, spread(0), spread(1)), zi, axis=0).transpose(1, 0, 2)
    back = lax.all_to_all(
        by_source.reshape(EXPERTS * NZ, CAP), ("y", "z"), split_axis=0, concat_axis=0, tiled=True
    )
    totals = jnp.sum(back.reshape(EXPERTS, NZ, CAP), axis=1)
    totals = totals + swap_core(totals)
    totals = totals + swap_x(totals, True)
    totals = totals + swap_x(totals, False)

    named = routes_t[:, None, :] == jnp.arange(EXPERTS, dtype=jnp.int32)[None, :, None]
    member = jnp.any(named, axis=0)
    order = jnp.arange(tokens, dtype=jnp.int32)
    earlier = (order[:, None] < order[None, :]).astype(BF)
    rank = jnp.dot(member.astype(BF), earlier, preferred_element_type=F32).astype(jnp.int32)
    chosen = member[:, None, :] & (rank[:, None, :] == jnp.arange(CAP, dtype=jnp.int32)[None, :, None])
    by_token = jnp.sum(jnp.where(chosen, totals[:, :, None], 0.0), axis=1)
    gate_grad = jnp.sum(jnp.where(named, by_token[None], 0.0), axis=1) / gates_t

    hiddens = (h0, h1, h2, h3)
    cost = (2 * MINE * ff * width, 5000000)
    (lent,) = call(
        lambda *refs: weight_body(1, *refs), [((ff, width), BF)], (table, *pieces, *hiddens), cost
    )
    (w_down_grad,) = call(
        lambda *refs: weight_body(0, *refs),
        [((ff, width), BF)],
        (table, *pieces, *hiddens, swap_core(lent)),
        cost,
    )
    flat = (EXPERTS * NZ * CAP, 128)
    return (w_down_grad, gate_pre_grad.reshape(flat), up_pre_grad.reshape(flat), gate_grad.T)


def solution(mesh):
    fine = Mesh(mesh.devices.reshape(EXPERTS, NZ, NX, 2), ("y", "z", "x", "c"))
    e, t = ("y", "z"), ("x", "c")
    return jax.shard_map(
        per_device,
        mesh=fine,
        in_specs=(P(e, t), P(e, None), P(e, None), P(e, t), P(None, e + t), P(None, e + t)),
        out_specs=(P(e, t), P(None, e + t), P(None, e + t), P(e, None)),
        check_vma=False,
    )
```

time: 229 us -> 162 us (0.71); the launches traced: 225 us -> 161 us
  waiting for transfers between devices: 68.3 us -> 25.4 us
  Pallas kernels: 0 us -> 23 us
  matrix products: 15.3 us -> 0.13 us
  between operations: 14.6 us -> 1.11 us
  blocking collectives: 39.7 us -> 32.3 us
  other arithmetic: 8.28 us -> 2.13 us
  local copies, waits for them, and re-layouts: 11.4 us -> 6.81 us
  starting transfers between devices: 67.5 us -> 70.3 us
    all_gather x1 -> x0, waiting for transfers between devices: 36.8 us -> none  [per_device(): lax.all_gather((swish_out * up_act).astype(BF), ('x', 'c'), axis=1, tiled...]
    pallas_call x0 -> x7, Pallas kernels: none -> 23 us  [call(): pl.pallas_call(body, out_shape=[jax.ShapeDtypeStruct(s, d) for s, d in ou...]
    psum x1 -> x0, blocking collectives: 22.1 us -> none  [per_device(): dots = lax.psum(dots, ('x', 'c'))]
    ppermute x13 -> x17, starting transfers between devices: 54.3 us -> 70.3 us  [the longest x6 25.4 us: swap_core(): return lax.ppermute(x, 'c', [(0, 1), (1, 0)])]
    dot_general x6 -> x1, matrix products: 15.3 us -> 0.13 us  [per_device(): jnp.dot(member.astype(BF), earlier, preferred_element_type=F32)]
    all_to_all x0 -> x1, blocking collectives: none -> 14.6 us  [per_device(): lax.all_to_all(by_source.reshape(EXPERTS * NZ, CAP), ('y', 'z'), split_ax...]
    all_to_all x1 -> x0, starting transfers between devices: 13.2 us -> none  [per_device(): lax.all_to_all(dots.reshape(ny * nz, CAP), ('y', 'z'), split_axis=0, conc...]
    unnamed x28 -> x32, local copies, waits for them, and re-layouts: 0.07 us -> 5.47 us
  transfers between devices with their start and end apart: 15 -> 17, of which waited for: 10 -> 10; matrix products, arithmetic and copies ran while one was open for 6% -> 1% of each run, Pallas kernels for 0% -> 7%
where the time goes in v2:
time: 162 us; the launch traced here: 161 us
  starting transfers between devices  70.3 us (43%)
  blocking collectives  32.3 us (20%)
  waiting for transfers between devices  25.4 us (16%)
  Pallas kernels  23 us (14%)
  local copies, waits for them, and re-layouts  6.81 us (4%)
  other arithmetic  2.13 us (1%)
    ppermute x6, starting transfers between devices, swap_core(): return lax.ppermute(x, 'c', [(0, 1), (1, 0)])  25.4 us
    pallas_call x7, Pallas kernels, call(): pl.pallas_call(body, out_shape=[jax.ShapeDtypeStruct(s, d) for s, d in ou...  23 us
    ppermute x4, starting transfers between devices, ring(): lax.ppermute(x, ('z', 'c'), [(z * 2 + c, (z + 1 - 2 * c) % NZ * 2 + c) fo...  22.6 us
    ppermute x7, starting transfers between devices, swap_x(): lax.ppermute(x, ('x', 'c'), [(i * 2 + c, (i ^ masks[c]) * 2 + c) for i in...  22.4 us
    all_to_all x1, blocking collectives, per_device(): lax.all_to_all(packed.reshape(EXPERTS, CAP, width), 'y', split_axis=0, co...  17.6 us
    all_to_all x1, blocking collectives, per_device(): lax.all_to_all(by_source.reshape(EXPERTS * NZ, CAP), ('y', 'z'), split_ax...  14.6 us
    ppermute x7, waiting for transfers between devices, swap_x(): lax.ppermute(x, ('x', 'c'), [(i * 2 + c, (i ^ masks[c]) * 2 + c) for i in...  14.1 us
    ppermute x4, waiting for transfers between devices, ring(): lax.ppermute(x, ('z', 'c'), [(z * 2 + c, (z + 1 - 2 * c) % NZ * 2 + c) fo...  8.3 us
  transfers between devices with their start and end apart: 17, of which 10 were waited for; matrix products, arithmetic and copies ran while one was open for 1% of the time, Pallas kernels for 7%

profile of v2, /device:TPU:1, one launch (start us, length us, event | category | flops | bytes accessed | tf_op | source)
XLA Modules:
  0.0 161.1 jit_solution(6705160866467038530)
XLA Ops:
  3.3 17.6 %all_to_all.14 = bf16[8,24,768]{2,1,0:T(8,128)(2,1)S(1)} all-to-all(bf16[8,24,768]{2,1,0:T(8,128)(2,1)S(1)} %bitcast.31), channel_id=1, replica_groups=mesh['y'=8,'z'=8,'x'=4,'c'=2] {'y'}, dimensions={0} | all-to-all | bytes 589824 | tf_op jit(solution)/shard_map/all_to_all | solution.py:158
  21.0 5.2 %collective-permute-start = (bf16[192,768]{1,0:T(8,128)(2,1)S(1)}, bf16[192,768]{1,0:T(8,128)(2,1)S(1)}, u32[]{:S(2)}, u32[]{:S(2)}) collective-permute-start(bf16[192,768]{1,0:T(8,128)(2,1)S(1)} %bitcast.37), channel_id=1, source_target_pairs={{0,1},{1,0},{2,3},{3,2},{4,5},{5,4},{6,7},{7,6},{8,9},{9,8},{10,11... | collective-permute-start | bytes 884744 | tf_op jit(solution)/shard_map/ppermute | solution.py:137
  27.5 10.7 %collective-permute-start.1 = (bf16[2,192,768]{2,1,0:T(8,128)(2,1)S(1)}, bf16[2,192,768]{2,1,0:T(8,128)(2,1)S(1)}, u32[]{:S(2)}, u32[]{:S(2)}) collective-permute-start(bf16[2,192,768]{2,1,0:T(8,128)(2,1)S(1)} %pad_maximum_fusion.refs_1_), channel_id=1, source_target_pairs={{0,8},{1,57},{8,16},{9,1},{16,24},{17,9},{24,32},{25,17},{32,40},{... | collective-permute-start | bytes 1769480 | tf_op jit(solution)/shard_map/ppermute | solution.py:140
  38.1 1.9 %collective-permute-start.10 = (bf16[1024,768]{1,0:T(8,128)(2,1)}, bf16[1024,768]{1,0:T(8,128)(2,1)}, u32[]{:S(2)}, u32[]{:S(2)}) collective-permute-start(bf16[1024,768]{1,0:T(8,128)(2,1)} %refs_6_.3), channel_id=1, source_target_pairs={{0,1},{1,0},{2,3},{3,2},{4,5},{5,4},{6,7},{7,6},{8,9},{9,8},{10,11... | collective-permute-start | bytes 4718600 | tf_op jit(solution)/shard_map/ppermute | solution.py:137
  40.1 4.9 %collective-permute-done.1.refs_2_ = bf16[2,192,768]{2,1,0:T(8,128)(2,1)S(1)} collective-permute-done((bf16[2,192,768]{2,1,0:T(8,128)(2,1)S(1)}, bf16[2,192,768]{2,1,0:T(8,128)(2,1)S(1)}, u32[]{:S(2)}, u32[]{:S(2)}) %collective-permute-start.1) | collective-permute-done | bytes 589856 | tf_op jit(solution)/shard_map/ppermute | solution.py:140
  45.0 5.0 %collective-permute-start.2 = (bf16[2,192,768]{2,1,0:T(8,128)(2,1)S(1)}, bf16[2,192,768]{2,1,0:T(8,128)(2,1)S(1)}, u32[]{:S(2)}, u32[]{:S(2)}) collective-permute-start(bf16[2,192,768]{2,1,0:T(8,128)(2,1)S(1)} %collective-permute-done.1.refs_2_), channel_id=1, source_target_pairs={{0,8},{1,57},{8,16},{9,1},{16,24},{17,9},{24,32},{25,17},{32,40},{... | collective-permute-start | bytes 1769480 | tf_op jit(solution)/shard_map/ppermute | solution.py:140
  54.8 2.0 %collective-permute-done.2.refs_3_ = bf16[2,192,768]{2,1,0:T(8,128)(2,1)S(1)} collective-permute-done((bf16[2,192,768]{2,1,0:T(8,128)(2,1)S(1)}, bf16[2,192,768]{2,1,0:T(8,128)(2,1)S(1)}, u32[]{:S(2)}, u32[]{:S(2)}) %collective-permute-start.2) | collective-permute-done | bytes 589856 | tf_op jit(solution)/shard_map/ppermute | solution.py:140
  56.8 5.0 %collective-permute-start.3 = (bf16[2,192,768]{2,1,0:T(8,128)(2,1)S(1)}, bf16[2,192,768]{2,1,0:T(8,128)(2,1)S(1)}, u32[]{:S(2)}, u32[]{:S(2)}) collective-permute-start(bf16[2,192,768]{2,1,0:T(8,128)(2,1)S(1)} %collective-permute-done.2.refs_3_), channel_id=1, source_target_pairs={{0,8},{1,57},{8,16},{9,1},{16,24},{17,9},{24,32},{25,17},{32,40},{... | collective-permute-start | bytes 1769480 | tf_op jit(solution)/shard_map/ppermute | solution.py:140
  61.9 4.4 %collective-permute-start.7 = (bf16[768,256]{1,0:T(8,128)(2,1)S(1)}, bf16[768,256]{1,0:T(8,128)(2,1)S(1)}, u32[]{:S(2)}, u32[]{:S(2)}) collective-permute-start(bf16[768,256]{1,0:T(8,128)(2,1)S(1)} %pad_maximum_fusion.1.refs_6_.refs_8_), channel_id=1, source_target_pairs={{0,2},{1,7},{2,0},{3,5},{4,6},{5,3},{6,4},{7,1},{8,10},{9,15},{10,... | collective-permute-start | bytes 1179656 | tf_op jit(solution)/shard_map/ppermute | solution.py:146
  66.3 5.6 %collective-permute-done.7.refs_8_ = bf16[768,256]{1,0:T(8,128)(2,1)S(1)} collective-permute-done((bf16[768,256]{1,0:T(8,128)(2,1)S(1)}, bf16[768,256]{1,0:T(8,128)(2,1)S(1)}, u32[]{:S(2)}, u32[]{:S(2)}) %collective-permute-start.7) | collective-permute-done | bytes 393248 | tf_op jit(solution)/shard_map/ppermute | solution.py:146
  76.5 3.4 %collective-permute-start.6 = (bf16[768,256]{1,0:T(8,128)(2,1)S(1)}, bf16[768,256]{1,0:T(8,128)(2,1)}, u32[]{:S(2)}, u32[]{:S(2)}) collective-permute-start(bf16[768,256]{1,0:T(8,128)(2,1)S(1)} %pad_maximum_fusion.1.refs_6_.refs_8_), channel_id=1, source_target_pairs={{0,6},{1,3},{2,4},{3,1},{4,2},{5,7},{6,0},{7,5},{8,14},{9,11},{10,... | collective-permute-start | bytes 1179656 | tf_op jit(solution)/shard_map/ppermute | solution.py:146
  82.3 6.1 %shard_map.125 = (bf16[768,512]{1,0:T(8,128)(2,1)S(1)}, f32[8,768]{1,0:T(8,128)S(1)}) custom-call(s32[40]{0:T(128)S(1)} %concatenate.28.table.refs_0_, bf16[2,192,768]{2,1,0:T(8,128)(2,1)S(1)} %pad_maximum_fusion.refs_1_, bf16[2,192,768]{2,1,0:T(8,128)(2,1)S(1)} %collective-permute-done.1.refs_2_, bf16[2,192,768]{2,1,0:T(8,128)(2,1)S(1)} %collective-permute-done.2.refs_3_, ...), custom_call_target="tpu_custom_call" | custom-call | flops 1207959552 | bytes 6000000 | tf_op jit(solution)/shard_map/pallas_call | solution.py:26
  89.3 6.2 %shard_map.124 = (f32[768,512]{1,0:T(8,128)S(1)}, f32[8,768]{1,0:T(8,128)S(1)}) custom-call(s32[40]{0:T(128)S(1)} %concatenate.28.table.refs_0_, bf16[2,192,768]{2,1,0:T(8,128)(2,1)S(1)} %pad_maximum_fusion.refs_1_, bf16[2,192,768]{2,1,0:T(8,128)(2,1)S(1)} %collective-permute-done.1.refs_2_, bf16[2,192,768]{2,1,0:T(8,128)(2,1)S(1)} %collective-permute-done.2.refs_3_, ...), custom_call_target="tpu_custom_call" | custom-call | flops 1207959552 | bytes 6000000 | tf_op jit(solution)/shard_map/pallas_call | solution.py:26
  97.1 4.7 %collective-permute-start.11 = (bf16[768,512]{1,0:T(8,128)(2,1)}, bf16[768,512]{1,0:T(8,128)(2,1)S(1)}, u32[]{:S(2)}, u32[]{:S(2)}) collective-permute-start(bf16[768,512]{1,0:T(8,128)(2,1)} %copy-done.11), channel_id=1, source_target_pairs={{0,2},{1,7},{2,0},{3,5},{4,6},{5,3},{6,4},{7,1},{8,10},{9,15},{10,... | collective-permute-start | bytes 2359304 | tf_op jit(solution)/shard_map/ppermute | solution.py:146
  101.9 14.6 %all_to_all.15 = f32[64,1,24]{2,1,0:T(1,128)S(1)} all-to-all(f32[64,1,24]{2,1,0:T(1,128)S(1)} %bitcast.40), channel_id=1, replica_groups=mesh['y'=8,'z'=8,'x'=4,'c'=2] {'y','z'}, dimensions={0} | all-to-all | bytes 12288 | tf_op jit(solution)/shard_map/all_to_all | solution.py:213
  116.6 7.5 %collective-permute-start.14 = (f32[8,24]{1,0:T(8,128)S(1)}, f32[8,24]{1,0:T(8,128)S(1)}, u32[]{:S(2)}, u32[]{:S(2)}) collective-permute-start(f32[8,24]{1,0:T(8,128)S(1)} %bitcast_reduce_fusion), channel_id=1, source_target_pairs={{0,1},{1,0},{2,3},{3,2},{4,5},{5,4},{6,7},{7,6},{8,9},{9,8},{10,11... | collective-permute-start | bytes 2312 | tf_op jit(solution)/shard_map/ppermute | solution.py:137
  124.9 3.3 %collective-permute-start.15 = (f32[8,24]{1,0:T(8,128)S(1)}, f32[8,24]{1,0:T(8,128)S(1)}, u32[]{:S(2)}, u32[]{:S(2)}) collective-permute-start(f32[8,24]{1,0:T(8,128)S(1)} %add.82), channel_id=1, source_target_pairs={{0,2},{1,7},{2,0},{3,5},{4,6},{5,3},{6,4},{7,1},{8,10},{9,15},{10,... | collective-permute-start | bytes 2312 | tf_op jit(solution)/shard_map/ppermute | solution.py:146
  128.2 3.4 %shard_map.122 = bf16[1024,768]{1,0:T(8,128)(2,1)S(1)} custom-call(s32[40]{0:T(128)S(1)} %concatenate.28.table.refs_0_, bf16[2,192,768]{2,1,0:T(8,128)(2,1)S(1)} %pad_maximum_fusion.refs_1_, bf16[2,192,768]{2,1,0:T(8,128)(2,1)S(1)} %collective-permute-done.1.refs_2_, bf16[2,192,768]{2,1,0:T(8,128)(2,1)S(1)} %collective-permute-done.2.refs_3_, ...), custom_call_target="tpu_custom_call" | custom-call | flops 1207959552 | bytes 5000000 | tf_op jit(solution)/shard_map/pallas_call | solution.py:26
  131.5 2.3 %collective-permute-start.9 = (bf16[1024,768]{1,0:T(8,128)(2,1)S(1)}, bf16[1024,768]{1,0:T(8,128)(2,1)S(1)}, u32[]{:S(2)}, u32[]{:S(2)}) collective-permute-start(bf16[1024,768]{1,0:T(8,128)(2,1)S(1)} %shard_map.122), channel_id=1, source_target_pairs={{0,1},{1,0},{2,3},{3,2},{4,5},{5,4},{6,7},{7,6},{8,9},{9,8},{10,11... | collective-permute-start | bytes 4718600 | tf_op jit(solution)/shard_map/ppermute | solution.py:137
  133.9 2.4 %collective-permute-start.16 = (f32[8,24]{1,0:T(8,128)S(1)}, f32[8,24]{1,0:T(8,128)S(1)}, u32[]{:S(2)}, u32[]{:S(2)}) collective-permute-start(f32[8,24]{1,0:T(8,128)S(1)} %add.83), channel_id=1, source_target_pairs={{0,6},{1,3},{2,4},{3,1},{4,2},{5,7},{6,0},{7,5},{8,14},{9,11},{10,... | collective-permute-start | bytes 2312 | tf_op jit(solution)/shard_map/ppermute | solution.py:146
  138.5 2.4 %collective-permute-start.12 = (bf16[768,256]{1,0:T(8,128)(2,1)S(1)}, bf16[768,256]{1,0:T(8,128)(2,1)S(1)}, u32[]{:S(2)}, u32[]{:S(2)}) collective-permute-start(bf16[768,256]{1,0:T(8,128)(2,1)S(1)} %slice.69), channel_id=1, source_target_pairs={{0,6},{1,3},{2,4},{3,1},{4,2},{5,7},{6,0},{7,5},{8,14},{9,11},{10,... | collective-permute-start | bytes 1179656 | tf_op jit(solution)/shard_map/ppermute | solution.py:146
  141.7 5.7 %collective-permute-done.12 = bf16[768,256]{1,0:T(8,128)(2,1)S(1)} collective-permute-done((bf16[768,256]{1,0:T(8,128)(2,1)S(1)}, bf16[768,256]{1,0:T(8,128)(2,1)S(1)}, u32[]{:S(2)}, u32[]{:S(2)}) %collective-permute-start.12) | collective-permute-done | bytes 393248 | tf_op jit(solution)/shard_map/ppermute | solution.py:146
  147.5 6.5 %collective-permute-start.13 = (bf16[768,128]{1,0:T(8,128)(2,1)S(1)}, bf16[768,128]{1,0:T(8,128)(2,1)S(1)}, u32[]{:S(2)}, u32[]{:S(2)}) collective-permute-start(bf16[768,128]{1,0:T(8,128)(2,1)S(1)} %select_convert_fusion), channel_id=1, source_target_pairs={{0,1},{1,0},{2,3},{3,2},{4,5},{5,4},{6,7},{7,6},{8,9},{9,8},{10,11... | collective-permute-start | bytes 589832 | tf_op jit(solution)/shard_map/ppermute | solution.py:137
  156.6 4.5 %shard_map.123 = bf16[1024,768]{1,0:T(8,128)(2,1)} custom-call(s32[40]{0:T(128)S(1)} %concatenate.28.table.refs_0_, bf16[2,192,768]{2,1,0:T(8,128)(2,1)S(1)} %pad_maximum_fusion.refs_1_, bf16[2,192,768]{2,1,0:T(8,128)(2,1)S(1)} %collective-permute-done.1.refs_2_, bf16[2,192,768]{2,1,0:T(8,128)(2,1)S(1)} %collective-permute-done.2.refs_3_, ...), custom_call_target="tpu_custom_call" | custom-call | flops 1207959552 | bytes 5000000 | tf_op jit(solution)/shard_map/pallas_call | solution.py:26
  (85 shorter events, 24.8 us)
Async XLA Ops:
  0.6 49.3 %copy-start.14 = (s32[8]{0:T(128)S(1)}, s32[8]{0:T(128)}, u32[]{:S(2)}) copy-start(s32[8]{0:T(128)} %constant.74.clone) | copy-start | bytes 100
  0.6 49.3 %copy-start.15 = (s32[8]{0:T(128)S(1)}, s32[8]{0:T(128)}, u32[]{:S(2)}) copy-start(s32[8]{0:T(128)} %constant.75.clone) | copy-start | bytes 100
  0.7 49.3 %copy-start.13 = (s32[8]{0:T(128)S(1)}, s32[8]{0:T(128)}, u32[]{:S(2)}) copy-start(s32[8]{0:T(128)} %constant.73.clone) | copy-start | bytes 100
  0.7 49.5 %copy-start.6 = (bf16[1536,128]{1,0:T(8,128)(2,1)S(1)}, bf16[1536,128]{1,0:T(8,128)(2,1)}, u32[]{:S(2)}) copy-start(bf16[1536,128]{1,0:T(8,128)(2,1)} %param.13) | copy-start | bytes 1179652
  0.7 49.5 %copy-start.7 = (bf16[1536,128]{1,0:T(8,128)(2,1)S(1)}, bf16[1536,128]{1,0:T(8,128)(2,1)}, u32[]{:S(2)}) copy-start(bf16[1536,128]{1,0:T(8,128)(2,1)} %param.14) | copy-start | bytes 1179652
  21.0 6.4 %collective-permute-start = (bf16[192,768]{1,0:T(8,128)(2,1)S(1)}, bf16[192,768]{1,0:T(8,128)(2,1)S(1)}, u32[]{:S(2)}, u32[]{:S(2)}) collective-permute-start(bf16[192,768]{1,0:T(8,128)(2,1)S(1)} %bitcast.37), channel_id=1, source_target_pairs={{0,1},{1,0},{2,3},{3,2},{4,5},{5,4},{6,7},{7,6},{8,9},{9,8},{10,11... | collective-permute-start | bytes 884744 | tf_op jit(solution)/shard_map/ppermute | solution.py:137
  27.5 17.5 %collective-permute-start.1 = (bf16[2,192,768]{2,1,0:T(8,128)(2,1)S(1)}, bf16[2,192,768]{2,1,0:T(8,128)(2,1)S(1)}, u32[]{:S(2)}, u32[]{:S(2)}) collective-permute-start(bf16[2,192,768]{2,1,0:T(8,128)(2,1)S(1)} %pad_maximum_fusion.refs_1_), channel_id=1, source_target_pairs={{0,8},{1,57},{8,16},{9,1},{16,24},{17,9},{24,32},{25,17},{32,40},{... | collective-permute-start | bytes 1769480 | tf_op jit(solution)/shard_map/ppermute | solution.py:140
  38.1 42.7 %collective-permute-start.10 = (bf16[1024,768]{1,0:T(8,128)(2,1)}, bf16[1024,768]{1,0:T(8,128)(2,1)}, u32[]{:S(2)}, u32[]{:S(2)}) collective-permute-start(bf16[1024,768]{1,0:T(8,128)(2,1)} %refs_6_.3), channel_id=1, source_target_pairs={{0,1},{1,0},{2,3},{3,2},{4,5},{5,4},{6,7},{7,6},{8,9},{9,8},{10,11... | collective-permute-start | bytes 4718600 | tf_op jit(solution)/shard_map/ppermute | solution.py:137
  45.0 11.8 %collective-permute-start.2 = (bf16[2,192,768]{2,1,0:T(8,128)(2,1)S(1)}, bf16[2,192,768]{2,1,0:T(8,128)(2,1)S(1)}, u32[]{:S(2)}, u32[]{:S(2)}) collective-permute-start(bf16[2,192,768]{2,1,0:T(8,128)(2,1)S(1)} %collective-permute-done.1.refs_2_), channel_id=1, source_target_pairs={{0,8},{1,57},{8,16},{9,1},{16,24},{17,9},{24,32},{25,17},{32,40},{... | collective-permute-start | bytes 1769480 | tf_op jit(solution)/shard_map/ppermute | solution.py:140
  52.8 9.0 %collective-permute-start.5 = (bf16[768,128]{1,0:T(8,128)(2,1)S(1)}, bf16[768,128]{1,0:T(8,128)(2,1)S(1)}, u32[]{:S(2)}, u32[]{:S(2)}) collective-permute-start(bf16[768,128]{1,0:T(8,128)(2,1)S(1)} %get-tuple-element.15), channel_id=1, source_target_pairs={{0,1},{1,0},{2,3},{3,2},{4,5},{5,4},{6,7},{7,6},{8,9},{9,8},{10,11... | collective-permute-start | bytes 589832 | tf_op jit(solution)/shard_map/ppermute | solution.py:137
  56.8 17.1 %collective-permute-start.3 = (bf16[2,192,768]{2,1,0:T(8,128)(2,1)S(1)}, bf16[2,192,768]{2,1,0:T(8,128)(2,1)S(1)}, u32[]{:S(2)}, u32[]{:S(2)}) collective-permute-start(bf16[2,192,768]{2,1,0:T(8,128)(2,1)S(1)} %collective-permute-done.2.refs_3_), channel_id=1, source_target_pairs={{0,8},{1,57},{8,16},{9,1},{16,24},{17,9},{24,32},{25,17},{32,40},{... | collective-permute-start | bytes 1769480 | tf_op jit(solution)/shard_map/ppermute | solution.py:140
  61.9 10.0 %collective-permute-start.7 = (bf16[768,256]{1,0:T(8,128)(2,1)S(1)}, bf16[768,256]{1,0:T(8,128)(2,1)S(1)}, u32[]{:S(2)}, u32[]{:S(2)}) collective-permute-start(bf16[768,256]{1,0:T(8,128)(2,1)S(1)} %pad_maximum_fusion.1.refs_6_.refs_8_), channel_id=1, source_target_pairs={{0,2},{1,7},{2,0},{3,5},{4,6},{5,3},{6,4},{7,1},{8,10},{9,15},{10,... | collective-permute-start | bytes 1179656 | tf_op jit(solution)/shard_map/ppermute | solution.py:146
  71.9 8.9 %collective-permute-start.8 = (bf16[768,256]{1,0:T(8,128)(2,1)S(1)}, bf16[768,256]{1,0:T(8,128)(2,1)}, u32[]{:S(2)}, u32[]{:S(2)}) collective-permute-start(bf16[768,256]{1,0:T(8,128)(2,1)S(1)} %collective-permute-done.7.refs_8_), channel_id=1, source_target_pairs={{0,6},{1,3},{2,4},{3,1},{4,2},{5,7},{6,0},{7,5},{8,14},{9,11},{10,... | collective-permute-start | bytes 1179656 | tf_op jit(solution)/shard_map/ppermute | solution.py:146
  74.6 7.7 %collective-permute-start.4 = (bf16[2,96,768]{2,1,0:T(8,128)(2,1)}, bf16[2,96,768]{2,1,0:T(8,128)(2,1)S(1)}, u32[]{:S(2)}, u32[]{:S(2)}) collective-permute-start(bf16[2,96,768]{2,1,0:T(8,128)(2,1)} %constant_dynamic-slice_fusion), channel_id=1, source_target_pairs={{0,8},{1,57},{8,16},{9,1},{16,24},{17,9},{24,32},{25,17},{32,40},{... | collective-permute-start | bytes 884744 | tf_op jit(solution)/shard_map/ppermute | solution.py:140
  76.5 12.8 %collective-permute-start.6 = (bf16[768,256]{1,0:T(8,128)(2,1)S(1)}, bf16[768,256]{1,0:T(8,128)(2,1)}, u32[]{:S(2)}, u32[]{:S(2)}) collective-permute-start(bf16[768,256]{1,0:T(8,128)(2,1)S(1)} %pad_maximum_fusion.1.refs_6_.refs_8_), channel_id=1, source_target_pairs={{0,6},{1,3},{2,4},{3,1},{4,2},{5,7},{6,0},{7,5},{8,14},{9,11},{10,... | collective-permute-start | bytes 1179656 | tf_op jit(solution)/shard_map/ppermute | solution.py:146
  89.3 34.8 %copy-start.10 = (s32[64,2]{0,1:T(2,128)S(1)}, s32[64,2]{0,1:T(2,128)}, u32[]{:S(2)}) copy-start(s32[64,2]{0,1:T(2,128)} %param.10) | copy-start | bytes 1540
  97.1 41.1 %collective-permute-start.11 = (bf16[768,512]{1,0:T(8,128)(2,1)}, bf16[768,512]{1,0:T(8,128)(2,1)S(1)}, u32[]{:S(2)}, u32[]{:S(2)}) collective-permute-start(bf16[768,512]{1,0:T(8,128)(2,1)} %copy-done.11), channel_id=1, source_target_pairs={{0,2},{1,7},{2,0},{3,5},{4,6},{5,3},{6,4},{7,1},{8,10},{9,15},{10,... | collective-permute-start | bytes 2359304 | tf_op jit(solution)/shard_map/ppermute | solution.py:146
  116.6 8.3 %collective-permute-start.14 = (f32[8,24]{1,0:T(8,128)S(1)}, f32[8,24]{1,0:T(8,128)S(1)}, u32[]{:S(2)}, u32[]{:S(2)}) collective-permute-start(f32[8,24]{1,0:T(8,128)S(1)} %bitcast_reduce_fusion), channel_id=1, source_target_pairs={{0,1},{1,0},{2,3},{3,2},{4,5},{5,4},{6,7},{7,6},{8,9},{9,8},{10,11... | collective-permute-start | bytes 2312 | tf_op jit(solution)/shard_map/ppermute | solution.py:137
  124.9 8.9 %collective-permute-start.15 = (f32[8,24]{1,0:T(8,128)S(1)}, f32[8,24]{1,0:T(8,128)S(1)}, u32[]{:S(2)}, u32[]{:S(2)}) collective-permute-start(f32[8,24]{1,0:T(8,128)S(1)} %add.82), channel_id=1, source_target_pairs={{0,2},{1,7},{2,0},{3,5},{4,6},{5,3},{6,4},{7,1},{8,10},{9,15},{10,... | collective-permute-start | bytes 2312 | tf_op jit(solution)/shard_map/ppermute | solution.py:146
  131.5 25.0 %collective-permute-start.9 = (bf16[1024,768]{1,0:T(8,128)(2,1)S(1)}, bf16[1024,768]{1,0:T(8,128)(2,1)S(1)}, u32[]{:S(2)}, u32[]{:S(2)}) collective-permute-start(bf16[1024,768]{1,0:T(8,128)(2,1)S(1)} %shard_map.122), channel_id=1, source_target_pairs={{0,1},{1,0},{2,3},{3,2},{4,5},{5,4},{6,7},{7,6},{8,9},{9,8},{10,11... | collective-permute-start | bytes 4718600 | tf_op jit(solution)/shard_map/ppermute | solution.py:137
  133.9 4.4 %collective-permute-start.16 = (f32[8,24]{1,0:T(8,128)S(1)}, f32[8,24]{1,0:T(8,128)S(1)}, u32[]{:S(2)}, u32[]{:S(2)}) collective-permute-start(f32[8,24]{1,0:T(8,128)S(1)} %add.83), channel_id=1, source_target_pairs={{0,6},{1,3},{2,4},{3,1},{4,2},{5,7},{6,0},{7,5},{8,14},{9,11},{10,... | collective-permute-start | bytes 2312 | tf_op jit(solution)/shard_map/ppermute | solution.py:146
  138.5 8.8 %collective-permute-start.12 = (bf16[768,256]{1,0:T(8,128)(2,1)S(1)}, bf16[768,256]{1,0:T(8,128)(2,1)S(1)}, u32[]{:S(2)}, u32[]{:S(2)}) collective-permute-start(bf16[768,256]{1,0:T(8,128)(2,1)S(1)} %slice.69), channel_id=1, source_target_pairs={{0,6},{1,3},{2,4},{3,1},{4,2},{5,7},{6,0},{7,5},{8,14},{9,11},{10,... | collective-permute-start | bytes 1179656 | tf_op jit(solution)/shard_map/ppermute | solution.py:146
  141.6 13.4 %copy-start.5 = (f32[1536,128]{1,0:T(8,128)S(1)}, f32[1536,128]{1,0:T(8,128)}, u32[]{:S(2)}) copy-start(f32[1536,128]{1,0:T(8,128)} %copy-done.4) | copy-start | bytes 2359300
  147.5 7.5 %collective-permute-start.13 = (bf16[768,128]{1,0:T(8,128)(2,1)S(1)}, bf16[768,128]{1,0:T(8,128)(2,1)S(1)}, u32[]{:S(2)}, u32[]{:S(2)}) collective-permute-start(bf16[768,128]{1,0:T(8,128)(2,1)S(1)} %select_convert_fusion), channel_id=1, source_target_pairs={{0,1},{1,0},{2,3},{3,2},{4,5},{5,4},{6,7},{7,6},{8,9},{9,8},{10,11... | collective-permute-start | bytes 589832 | tf_op jit(solution)/shard_map/ppermute | solution.py:137
  (9 other events, 35.0 us)

commit v3 on v2

--- a/solution.py
+++ b/solution.py
@@ -21,13 +21,15 @@
 SM = pl.BlockSpec(memory_space=pltpu.SMEM)
 
 
-def call(body, outs, ins, cost):
+def call(body, outs, ins, cost, scratch=(), aliases={}):
     specs = [SM if a.dtype == jnp.int32 and a.shape == (40,) else VM for a in ins]
     return pl.pallas_call(
         body,
         out_shape=[jax.ShapeDtypeStruct(s, d) for s, d in outs],
         in_specs=specs,
         out_specs=[VM] * len(outs),
+        scratch_shapes=[pltpu.VMEM(s, BF) for s in scratch],
+        input_output_aliases=aliases,
         compiler_params=pltpu.CompilerParams(vmem_limit_bytes=48 * 2**20),
         cost_estimate=pl.CostEstimate(flops=cost[0], bytes_accessed=cost[1], transcendentals=0),
     )(*ins)
@@ -55,53 +57,74 @@
     out[...] = dot(jnp.concatenate(chosen, axis=0).astype(BF), rows[...], 1, 0).astype(BF)
 
 
-def act_body(table, gate, up, mine, other, by_gate, by_up):
+def act_body(table, gate, up, hidden, by_gate, by_up):
+    core = table[36]
     for g in range(16):
         zs, half = table[g], table[16 + g]
         a = gate[pl.ds(half * 4, 4), zs].astype(F32).reshape(HALF, 128)
         b = up[pl.ds(half * 4, 4), zs].astype(F32).reshape(HALF, 128)
         sig = 1.0 / (1.0 + jnp.exp(-a))
         swish = a * sig
-        at = pl.ds((g % 8) * HALF, HALF)
-        (mine if g < 8 else other)[at, :] = (swish * b).astype(BF)
+        hidden[core if g < 8 else 1 - core, pl.ds((g % 8) * HALF, HALF), :] = (swish * b).astype(BF)
         by_gate[pl.ds(g * HALF, HALF), :] = b * sig * (1.0 + a * (1.0 - sig))
         by_up[pl.ds(g * HALF, HALF), :] = swish
 
 
-def product_body(labels, table, r0, r1, r2, r3, r4, w_own, w_other, ha, hb, out, dots):
-    ones = jnp.ones((8, 256), F32)
-    core = table[36]
-    first = pl.ds(pl.multiple_of(core * HALF, HALF), HALF)
-    for piece, (ref, size, start) in enumerate(zip((r0, r1, r2, r3, r4), SIZES, STARTS)):
-        rows = first if piece == 0 else pl.ds(0, size)
-        own, other = ref[0, rows, :], ref[1, rows, :]
-        total = None
-        for i, h in enumerate((ha, hb)):
-            at = pl.ds(pl.multiple_of(table[32 + labels[i]] * 256, 256), 256)
-            part = dot(own, w_own[at, :], 1, 1) + dot(other, w_other[at, :], 1, 1)
-            out[pl.ds(start, size), pl.ds(i * 256, 256)] = part.astype(out.dtype)
-            term = part * h[pl.ds(start, size), :].astype(F32)
+def half_of(core):
+    return pl.ds(pl.multiple_of(core * HALF, HALF), HALF)
+
+
+def product(table, own, other, w_own, w_other, hidden, start, send, keep, dots):
+    core = table[36]
+    size = own.shape[0]
+    at = pl.ds(start, size)
+    total = None
+    for label in (2, 3, 0, 1):
+        unit = table[32 + label]
+        w = pl.ds(pl.multiple_of(unit * 256, 256), 256)
+        part = dot(own[...], w_own[w, :], 1, 1) + dot(other[...], w_other[w, :], 1, 1)
+        if label >= 2:
+            send[at, pl.ds((label - 2) * 256, 256)] = part.astype(BF)
+        else:
+            keep[at, pl.ds(label * 256, 256)] = part
+        for i in range(2):
+            term = part[:, i * 128 : i * 128 + 128] * hidden[2 * unit + i, core, at, :].astype(F32)
             total = term if total is None else total + term
-        dots[:, pl.ds(start, size)] = lax.dot_general(
-            ones, total, (((1,), (1,)), ((), ())), precision=lax.Precision.HIGHEST,
-            preferred_element_type=F32,
-        )
-
-
-def weight_body(which, table, r0, r1, r2, r3, r4, h0, h1, h2, h3, *rest):
-    out = rest[-1]
-    core = table[36]
-    first = pl.ds(pl.multiple_of(core * HALF, HALF), HALF)
-    for label, h in enumerate((h0, h1, h2, h3)):
-        total = None
-        for piece, (ref, size, start) in enumerate(zip((r0, r1, r2, r3, r4), SIZES, STARTS)):
-            rows = first if piece == 0 else pl.ds(0, size)
-            term = dot(h[pl.ds(start, size), :], ref[which, rows, :], 0, 0)
-            total = term if total is None else total + term
-        at = pl.ds(pl.multiple_of(table[32 + label] * 256, 256), 256)
-        if len(rest) == 2:
-            total = total + rest[0][at, :].astype(F32)
-        out[at, :] = total.astype(BF)
+    dots[...] = lax.dot_general(
+        jnp.ones((8, 128), F32), total, (((1,), (1,)), ((), ())),
+        precision=lax.Precision.HIGHEST, preferred_element_type=F32,
+    )
+
+
+def near_body(table, r0, r1, r2, r3, w_own, w_other, hidden, send, keep, dots, own, other):
+    core = table[36]
+    for side, dst in enumerate((own, other)):
+        dst[pl.ds(0, HALF), :] = r0[side, half_of(core), :]
+        for piece, ref in enumerate((r1, r2, r3)):
+            dst[pl.ds(STARTS[piece + 1], BLOCK), :] = ref[side]
+    product(table, own, other, w_own, w_other, hidden, 0, send, keep, dots)
+
+
+def far_body(table, r4, w_own, w_other, hidden, send_in, keep_in, send, keep, dots, own, other):
+    del send_in, keep_in
+    own[...] = r4[0]
+    other[...] = r4[1]
+    product(table, own, other, w_own, w_other, hidden, STARTS[4], send, keep, dots)
+
+
+def weight_body(table, r0, r1, r2, r3, r4, lent, hidden, out, rows, units):
+    core = table[36]
+    rows[pl.ds(0, HALF), :] = r0[0, half_of(core), :]
+    for ref, size, start in zip((r1, r2, r3, r4), SIZES[1:], STARTS[1:]):
+        rows[pl.ds(start, size), :] = ref[0]
+    rows[pl.ds(MINE, HALF), :] = r0[0, half_of(1 - core), :]
+    rows[pl.ds(MINE + HALF, MINE - HALF), :] = lent[...]
+    for pair in range(4):
+        for i in range(2):
+            lanes = pl.ds(i * 128, 128)
+            units[pl.ds(0, MINE), lanes] = hidden[2 * pair + i, core]
+            units[pl.ds(MINE, MINE), lanes] = hidden[2 * pair + i, 1 - core]
+        out[pl.ds(pair * 256, 256), :] = dot(units[...], rows[...], 0, 0).astype(BF)
 
 
 def grad_body(table, kept, got, by_gate, by_up, gate_out, up_out):
@@ -147,10 +170,6 @@
             x, ("x", "c"), [(i * 2 + c, (i ^ masks[c]) * 2 + c) for i in range(NX) for c in range(2)]
         )
 
-    def pair(own, other):
-        low, high = jnp.where(ci == 0, own, other), jnp.where(ci == 0, other, own)
-        return jnp.concatenate([low, high], axis=1)
-
     routes_t, gates_t = routes.T, gates.T.astype(F32)
     (packed,) = call(
         pack_body, [((BLOCK, width), BF)], (routes_t, gates_t, grad_out), (2 * BLOCK * tokens * width, 400000)
@@ -161,34 +180,37 @@
     w_other = swap_core(w_down)
 
     view = (EXPERTS, NZ, CAP, 128)
-    mine, other, by_gate, by_up = call(
+    mine, by_gate, by_up = call(
         act_body,
-        [((MINE, 128), BF), ((MINE, 128), BF), ((2 * MINE, 128), F32), ((2 * MINE, 128), F32)],
+        [((2, MINE, 128), BF), ((2 * MINE, 128), F32), ((2 * MINE, 128), F32)],
         (table, gate_pre.reshape(view), up_pre.reshape(view)),
         (20 * 2 * MINE * 128, 3000000),
     )
-    h0 = pair(mine, swap_core(other))
-    h2 = swap_x(h0, True)
-    h1 = swap_x(h0, False)
-    h3 = swap_x(h2, False)
-
+    hidden = lax.all_gather(mine, ("x", "c"), axis=0)
+
+    own, w_other, mine = lax.optimization_barrier((own, w_other, mine))
     r0 = jnp.stack([own, swap_core(own)])
     r1 = ring(r0)
     r2 = ring(r1)
     r3 = ring(r2)
     r4 = ring(lax.dynamic_slice_in_dim(r3, ci * HALF, HALF, 1))
-    pieces = (r0, r1, r2, r3, r4)
-
-    def product(labels, ha, hb, dtype):
-        return call(
-            lambda *refs: product_body(labels, *refs),
-            [((MINE, 512), dtype), ((8, MINE), F32)],
-            (table, *pieces, w_down, w_other, ha, hb),
-            (2 * MINE * 512 * 2 * width, 6000000),
-        )
-
-    send, dots_a = product((2, 3), h2, h3, BF)
-    keep, dots_b = product((0, 1), h0, h1, F32)
+
+    outs = [((MINE, 512), BF), ((MINE, 512), F32)]
+    send, keep, dots_a = call(
+        near_body,
+        outs + [((8, STARTS[4]), F32)],
+        (table, r0, r1, r2, r3, w_down, w_other, hidden),
+        (2 * MINE * ff * 2 * width, 9000000),
+        ((STARTS[4], width),) * 2,
+    )
+    send, keep, dots_b = call(
+        far_body,
+        outs + [((8, HALF), F32)],
+        (table, r4, w_down, w_other, hidden, send, keep),
+        (2 * HALF * ff * 2 * width, 6000000),
+        ((HALF, width),) * 2,
+        {5: 0, 6: 1},
+    )
     part = keep + swap_x(send, True).astype(F32)
     whole = part[:, :256] + swap_x(part[:, 256:].astype(BF), False).astype(F32)
     low, high = whole[:, :128], whole[:, 128:]
@@ -198,7 +220,7 @@
         grad_body, [(view, BF), (view, BF)], (table, kept, got, by_gate, by_up), (4 * MINE * 128, 3000000)
     )
 
-    dots = (dots_a[0] + dots_b[0]).reshape(8, 4, CAP)
+    dots = jnp.concatenate([dots_a[0], dots_b[0]]).reshape(8, 4, CAP)
     zero = jnp.zeros((1, 4, CAP), F32)
     near = dots[1:7].reshape(3, EXPERTS, CAP)
     none = jnp.zeros_like(near)
@@ -227,16 +249,13 @@
     by_token = jnp.sum(jnp.where(chosen, totals[:, :, None], 0.0), axis=1)
     gate_grad = jnp.sum(jnp.where(named, by_token[None], 0.0), axis=1) / gates_t
 
-    hiddens = (h0, h1, h2, h3)
-    cost = (2 * MINE * ff * width, 5000000)
-    (lent,) = call(
-        lambda *refs: weight_body(1, *refs), [((ff, width), BF)], (table, *pieces, *hiddens), cost
-    )
+    lent = swap_core(jnp.concatenate([r1[1], r2[1], r3[1], r4[1]], axis=0))
     (w_down_grad,) = call(
-        lambda *refs: weight_body(0, *refs),
+        weight_body,
         [((ff, width), BF)],
-        (table, *pieces, *hiddens, swap_core(lent)),
-        cost,
+        (table, r0, r1, r2, r3, r4, lent, hidden),
+        (2 * 2 * MINE * ff * width, 9000000),
+        ((2 * MINE, width), (2 * MINE, 256)),
     )
     flat = (EXPERTS * NZ * CAP, 128)
     return (w_down_grad, gate_pre_grad.reshape(flat), up_pre_grad.reshape(flat), gate_grad.T)

time: 162 us -> 181 us (1.12)
  between operations: 1.11 us -> 14.4 us
  waiting for transfers between devices: 25.4 us -> 32 us
  local copies, waits for them, and re-layouts: 6.81 us -> 13.2 us
  starting transfers between devices: 70.3 us -> 65.1 us
  Pallas kernels: 23 us -> 19.2 us
  other arithmetic: 2.13 us -> 4.85 us
    ppermute x4, waiting for transfers between devices: 8.3 us -> 22.5 us  [ring(): lax.ppermute(x, ('z', 'c'), [(z * 2 + c, (z + 1 - 2 * c) % NZ * 2 + c) fo...]
    ppermute x7 -> x4, starting transfers between devices: 22.4 us -> 13.4 us  [swap_x(): lax.ppermute(x, ('x', 'c'), [(i * 2 + c, (i ^ masks[c]) * 2 + c) for i in...]
    ppermute x7 -> x4, waiting for transfers between devices: 14.1 us -> 6.43 us  [swap_x(): lax.ppermute(x, ('x', 'c'), [(i * 2 + c, (i ^ masks[c]) * 2 + c) for i in...]
    unnamed x32 -> x44, local copies, waits for them, and re-layouts: 5.47 us -> 11.5 us
    pallas_call x7 -> x6, Pallas kernels: 23 us -> 19.2 us  [call(): pl.pallas_call(body, out_shape=[jax.ShapeDtypeStruct(s, d) for s, d in ou...]
    all_to_all x1, blocking collectives: 17.6 us -> 15.1 us  [per_device(): lax.all_to_all(packed.reshape(EXPERTS, CAP, width), 'y', split_axis=0, co...]
    ppermute x4, starting transfers between devices: 22.6 us -> 24.5 us  [ring(): lax.ppermute(x, ('z', 'c'), [(z * 2 + c, (z + 1 - 2 * c) % NZ * 2 + c) fo...]
    ppermute x6 -> x5, starting transfers between devices: 25.4 us -> 27.1 us  [swap_core(): return lax.ppermute(x, 'c', [(0, 1), (1, 0)])]
  transfers between devices with their start and end apart: 17 -> 14, of which waited for: 10 -> 9; matrix products, arithmetic and copies ran while one was open for 1% -> 2% of each run, Pallas kernels for 7% -> 9%
where the time goes in v3:
time: 181 us; the launch traced here: 180 us
  starting transfers between devices  65.1 us (36%)
  waiting for transfers between devices  32 us (18%)
  blocking collectives  31.1 us (17%)
  Pallas kernels  19.2 us (11%)
  between operations  14.4 us (8%)
  local copies, waits for them, and re-layouts  13.2 us (7%)
  other arithmetic  4.85 us (3%)
    ppermute x5, starting transfers between devices, swap_core(): return lax.ppermute(x, 'c', [(0, 1), (1, 0)])  27.1 us
    ppermute x4, starting transfers between devices, ring(): lax.ppermute(x, ('z', 'c'), [(z * 2 + c, (z + 1 - 2 * c) % NZ * 2 + c) fo...  24.5 us
    ppermute x4, waiting for transfers between devices, ring(): lax.ppermute(x, ('z', 'c'), [(z * 2 + c, (z + 1 - 2 * c) % NZ * 2 + c) fo...  22.5 us
    pallas_call x6, Pallas kernels, call(): pl.pallas_call(body, out_shape=[jax.ShapeDtypeStruct(s, d) for s, d in ou...  19.2 us
    all_to_all x1, blocking collectives, per_device(): lax.all_to_all(by_source.reshape(EXPERTS * NZ, CAP), ('y', 'z'), split_ax...  16 us
    all_to_all x1, blocking collectives, per_device(): lax.all_to_all(packed.reshape(EXPERTS, CAP, width), 'y', split_axis=0, co...  15.1 us
    ppermute x4, starting transfers between devices, swap_x(): lax.ppermute(x, ('x', 'c'), [(i * 2 + c, (i ^ masks[c]) * 2 + c) for i in...  13.4 us
    unnamed x44, local copies, waits for them, and re-layouts  11.5 us
  transfers between devices with their start and end apart: 14, of which 9 were waited for; matrix products, arithmetic and copies ran while one was open for 2% of the time, Pallas kernels for 9%

profile of v3, /device:TPU:1, one launch (start us, length us, event | category | flops | bytes accessed | tf_op | source)
XLA Modules:
  0.0 180.0 jit_solution(3138824696926185501)
XLA Ops:
  13.4 8.8 %collective-permute-start = (bf16[1024,768]{1,0:T(8,128)(2,1)}, bf16[1024,768]{1,0:T(8,128)(2,1)S(1)}, u32[]{:S(2)}, u32[]{:S(2)}) collective-permute-start(bf16[1024,768]{1,0:T(8,128)(2,1)} %w_own.3), channel_id=1, source_target_pairs={{0,1},{1,0},{2,3},{3,2},{4,5},{5,4},{6,7},{7,6},{8,9},{9,8},{10,11... | collective-permute-start | bytes 4718600 | tf_op jit(solution)/shard_map/ppermute | solution.py:160
  24.7 15.1 %all_to_all.14 = bf16[8,24,768]{2,1,0:T(8,128)(2,1)S(1)} all-to-all(bf16[8,24,768]{2,1,0:T(8,128)(2,1)S(1)} %bitcast.40), channel_id=1, replica_groups=mesh['y'=8,'z'=8,'x'=4,'c'=2] {'y'}, dimensions={0} | all-to-all | bytes 589824 | tf_op jit(solution)/shard_map/all_to_all | solution.py:177
  39.8 2.7 %collective-permute-start.1 = (bf16[192,768]{1,0:T(8,128)(2,1)S(1)}, bf16[192,768]{1,0:T(8,128)(2,1)S(1)}, u32[]{:S(2)}, u32[]{:S(2)}) collective-permute-start(bf16[192,768]{1,0:T(8,128)(2,1)S(1)} %bitcast.49), channel_id=1, source_target_pairs={{0,1},{1,0},{2,3},{3,2},{4,5},{5,4},{6,7},{7,6},{8,9},{9,8},{10,11... | collective-permute-start | bytes 884744 | tf_op jit(solution)/shard_map/ppermute | solution.py:160
  43.9 9.5 %collective-permute-start.2 = (bf16[2,192,768]{2,1,0:T(8,128)(2,1)S(1)}, bf16[2,192,768]{2,1,0:T(8,128)(2,1)S(1)}, u32[]{:S(2)}, u32[]{:S(2)}) collective-permute-start(bf16[2,192,768]{2,1,0:T(8,128)(2,1)S(1)} %pad_maximum_fusion.1.r0), channel_id=1, source_target_pairs={{0,8},{1,57},{8,16},{9,1},{16,24},{17,9},{24,32},{25,17},{32,40},{... | collective-permute-start | bytes 1769480 | tf_op jit(solution)/shard_map/ppermute | solution.py:163
  54.2 6.0 %collective-permute-done.2.r1 = bf16[2,192,768]{2,1,0:T(8,128)(2,1)S(1)} collective-permute-done((bf16[2,192,768]{2,1,0:T(8,128)(2,1)S(1)}, bf16[2,192,768]{2,1,0:T(8,128)(2,1)S(1)}, u32[]{:S(2)}, u32[]{:S(2)}) %collective-permute-start.2) | collective-permute-done | bytes 589856 | tf_op jit(solution)/shard_map/ppermute | solution.py:163
  60.2 5.0 %collective-permute-start.3 = (bf16[2,192,768]{2,1,0:T(8,128)(2,1)S(1)}, bf16[2,192,768]{2,1,0:T(8,128)(2,1)}, u32[]{:S(2)}, u32[]{:S(2)}) collective-permute-start(bf16[2,192,768]{2,1,0:T(8,128)(2,1)S(1)} %collective-permute-done.2.r1), channel_id=1, source_target_pairs={{0,8},{1,57},{8,16},{9,1},{16,24},{17,9},{24,32},{25,17},{32,40},{... | collective-permute-start | bytes 1769480 | tf_op jit(solution)/shard_map/ppermute | solution.py:163
  65.2 6.8 %collective-permute-done.3.r2 = bf16[2,192,768]{2,1,0:T(8,128)(2,1)} collective-permute-done((bf16[2,192,768]{2,1,0:T(8,128)(2,1)S(1)}, bf16[2,192,768]{2,1,0:T(8,128)(2,1)}, u32[]{:S(2)}, u32[]{:S(2)}) %collective-permute-start.3) | collective-permute-done | bytes 589856 | tf_op jit(solution)/shard_map/ppermute | solution.py:163
  72.0 5.1 %collective-permute-start.4 = (bf16[2,192,768]{2,1,0:T(8,128)(2,1)}, bf16[2,192,768]{2,1,0:T(8,128)(2,1)S(1)}, u32[]{:S(2)}, u32[]{:S(2)}) collective-permute-start(bf16[2,192,768]{2,1,0:T(8,128)(2,1)} %collective-permute-done.3.r2), channel_id=1, source_target_pairs={{0,8},{1,57},{8,16},{9,1},{16,24},{17,9},{24,32},{25,17},{32,40},{... | collective-permute-start | bytes 1769480 | tf_op jit(solution)/shard_map/ppermute | solution.py:163
  77.2 7.1 %collective-permute-done.4.r3 = bf16[2,192,768]{2,1,0:T(8,128)(2,1)S(1)} collective-permute-done((bf16[2,192,768]{2,1,0:T(8,128)(2,1)}, bf16[2,192,768]{2,1,0:T(8,128)(2,1)S(1)}, u32[]{:S(2)}, u32[]{:S(2)}) %collective-permute-start.4) | collective-permute-done | bytes 589856 | tf_op jit(solution)/shard_map/ppermute | solution.py:163
  84.3 4.9 %collective-permute-start.5 = (bf16[2,96,768]{2,1,0:T(8,128)(2,1)S(1)}, bf16[2,96,768]{2,1,0:T(8,128)(2,1)S(1)}, u32[]{:S(2)}, u32[]{:S(2)}) collective-permute-start(bf16[2,96,768]{2,1,0:T(8,128)(2,1)S(1)} %constant_dynamic-slice_fusion), channel_id=1, source_target_pairs={{0,8},{1,57},{8,16},{9,1},{16,24},{17,9},{24,32},{25,17},{32,40},{... | collective-permute-start | bytes 884744 | tf_op jit(solution)/shard_map/ppermute | solution.py:163
  90.2 2.6 %collective-permute-done.5.r4 = bf16[2,96,768]{2,1,0:T(8,128)(2,1)S(1)} collective-permute-done((bf16[2,96,768]{2,1,0:T(8,128)(2,1)S(1)}, bf16[2,96,768]{2,1,0:T(8,128)(2,1)S(1)}, u32[]{:S(2)}, u32[]{:S(2)}) %collective-permute-start.5) | collective-permute-done | bytes 294944 | tf_op jit(solution)/shard_map/ppermute | solution.py:163
  93.9 7.0 %collective-permute-start.6 = (bf16[672,768]{1,0:T(8,128)(2,1)}, bf16[672,768]{1,0:T(8,128)(2,1)}, u32[]{:S(2)}, u32[]{:S(2)}) collective-permute-start(bf16[672,768]{1,0:T(8,128)(2,1)} %pad_maximum_fusion), channel_id=1, source_target_pairs={{0,1},{1,0},{2,3},{3,2},{4,5},{5,4},{6,7},{7,6},{8,9},{9,8},{10,11... | collective-permute-start | bytes 3096584 | tf_op jit(solution)/shard_map/ppermute | solution.py:160
  104.2 6.0 %shard_map.123 = (bf16[768,512]{1,0:T(8,128)(2,1)S(1)}, f32[768,512]{1,0:T(8,128)S(1)}, f32[8,672]{1,0:T(8,128)S(1)}) custom-call(s32[40]{0:T(128)S(1)} %concatenate.29.table, bf16[2,192,768]{2,1,0:T(8,128)(2,1)S(1)} %copy-done.8, bf16[2,192,768]{2,1,0:T(8,128)(2,1)S(1)} %copy-done.16, bf16[2,192,768]{2,1,0:T(8,128)(2,1)} %collective-permute-done.3.r2, ...), custom_call_target="tpu_custom_call" | custom-call | flops 2415919104 | bytes 9000000 | tf_op jit(solution)/shard_map/pallas_call | solution.py:26
  110.3 3.3 %shard_map.124 = (bf16[768,512]{1,0:T(8,128)(2,1)S(1)}, f32[768,512]{1,0:T(8,128)S(1)}, f32[8,96]{1,0:T(8,128)S(1)}) custom-call(s32[40]{0:T(128)S(1)} %concatenate.29.table, bf16[2,96,768]{2,1,0:T(8,128)(2,1)S(1)} %collective-permute-done.5.r4, bf16[1024,768]{1,0:T(8,128)(2,1)S(1)} %copy-done, ...), custom_call_target="tpu_custom_call", output_to_operand_aliasing={{0}: (5, {}), {1}: (6, {})} | custom-call | flops 301989888 | bytes 6000000 | tf_op jit(solution)/shard_map/pallas_call | solution.py:26
  113.6 4.4 %collective-permute-start.7 = (bf16[768,512]{1,0:T(8,128)(2,1)S(1)}, bf16[768,512]{1,0:T(8,128)(2,1)}, u32[]{:S(2)}, u32[]{:S(2)}) collective-permute-start(bf16[768,512]{1,0:T(8,128)(2,1)S(1)} %get-tuple-element.23), channel_id=1, source_target_pairs={{0,2},{1,7},{2,0},{3,5},{4,6},{5,3},{6,4},{7,1},{8,10},{9,15},{10,... | collective-permute-start | bytes 2359304 | tf_op jit(solution)/shard_map/ppermute | solution.py:169
  118.6 16.0 %all_to_all.15 = f32[64,1,24]{2,1,0:T(1,128)S(1)} all-to-all(f32[64,1,24]{2,1,0:T(1,128)S(1)} %bitcast.52), channel_id=1, replica_groups=mesh['y'=8,'z'=8,'x'=4,'c'=2] {'y','z'}, dimensions={0} | all-to-all | bytes 12288 | tf_op jit(solution)/shard_map/all_to_all | solution.py:235
  134.6 2.2 %collective-permute-start.10 = (f32[8,24]{1,0:T(8,128)S(1)}, f32[8,24]{1,0:T(8,128)S(1)}, u32[]{:S(2)}, u32[]{:S(2)}) collective-permute-start(f32[8,24]{1,0:T(8,128)S(1)} %bitcast_reduce_fusion), channel_id=1, source_target_pairs={{0,1},{1,0},{2,3},{3,2},{4,5},{5,4},{6,7},{7,6},{8,9},{9,8},{10,11... | collective-permute-start | bytes 2312 | tf_op jit(solution)/shard_map/ppermute | solution.py:160
  137.7 3.7 %collective-permute-start.11 = (f32[8,24]{1,0:T(8,128)S(1)}, f32[8,24]{1,0:T(8,128)S(1)}, u32[]{:S(2)}, u32[]{:S(2)}) collective-permute-start(f32[8,24]{1,0:T(8,128)S(1)} %add.74), channel_id=1, source_target_pairs={{0,2},{1,7},{2,0},{3,5},{4,6},{5,3},{6,4},{7,1},{8,10},{9,15},{10,... | collective-permute-start | bytes 2312 | tf_op jit(solution)/shard_map/ppermute | solution.py:169
  141.5 1.7 collective-permute-done.11
  143.2 1.9 %collective-permute-start.12 = (f32[8,24]{1,0:T(8,128)S(1)}, f32[8,24]{1,0:T(8,128)S(1)}, u32[]{:S(2)}, u32[]{:S(2)}) collective-permute-start(f32[8,24]{1,0:T(8,128)S(1)} %add.75), channel_id=1, source_target_pairs={{0,6},{1,3},{2,4},{3,1},{4,2},{5,7},{6,0},{7,5},{8,14},{9,11},{10,... | collective-permute-start | bytes 2312 | tf_op jit(solution)/shard_map/ppermute | solution.py:169
  147.3 6.5 %shard_map.122 = bf16[1024,768]{1,0:T(8,128)(2,1)} custom-call(s32[40]{0:T(128)S(1)} %concatenate.29.table, bf16[2,192,768]{2,1,0:T(8,128)(2,1)S(1)} %copy-done.9, bf16[2,192,768]{2,1,0:T(8,128)(2,1)S(1)} %copy-done.17, bf16[2,192,768]{2,1,0:T(8,128)(2,1)} %collective-permute-done.3.r2, bf16[2,192,768]{2,1,0:T(8,128)(2,1)S(1)} %copy-done.12, ...), custom_call_target="tpu_custom_call" | custom-call | flops 2415919104 | bytes 9000000 | tf_op jit(solution)/shard_map/pallas_call | solution.py:26
  155.2 3.4 %collective-permute-start.8 = (bf16[768,256]{1,0:T(8,128)(2,1)S(1)}, bf16[768,256]{1,0:T(8,128)(2,1)S(1)}, u32[]{:S(2)}, u32[]{:S(2)}) collective-permute-start(bf16[768,256]{1,0:T(8,128)(2,1)S(1)} %slice.84), channel_id=1, source_target_pairs={{0,6},{1,3},{2,4},{3,1},{4,2},{5,7},{6,0},{7,5},{8,14},{9,11},{10,... | collective-permute-start | bytes 1179656 | tf_op jit(solution)/shard_map/ppermute | solution.py:169
  159.3 4.7 %collective-permute-done.8 = bf16[768,256]{1,0:T(8,128)(2,1)S(1)} collective-permute-done((bf16[768,256]{1,0:T(8,128)(2,1)S(1)}, bf16[768,256]{1,0:T(8,128)(2,1)S(1)}, u32[]{:S(2)}, u32[]{:S(2)}) %collective-permute-start.8) | collective-permute-done | bytes 393248 | tf_op jit(solution)/shard_map/ppermute | solution.py:169
  164.2 6.4 %collective-permute-start.9 = (bf16[768,128]{1,0:T(8,128)(2,1)S(1)}, bf16[768,128]{1,0:T(8,128)(2,1)S(1)}, u32[]{:S(2)}, u32[]{:S(2)}) collective-permute-start(bf16[768,128]{1,0:T(8,128)(2,1)S(1)} %select_convert_fusion), channel_id=1, source_target_pairs={{0,1},{1,0},{2,3},{3,2},{4,5},{5,4},{6,7},{7,6},{8,9},{9,8},{10,11... | collective-permute-start | bytes 589832 | tf_op jit(solution)/shard_map/ppermute | solution.py:160
  (94 shorter events, 24.7 us)
Async XLA Ops:
  7.2 93.8 %all-gather.3.cloned.1.call-start = ((), (), s32[]{:S(2)}) async-start(), calls=%async_computation.2 | async-start | bytes 3538944 | tf_op jit(solution)/shard_map/all_gather | solution.py:189
  13.4 26.5 %collective-permute-start = (bf16[1024,768]{1,0:T(8,128)(2,1)}, bf16[1024,768]{1,0:T(8,128)(2,1)S(1)}, u32[]{:S(2)}, u32[]{:S(2)}) collective-permute-start(bf16[1024,768]{1,0:T(8,128)(2,1)} %w_own.3), channel_id=1, source_target_pairs={{0,1},{1,0},{2,3},{3,2},{4,5},{5,4},{6,7},{7,6},{8,9},{9,8},{10,11... | collective-permute-start | bytes 4718600 | tf_op jit(solution)/shard_map/ppermute | solution.py:160
  39.8 50.4 %copy-start.1 = (bf16[1024,768]{1,0:T(8,128)(2,1)}, bf16[1024,768]{1,0:T(8,128)(2,1)S(1)}, u32[]{:S(2)}) copy-start(bf16[1024,768]{1,0:T(8,128)(2,1)S(1)} %collective-permute-done.w_other) | copy-start | bytes 4718596
  39.8 4.0 %collective-permute-start.1 = (bf16[192,768]{1,0:T(8,128)(2,1)S(1)}, bf16[192,768]{1,0:T(8,128)(2,1)S(1)}, u32[]{:S(2)}, u32[]{:S(2)}) collective-permute-start(bf16[192,768]{1,0:T(8,128)(2,1)S(1)} %bitcast.49), channel_id=1, source_target_pairs={{0,1},{1,0},{2,3},{3,2},{4,5},{5,4},{6,7},{7,6},{8,9},{9,8},{10,11... | collective-permute-start | bytes 884744 | tf_op jit(solution)/shard_map/ppermute | solution.py:160
  43.9 16.3 %collective-permute-start.2 = (bf16[2,192,768]{2,1,0:T(8,128)(2,1)S(1)}, bf16[2,192,768]{2,1,0:T(8,128)(2,1)S(1)}, u32[]{:S(2)}, u32[]{:S(2)}) collective-permute-start(bf16[2,192,768]{2,1,0:T(8,128)(2,1)S(1)} %pad_maximum_fusion.1.r0), channel_id=1, source_target_pairs={{0,8},{1,57},{8,16},{9,1},{16,24},{17,9},{24,32},{25,17},{32,40},{... | collective-permute-start | bytes 1769480 | tf_op jit(solution)/shard_map/ppermute | solution.py:163
  60.2 33.7 %copy-start.15 = (bf16[2,192,768]{2,1,0:T(8,128)(2,1)}, bf16[2,192,768]{2,1,0:T(8,128)(2,1)S(1)}, u32[]{:S(2)}) copy-start(bf16[2,192,768]{2,1,0:T(8,128)(2,1)S(1)} %collective-permute-done.2.r1) | copy-start | bytes 1769476
  60.2 11.8 %collective-permute-start.3 = (bf16[2,192,768]{2,1,0:T(8,128)(2,1)S(1)}, bf16[2,192,768]{2,1,0:T(8,128)(2,1)}, u32[]{:S(2)}, u32[]{:S(2)}) collective-permute-start(bf16[2,192,768]{2,1,0:T(8,128)(2,1)S(1)} %collective-permute-done.2.r1), channel_id=1, source_target_pairs={{0,8},{1,57},{8,16},{9,1},{16,24},{17,9},{24,32},{25,17},{32,40},{... | collective-permute-start | bytes 1769480 | tf_op jit(solution)/shard_map/ppermute | solution.py:163
  72.0 12.2 %collective-permute-start.4 = (bf16[2,192,768]{2,1,0:T(8,128)(2,1)}, bf16[2,192,768]{2,1,0:T(8,128)(2,1)S(1)}, u32[]{:S(2)}, u32[]{:S(2)}) collective-permute-start(bf16[2,192,768]{2,1,0:T(8,128)(2,1)} %collective-permute-done.3.r2), channel_id=1, source_target_pairs={{0,8},{1,57},{8,16},{9,1},{16,24},{17,9},{24,32},{25,17},{32,40},{... | collective-permute-start | bytes 1769480 | tf_op jit(solution)/shard_map/ppermute | solution.py:163
  84.3 9.7 %copy-start.10 = (bf16[2,192,768]{2,1,0:T(8,128)(2,1)}, bf16[2,192,768]{2,1,0:T(8,128)(2,1)S(1)}, u32[]{:S(2)}) copy-start(bf16[2,192,768]{2,1,0:T(8,128)(2,1)S(1)} %collective-permute-done.4.r3) | copy-start | bytes 1769476
  84.3 8.6 %collective-permute-start.5 = (bf16[2,96,768]{2,1,0:T(8,128)(2,1)S(1)}, bf16[2,96,768]{2,1,0:T(8,128)(2,1)S(1)}, u32[]{:S(2)}, u32[]{:S(2)}) collective-permute-start(bf16[2,96,768]{2,1,0:T(8,128)(2,1)S(1)} %constant_dynamic-slice_fusion), channel_id=1, source_target_pairs={{0,8},{1,57},{8,16},{9,1},{16,24},{17,9},{24,32},{25,17},{32,40},{... | collective-permute-start | bytes 884744 | tf_op jit(solution)/shard_map/ppermute | solution.py:163
  93.9 51.2 %collective-permute-start.6 = (bf16[672,768]{1,0:T(8,128)(2,1)}, bf16[672,768]{1,0:T(8,128)(2,1)}, u32[]{:S(2)}, u32[]{:S(2)}) collective-permute-start(bf16[672,768]{1,0:T(8,128)(2,1)} %pad_maximum_fusion), channel_id=1, source_target_pairs={{0,1},{1,0},{2,3},{3,2},{4,5},{5,4},{6,7},{7,6},{8,9},{9,8},{10,11... | collective-permute-start | bytes 3096584 | tf_op jit(solution)/shard_map/ppermute | solution.py:160
  104.2 6.0 %copy-start = (bf16[1024,768]{1,0:T(8,128)(2,1)S(1)}, bf16[1024,768]{1,0:T(8,128)(2,1)}, u32[]{:S(2)}) copy-start(bf16[1024,768]{1,0:T(8,128)(2,1)} %w_own.3) | copy-start | bytes 4718596
  104.2 6.0 %copy-start.2 = (bf16[1024,768]{1,0:T(8,128)(2,1)S(1)}, bf16[1024,768]{1,0:T(8,128)(2,1)}, u32[]{:S(2)}) copy-start(bf16[1024,768]{1,0:T(8,128)(2,1)} %copy-done.1) | copy-start | bytes 4718596
  110.2 26.6 %copy-start.20 = (s32[64,2]{0,1:T(2,128)S(1)}, s32[64,2]{0,1:T(2,128)}, u32[]{:S(2)}) copy-start(s32[64,2]{0,1:T(2,128)} %param.10) | copy-start | bytes 1540
  110.3 34.9 %copy-start.9 = (bf16[2,192,768]{2,1,0:T(8,128)(2,1)S(1)}, bf16[2,192,768]{2,1,0:T(8,128)(2,1)}, u32[]{:S(2)}) copy-start(bf16[2,192,768]{2,1,0:T(8,128)(2,1)} %copy-done.7) | copy-start | bytes 1769476
  113.6 40.1 %collective-permute-start.7 = (bf16[768,512]{1,0:T(8,128)(2,1)S(1)}, bf16[768,512]{1,0:T(8,128)(2,1)}, u32[]{:S(2)}, u32[]{:S(2)}) collective-permute-start(bf16[768,512]{1,0:T(8,128)(2,1)S(1)} %get-tuple-element.23), channel_id=1, source_target_pairs={{0,2},{1,7},{2,0},{3,5},{4,6},{5,3},{6,4},{7,1},{8,10},{9,15},{10,... | collective-permute-start | bytes 2359304 | tf_op jit(solution)/shard_map/ppermute | solution.py:169
  134.6 3.1 %collective-permute-start.10 = (f32[8,24]{1,0:T(8,128)S(1)}, f32[8,24]{1,0:T(8,128)S(1)}, u32[]{:S(2)}, u32[]{:S(2)}) collective-permute-start(f32[8,24]{1,0:T(8,128)S(1)} %bitcast_reduce_fusion), channel_id=1, source_target_pairs={{0,1},{1,0},{2,3},{3,2},{4,5},{5,4},{6,7},{7,6},{8,9},{9,8},{10,11... | collective-permute-start | bytes 2312 | tf_op jit(solution)/shard_map/ppermute | solution.py:160
  137.7 5.6 %collective-permute-start.11 = (f32[8,24]{1,0:T(8,128)S(1)}, f32[8,24]{1,0:T(8,128)S(1)}, u32[]{:S(2)}, u32[]{:S(2)}) collective-permute-start(f32[8,24]{1,0:T(8,128)S(1)} %add.74), channel_id=1, source_target_pairs={{0,2},{1,7},{2,0},{3,5},{4,6},{5,3},{6,4},{7,1},{8,10},{9,15},{10,... | collective-permute-start | bytes 2312 | tf_op jit(solution)/shard_map/ppermute | solution.py:169
  143.2 10.5 %collective-permute-start.12 = (f32[8,24]{1,0:T(8,128)S(1)}, f32[8,24]{1,0:T(8,128)S(1)}, u32[]{:S(2)}, u32[]{:S(2)}) collective-permute-start(f32[8,24]{1,0:T(8,128)S(1)} %add.75), channel_id=1, source_target_pairs={{0,6},{1,3},{2,4},{3,1},{4,2},{5,7},{6,0},{7,5},{8,14},{9,11},{10,... | collective-permute-start | bytes 2312 | tf_op jit(solution)/shard_map/ppermute | solution.py:169
  153.8 5.0 %copy-start.21 = (bf16[64,2]{0,1:T(2,128)(2,1)S(1)}, bf16[64,2]{0,1:T(2,128)(2,1)}, u32[]{:S(2)}) copy-start(bf16[64,2]{0,1:T(2,128)(2,1)} %param.11) | copy-start | bytes 772
  155.2 8.8 %collective-permute-start.8 = (bf16[768,256]{1,0:T(8,128)(2,1)S(1)}, bf16[768,256]{1,0:T(8,128)(2,1)S(1)}, u32[]{:S(2)}, u32[]{:S(2)}) collective-permute-start(bf16[768,256]{1,0:T(8,128)(2,1)S(1)} %slice.84), channel_id=1, source_target_pairs={{0,6},{1,3},{2,4},{3,1},{4,2},{5,7},{6,0},{7,5},{8,14},{9,11},{10,... | collective-permute-start | bytes 1179656 | tf_op jit(solution)/shard_map/ppermute | solution.py:169
  159.3 12.3 %copy-start.4 = (f32[1536,128]{1,0:T(8,128)S(1)}, f32[1536,128]{1,0:T(8,128)}, u32[]{:S(2)}) copy-start(f32[1536,128]{1,0:T(8,128)} %copy-done.3) | copy-start | bytes 2359300
  159.3 12.3 %copy-start.6 = (f32[1536,128]{1,0:T(8,128)S(1)}, f32[1536,128]{1,0:T(8,128)}, u32[]{:S(2)}) copy-start(f32[1536,128]{1,0:T(8,128)} %copy-done.5) | copy-start | bytes 2359300
  164.2 7.4 %collective-permute-start.9 = (bf16[768,128]{1,0:T(8,128)(2,1)S(1)}, bf16[768,128]{1,0:T(8,128)(2,1)S(1)}, u32[]{:S(2)}, u32[]{:S(2)}) collective-permute-start(bf16[768,128]{1,0:T(8,128)(2,1)S(1)} %select_convert_fusion), channel_id=1, source_target_pairs={{0,1},{1,0},{2,3},{3,2},{4,5},{5,4},{6,7},{7,6},{8,9},{9,8},{10,11... | collective-permute-start | bytes 589832 | tf_op jit(solution)/shard_map/ppermute | solution.py:160
  (12 other events, 11.5 us)
Sparse Core Ops, SparseCore 0:
  13.5 38.9 all-gather.2

commit v4 on v3

v4 whole, which is shorter than its diff:
```python
import jax
import jax.numpy as jnp
from jax import lax
from jax.experimental import pallas as pl
from jax.experimental.pallas import tpu as pltpu
from jax.sharding import Mesh
from jax.sharding import PartitionSpec as P

EXPERTS = 8
CAP = 24
NZ = 8
NX = 4
BLOCK = EXPERTS * CAP
HALF = BLOCK // 2
NEAR = 5 * HALF
FAR = 3 * HALF
MINE = 768
BF = jnp.bfloat16
F32 = jnp.float32
VM = pl.BlockSpec()
SM = pl.BlockSpec(memory_space=pltpu.SMEM)


def call(body, outs, ins, cost, scratch=(), limit=40):
    specs = [SM if a.dtype == jnp.int32 and a.shape == (3,) else VM for a in ins]
    return pl.pallas_call(
        body,
        out_shape=[jax.ShapeDtypeStruct(s, d) for s, d in outs],
        in_specs=specs,
        out_specs=[VM] * len(outs),
        scratch_shapes=[pltpu.VMEM(s, BF) for s in scratch],
        compiler_params=pltpu.CompilerParams(vmem_limit_bytes=limit * 2**20),
        cost_estimate=pl.CostEstimate(flops=cost[0], bytes_accessed=cost[1], transcendentals=0),
    )(*ins)


def dot(a, b, da, db):
    return lax.dot_general(a, b, (((da,), (db,)), ((), ())), preferred_element_type=F32)


def pack_body(routes, gates_ref, rows, out):
    gates = gates_ref[...].astype(F32)
    tokens = rows.shape[0]
    expert = lax.broadcasted_iota(jnp.int32, (EXPERTS, tokens), 0)
    first, second = routes[0:1, :] == expert, routes[1:2, :] == expert
    weight = jnp.where(first, gates[0:1, :], 0.0) + jnp.where(second, gates[1:2, :], 0.0)
    member = jnp.where(first | second, 1.0, 0.0)
    at = lax.broadcasted_iota(jnp.int32, (tokens, tokens), 0)
    to = lax.broadcasted_iota(jnp.int32, (tokens, tokens), 1)
    earlier = jnp.where(at < to, 1.0, 0.0).astype(BF)
    rank = dot(member.astype(BF), earlier, 1, 0)
    rank = jnp.where(member > 0.0, rank, -1.0).astype(jnp.int32)
    place = lax.broadcasted_iota(jnp.int32, (CAP, tokens), 0)
    chosen = [
        jnp.where(rank[e : e + 1] == place, weight[e : e + 1], 0.0) for e in range(EXPERTS)
    ]
    out[...] = dot(jnp.concatenate(chosen, axis=0).astype(BF), rows[...], 1, 0).astype(BF)


STEPS = (0, 1, 1, 2, 2, 3, 3, 4)
FLIPS = (0, 0, 1, 0, 1, 0, 1, 0)


def group(place, g):
    core = place[2] if g < 8 else 1 - place[2]
    step = STEPS[g % 8]
    return (place[0] + NZ + (2 * core - 1) * step) % NZ, core ^ FLIPS[g % 8]


def unit_of(place, label):
    first = 1 + 2 * place[2]
    masks = (0, 4 - first, first, 2)
    return place[1] ^ masks[label]


def act_body(table, gate, up, hidden):
    core = table[2]
    for g in range(16):
        zs, half = group(table, g)
        a = gate[pl.ds(half * 4, 4), zs].astype(F32).reshape(HALF, 128)
        b = up[pl.ds(half * 4, 4), zs].astype(F32).reshape(HALF, 128)
        sig = 1.0 / (1.0 + jnp.exp(-a))
        hidden[core if g < 8 else 1 - core, pl.ds((g % 8) * HALF, HALF), :] = (a * sig * b).astype(BF)


def product_body(count, start, table, *refs):
    pieces, (w_own, w_other, hidden, send, keep, dots, own, other) = refs[:count], refs[count:]
    core = table[2]
    size = count * HALF
    for piece, ref in enumerate(pieces):
        own[pl.ds(piece * HALF, HALF), :] = ref[0]
        other[pl.ds(piece * HALF, HALF), :] = ref[1]
    total = None
    for label in (2, 3, 0, 1):
        unit = unit_of(table, label)
        w = pl.ds(pl.multiple_of(unit * 256, 256), 256)
        part = dot(own[...], w_own[w, :], 1, 1) + dot(other[...], w_other[w, :], 1, 1)
        if label >= 2:
            send[:, pl.ds((label - 2) * 256, 256)] = part.astype(BF)
        else:
            keep[:, pl.ds(label * 256, 256)] = part
        for i in range(2):
            h = hidden[2 * unit + i, core, pl.ds(start, size), :]
            term = part[:, i * 128 : i * 128 + 128] * h.astype(F32)
            total = term if total is None else total + term
    dots[...] = lax.dot_general(
        jnp.ones((8, 128), F32), total, (((1,), (1,)), ((), ())),
        precision=lax.Precision.HIGHEST, preferred_element_type=F32,
    )


def weight_body(table, *refs):
    pieces, (spare, lent, hidden, out, rows, units) = refs[:8], refs[8:]
    core = table[2]
    for piece, ref in enumerate(pieces):
        rows[pl.ds(piece * HALF, HALF), :] = ref[0]
    rows[pl.ds(MINE, HALF), :] = spare[0]
    rows[pl.ds(MINE + HALF, MINE - HALF), :] = lent[...]
    for pair in range(4):
        for i in range(2):
            lanes = pl.ds(i * 128, 128)
            units[pl.ds(0, MINE), lanes] = hidden[2 * pair + i, core]
            units[pl.ds(MINE, MINE), lanes] = hidden[2 * pair + i, 1 - core]
        out[pl.ds(pair * 256, 256), :] = dot(units[...], rows[...], 0, 0).astype(BF)


def grad_body(table, kept, got, gate, up, gate_out, up_out):
    for g in range(16):
        zs, half = group(table, g)
        planes = pl.ds(half * 4, 4)
        src = (kept if g < 8 else got)[pl.ds((g % 8) * HALF, HALF), :].astype(F32).reshape(4, CAP, 128)
        a, b = gate[planes, zs].astype(F32), up[planes, zs].astype(F32)
        sig = 1.0 / (1.0 + jnp.exp(-a))
        gate_out[planes, zs] = (src * b * sig * (1.0 + a * (1.0 - sig))).astype(BF)
        up_out[planes, zs] = (src * (a * sig)).astype(BF)


def per_device(grad_out, routes, gates, w_down, gate_pre, up_pre):
    zi, xi, ci = lax.axis_index("z"), lax.axis_index("x"), lax.axis_index("c")
    tokens, width = grad_out.shape
    ff = w_down.shape[0]

    table = jnp.stack([zi, xi, ci]).astype(jnp.int32)

    def after(x, *others):
        return lax.optimization_barrier((x, *others))[0]

    def swap_core(x):
        return lax.ppermute(x, "c", [(0, 1), (1, 0)])

    def ring(x):
        return lax.ppermute(
            x, ("z", "c"), [(z * 2 + c, (z + 1 - 2 * c) % NZ * 2 + c) for z in range(NZ) for c in range(2)]
        )

    def swap_x(x, first):
        masks = (1, 3) if first else (3, 1)
        return lax.ppermute(
            x, ("x", "c"), [(i * 2 + c, (i ^ masks[c]) * 2 + c) for i in range(NX) for c in range(2)]
        )

    routes_t, gates_t = routes.T, gates.T
    (packed,) = call(
        pack_body, [((BLOCK, width), BF)], (routes_t, gates_t, grad_out), (2 * BLOCK * tokens * width, 400000)
    )
    own = lax.all_to_all(
        packed.reshape(EXPERTS, CAP, width), "y", split_axis=0, concat_axis=0, tiled=True
    ).reshape(BLOCK, width)
    view = (EXPERTS, NZ, CAP, 128)
    gate_view, up_view = gate_pre.reshape(view), up_pre.reshape(view)
    (mine,) = call(
        act_body, [((2, MINE, 128), BF)], (table, gate_view, up_view), (20 * 2 * MINE * 128, 2000000)
    )
    hidden = lax.all_gather(mine, ("x", "c"), axis=0)

    sides = jnp.stack([own, swap_core(own)])
    ra = [lax.dynamic_slice_in_dim(sides, ci * HALF, HALF, 1)]
    rb = [lax.dynamic_slice_in_dim(sides, (1 - ci) * HALF, HALF, 1)]
    for step in range(3):
        ra.append(ring(ra[-1]))
        rb.append(ring(rb[-1]))
    w_other = swap_core(after(w_down, ra[1]))

    def product(pieces, start):
        size = len(pieces) * HALF
        return call(
            lambda *refs: product_body(len(pieces), start, *refs),
            [((size, 512), BF), ((size, 512), F32), ((8, size), F32)],
            (table, *pieces, w_down, w_other, hidden),
            (2 * size * ff * 2 * width, 9000000),
            ((size, width),) * 2,
        )

    send, keep, dots_near = product((ra[0], ra[1], rb[1], ra[2], rb[2]), 0)
    ra.append(ring(after(ra[3], send)))
    part = keep + swap_x(send, True).astype(F32)
    near = part[:, :256] + swap_x(part[:, 256:].astype(BF), False).astype(F32)
    send, keep, dots_far = product((ra[3], rb[3], after(ra[4], near)), NEAR)
    part = keep + swap_x(send, True).astype(F32)
    last = part[:, 256:].astype(BF)
    far = part[:, :256] + swap_x(last, False).astype(F32)
    pieces = (ra[0], ra[1], rb[1], ra[2], rb[2], ra[3], rb[3], ra[4])
    whole = jnp.concatenate([near, far], axis=0)
    low, high = whole[:, :128], whole[:, 128:]
    kept = jnp.where(ci == 0, low, high)
    got = swap_core(jnp.where(ci == 0, high, low).astype(BF))
    gate_pre_grad, up_pre_grad = call(
        grad_body, [(view, BF), (view, BF)], (table, kept, got, gate_view, up_view), (4 * MINE * 128, 3000000)
    )

    dots = jnp.concatenate([dots_near[0], dots_far[0]]).reshape(8, 4, CAP)
    zero = jnp.zeros((1, 4, CAP), F32)
    sides_of = dots[1:7].reshape(3, 2, 4, CAP)
    none = jnp.zeros((3, EXPERTS, CAP), F32)
    at0, at4 = dots[0:1], dots[7:8]

    def spread(c):
        ends = [jnp.concatenate([a, zero] if c == 0 else [zero, a], axis=1) for a in (at0, at4)]
        flat = (sides_of if c == 0 else sides_of[:, ::-1]).reshape(3, EXPERTS, CAP)
        sides = (none, flat[::-1]) if c == 0 else (flat, none)
        return jnp.concatenate([ends[0], sides[0], ends[1], sides[1]], axis=0)

    by_source = jnp.roll(jnp.where(ci == 0, spread(0), spread(1)), zi, axis=0).transpose(1, 0, 2)
    back = lax.all_to_all(
        by_source.reshape(EXPERTS * NZ, CAP), ("y", "z"), split_axis=0, concat_axis=0, tiled=True
    )
    totals = jnp.sum(back.reshape(EXPERTS, NZ, CAP), axis=1)
    totals = totals + swap_core(totals)
    totals = totals + swap_x(totals, True)
    totals = totals + swap_x(totals, False)

    named = routes_t[:, None, :] == jnp.arange(EXPERTS, dtype=jnp.int32)[None, :, None]
    member = jnp.any(named, axis=0)
    order = jnp.arange(tokens, dtype=jnp.int32)
    earlier = (order[:, None] < order[None, :]).astype(BF)
    rank = jnp.dot(member.astype(BF), earlier, preferred_element_type=F32).astype(jnp.int32)
    chosen = member[:, None, :] & (rank[:, None, :] == jnp.arange(CAP, dtype=jnp.int32)[None, :, None])
    by_token = jnp.sum(jnp.where(chosen, totals[:, :, None], 0.0), axis=1)
    gate_grad = jnp.sum(jnp.where(named, by_token[None], 0.0), axis=1) / gates_t.astype(F32)

    lent = swap_core(jnp.concatenate([piece[1] for piece in pieces[1:]], axis=0))
    (w_down_grad,) = call(
        weight_body,
        [((ff, width), BF)],
        (table, *pieces, rb[0], after(lent, last), hidden),
        (2 * 2 * MINE * ff * width, 9000000),
        ((2 * MINE, width), (2 * MINE, 256)),
    )
    flat = (EXPERTS * NZ * CAP, 128)
    return (w_down_grad, gate_pre_grad.reshape(flat), up_pre_grad.reshape(flat), gate_grad.T)


def solution(mesh):
    fine = Mesh(mesh.devices.reshape(EXPERTS, NZ, NX, 2), ("y", "z", "x", "c"))
    e, t = ("y", "z"), ("x", "c")
    return jax.shard_map(
        per_device,
        mesh=fine,
        in_specs=(P(e, t), P(e, None), P(e, None), P(e, t), P(None, e + t), P(None, e + t)),
        out_specs=(P(e, t), P(None, e + t), P(None, e + t), P(e, None)),
        check_vma=False,
    )
```

time: 181 us -> 185 us (1.022)
  local copies, waits for them, and re-layouts: 13.2 us -> 29.3 us
  starting transfers between devices: 65.1 us -> 80.2 us
  blocking collectives: 31.1 us -> 17.8 us
  waiting for transfers between devices: 32 us -> 21.5 us
  Pallas kernels: 19.2 us -> 14.8 us
    all_to_all x1 -> x0, blocking collectives: 16 us -> none  [per_device(): lax.all_to_all(by_source.reshape(EXPERTS * NZ, CAP), ('y', 'z'), split_ax...]
    ppermute x4 -> x7, waiting for transfers between devices: 22.5 us -> 7.9 us  [ring(): lax.ppermute(x, ('z', 'c'), [(z * 2 + c, (z + 1 - 2 * c) % NZ * 2 + c) fo...]
    unnamed x44 -> x76, local copies, waits for them, and re-layouts: 11.5 us -> 25.7 us
    all_to_all x0 -> x1, waiting for transfers between devices: none -> 9.26 us  [per_device(): lax.all_to_all(by_source.reshape(EXPERTS * NZ, CAP), ('y', 'z'), split_ax...]
    ppermute x4 -> x7, starting transfers between devices: 24.5 us -> 31 us  [ring(): lax.ppermute(x, ('z', 'c'), [(z * 2 + c, (z + 1 - 2 * c) % NZ * 2 + c) fo...]
    ppermute x4 -> x6, starting transfers between devices: 13.4 us -> 18.3 us  [swap_x(): lax.ppermute(x, ('x', 'c'), [(i * 2 + c, (i ^ masks[c]) * 2 + c) for i in...]
    all_to_all x0 -> x1, starting transfers between devices: none -> 4.61 us  [per_device(): lax.all_to_all(by_source.reshape(EXPERTS * NZ, CAP), ('y', 'z'), split_ax...]
    pallas_call x6, Pallas kernels: 19.2 us -> 14.8 us  [call(): pl.pallas_call(body, out_shape=[jax.ShapeDtypeStruct(s, d) for s, d in ou...]
  transfers between devices with their start and end apart: 14 -> 20, of which waited for: 9 -> 8; matrix products, arithmetic and copies ran while one was open for 2% -> 8% of each run, Pallas kernels for 9% -> 3%
where the time goes in v4:
time: 185 us; the launch traced here: 184 us
  starting transfers between devices  80.2 us (43%)
  local copies, waits for them, and re-layouts  29.3 us (16%)
  waiting for transfers between devices  21.5 us (12%)
  blocking collectives  17.8 us (10%)
  Pallas kernels  14.8 us (8%)
  between operations  14.6 us (8%)
  other arithmetic  5.77 us (3%)
    ppermute x7, starting transfers between devices, ring(): lax.ppermute(x, ('z', 'c'), [(z * 2 + c, (z + 1 - 2 * c) % NZ * 2 + c) fo...  31 us
    ppermute x5, starting transfers between devices, swap_core(): return lax.ppermute(x, 'c', [(0, 1), (1, 0)])  26.3 us
    unnamed x76, local copies, waits for them, and re-layouts  25.7 us
    ppermute x6, starting transfers between devices, swap_x(): lax.ppermute(x, ('x', 'c'), [(i * 2 + c, (i ^ masks[c]) * 2 + c) for i in...  18.3 us
    all_to_all x1, blocking collectives, per_device(): lax.all_to_all(packed.reshape(EXPERTS, CAP, width), 'y', split_axis=0, co...  17.8 us
    pallas_call x6, Pallas kernels, call(): pl.pallas_call(body, out_shape=[jax.ShapeDtypeStruct(s, d) for s, d in ou...  14.8 us
    all_to_all x1, waiting for transfers between devices, per_device(): lax.all_to_all(by_source.reshape(EXPERTS * NZ, CAP), ('y', 'z'), split_ax...  9.26 us
    ppermute x7, waiting for transfers between devices, ring(): lax.ppermute(x, ('z', 'c'), [(z * 2 + c, (z + 1 - 2 * c) % NZ * 2 + c) fo...  7.9 us
  transfers between devices with their start and end apart: 20, of which 8 were waited for; matrix products, arithmetic and copies ran while one was open for 8% of the time, Pallas kernels for 3%

profile of v4, /device:TPU:1, one launch (start us, length us, event | category | flops | bytes accessed | tf_op | source)
XLA Modules:
  0.0 184.0 jit_solution(15618080434821008755)
XLA Ops:
  11.3 17.8 %all_to_all.14 = bf16[8,24,768]{2,1,0:T(8,128)(2,1)S(1)} all-to-all(bf16[8,24,768]{2,1,0:T(8,128)(2,1)S(1)} %bitcast.62), channel_id=1, replica_groups=mesh['y'=8,'z'=8,'x'=4,'c'=2] {'y'}, dimensions={0} | all-to-all | bytes 589824 | tf_op jit(solution)/shard_map/all_to_all | solution.py:166
  29.0 5.2 %collective-permute-start = (bf16[192,768]{1,0:T(8,128)(2,1)S(1)}, bf16[192,768]{1,0:T(8,128)(2,1)S(1)}, u32[]{:S(2)}, u32[]{:S(2)}) collective-permute-start(bf16[192,768]{1,0:T(8,128)(2,1)S(1)} %bitcast.67), channel_id=1, source_target_pairs={{0,1},{1,0},{2,3},{3,2},{4,5},{5,4},{6,7},{7,6},{8,9},{9,8},{10,11... | collective-permute-start | bytes 884744 | tf_op jit(solution)/shard_map/ppermute | solution.py:149
  35.5 10.7 %collective-permute-start.1 = (bf16[2,96,768]{2,1,0:T(8,128)(2,1)S(1)}, bf16[2,96,768]{2,1,0:T(8,128)(2,1)S(1)}, u32[]{:S(2)}, u32[]{:S(2)}) collective-permute-start(bf16[2,96,768]{2,1,0:T(8,128)(2,1)S(1)} %get-tuple-element.29.refs_1_.refs_0_), channel_id=1, source_target_pairs={{0,8},{1,57},{8,16},{9,1},{16,24},{17,9},{24,32},{25,17},{32,40},{... | collective-permute-start | bytes 884744 | tf_op jit(solution)/shard_map/ppermute | solution.py:152
  46.2 3.6 %collective-permute-done.1.refs_2_.refs_1_ = bf16[2,96,768]{2,1,0:T(8,128)(2,1)S(1)} collective-permute-done((bf16[2,96,768]{2,1,0:T(8,128)(2,1)S(1)}, bf16[2,96,768]{2,1,0:T(8,128)(2,1)S(1)}, u32[]{:S(2)}, u32[]{:S(2)}) %collective-permute-start.1) | collective-permute-done | bytes 294944 | tf_op jit(solution)/shard_map/ppermute | solution.py:152
  49.8 3.6 %collective-permute-start.7 = (bf16[1024,768]{1,0:T(8,128)(2,1)S(1)}, bf16[1024,768]{1,0:T(8,128)(2,1)S(1)}, u32[]{:S(2)}, u32[]{:S(2)}) collective-permute-start(bf16[1024,768]{1,0:T(8,128)(2,1)S(1)} %copy-done.2), channel_id=1, source_target_pairs={{0,1},{1,0},{2,3},{3,2},{4,5},{5,4},{6,7},{7,6},{8,9},{9,8},{10,11... | collective-permute-start | bytes 4718600 | tf_op jit(solution)/shard_map/ppermute | solution.py:149
  53.4 3.6 %collective-permute-start.2 = (bf16[2,96,768]{2,1,0:T(8,128)(2,1)S(1)}, bf16[2,96,768]{2,1,0:T(8,128)(2,1)S(1)}, u32[]{:S(2)}, u32[]{:S(2)}) collective-permute-start(bf16[2,96,768]{2,1,0:T(8,128)(2,1)S(1)} %get-tuple-element.28.refs_8_), channel_id=1, source_target_pairs={{0,8},{1,57},{8,16},{9,1},{16,24},{17,9},{24,32},{25,17},{32,40},{... | collective-permute-start | bytes 884744 | tf_op jit(solution)/shard_map/ppermute | solution.py:152
  57.8 2.2 %collective-permute-start.3 = (bf16[2,96,768]{2,1,0:T(8,128)(2,1)S(1)}, bf16[2,96,768]{2,1,0:T(8,128)(2,1)S(1)}, u32[]{:S(2)}, u32[]{:S(2)}) collective-permute-start(bf16[2,96,768]{2,1,0:T(8,128)(2,1)S(1)} %collective-permute-done.1.refs_2_.refs_1_), channel_id=1, source_target_pairs={{0,8},{1,57},{8,16},{9,1},{16,24},{17,9},{24,32},{25,17},{32,40},{... | collective-permute-start | bytes 884744 | tf_op jit(solution)/shard_map/ppermute | solution.py:152
  61.2 4.5 %collective-permute-start.4 = (bf16[2,96,768]{2,1,0:T(8,128)(2,1)S(1)}, bf16[2,96,768]{2,1,0:T(8,128)(2,1)S(1)}, u32[]{:S(2)}, u32[]{:S(2)}) collective-permute-start(bf16[2,96,768]{2,1,0:T(8,128)(2,1)S(1)} %collective-permute-done.2.refs_3_.refs_2_), channel_id=1, source_target_pairs={{0,8},{1,57},{8,16},{9,1},{16,24},{17,9},{24,32},{25,17},{32,40},{... | collective-permute-start | bytes 884744 | tf_op jit(solution)/shard_map/ppermute | solution.py:152
  67.2 2.2 %collective-permute-done.4.refs_5_.refs_4_ = bf16[2,96,768]{2,1,0:T(8,128)(2,1)S(1)} collective-permute-done((bf16[2,96,768]{2,1,0:T(8,128)(2,1)S(1)}, bf16[2,96,768]{2,1,0:T(8,128)(2,1)S(1)}, u32[]{:S(2)}, u32[]{:S(2)}) %collective-permute-start.4) | collective-permute-done | bytes 294944 | tf_op jit(solution)/shard_map/ppermute | solution.py:152
  70.1 2.5 %copy-done = bf16[16,768,128]{2,1,0:T(8,128)(2,1)S(1)} copy-done((bf16[16,768,128]{2,1,0:T(8,128)(2,1)S(1)}, bf16[16,768,128]{2,1,0:T(8,128)(2,1)}, u32[]{:S(2)}) %copy-start) | copy-done | bytes 3145752
  76.4 3.1 %shard_map.95 = (bf16[480,512]{1,0:T(8,128)(2,1)}, f32[480,512]{1,0:T(8,128)S(1)}, f32[8,480]{1,0:T(8,128)S(1)}) custom-call(s32[3]{0:T(128)S(1)} %pad_add_fusion.table.refs_0_, bf16[2,96,768]{2,1,0:T(8,128)(2,1)S(1)} %get-tuple-element.29.refs_1_.refs_0_, bf16[2,96,768]{2,1,0:T(8,128)(2,1)S(1)} %copy-done.12, bf16[2,96,768]{2,1,0:T(8,128)(2,1)S(1)} %copy-done.15, ...), custom_call_target="tpu_custom_call" | custom-call | flops 1509949440 | bytes 9000000 | tf_op jit(solution)/shard_map/pallas_call | solution.py:26
  80.5 4.4 %collective-permute-start.10 = (bf16[480,512]{1,0:T(8,128)(2,1)}, bf16[480,512]{1,0:T(8,128)(2,1)S(1)}, u32[]{:S(2)}, u32[]{:S(2)}) collective-permute-start(bf16[480,512]{1,0:T(8,128)(2,1)} %get-tuple-element.17), channel_id=1, source_target_pairs={{0,2},{1,7},{2,0},{3,5},{4,6},{5,3},{6,4},{7,1},{8,10},{9,15},{10,... | collective-permute-start | bytes 1474568 | tf_op jit(solution)/shard_map/ppermute | solution.py:158
  87.0 5.0 %collective-permute-start.5 = (bf16[2,96,768]{2,1,0:T(8,128)(2,1)}, bf16[2,96,768]{2,1,0:T(8,128)(2,1)}, u32[]{:S(2)}, u32[]{:S(2)}) collective-permute-start(bf16[2,96,768]{2,1,0:T(8,128)(2,1)} %copy-done.17), channel_id=1, source_target_pairs={{0,8},{1,57},{8,16},{9,1},{16,24},{17,9},{24,32},{25,17},{32,40},{... | collective-permute-start | bytes 884744 | tf_op jit(solution)/shard_map/ppermute | solution.py:152
  100.1 3.0 %collective-permute-start.8 = (bf16[2,96,768]{2,1,0:T(8,128)(2,1)}, bf16[2,96,768]{2,1,0:T(8,128)(2,1)}, u32[]{:S(2)}, u32[]{:S(2)}) collective-permute-start(bf16[2,96,768]{2,1,0:T(8,128)(2,1)} %collective-permute-done.5.refs_1_.refs_5_), channel_id=1, source_target_pairs={{0,8},{1,57},{8,16},{9,1},{16,24},{17,9},{24,32},{25,17},{32,40},{... | collective-permute-start | bytes 884744 | tf_op jit(solution)/shard_map/ppermute | solution.py:152
  110.7 2.6 %shard_map.96 = (bf16[288,512]{1,0:T(8,128)(2,1)S(1)}, f32[288,512]{1,0:T(8,128)S(1)}, f32[8,288]{1,0:T(8,128)S(1)}) custom-call(s32[3]{0:T(128)S(1)} %pad_add_fusion.table.refs_0_, bf16[2,96,768]{2,1,0:T(8,128)(2,1)} %collective-permute-done.5.refs_1_.refs_5_, bf16[2,96,768]{2,1,0:T(8,128)(2,1)} %collective-permute-done.6.refs_2_.refs_6_, ...), custom_call_target="tpu_custom_call" | custom-call | flops 905969664 | bytes 9000000 | tf_op jit(solution)/shard_map/pallas_call | solution.py:26
  116.1 4.6 %all-to-all-start.1 = ((f32[64,1,24]{2,1,0:T(1,128)}), f32[64,1,24]{2,1,0:T(1,128)S(1)}, u32[]{:S(2)}, u32[]{:S(2)}) async-start(f32[64,1,24]{2,1,0:T(1,128)} %bitcast.25), calls=%async_computation.1 | async-start | bytes 65536 | tf_op jit(solution)/shard_map/all_to_all | solution.py:224
  122.3 9.3 %all-to-all-done.1 = f32[64,1,24]{2,1,0:T(1,128)S(1)} async-done(((f32[64,1,24]{2,1,0:T(1,128)}), f32[64,1,24]{2,1,0:T(1,128)S(1)}, u32[]{:S(2)}, u32[]{:S(2)}) %all-to-all-start.1) | async-done | bytes 6176 | tf_op jit(solution)/shard_map/all_to_all | solution.py:224
  131.6 10.6 %collective-permute-start.15 = (f32[8,24]{1,0:T(8,128)S(1)}, f32[8,24]{1,0:T(8,128)S(1)}, u32[]{:S(2)}, u32[]{:S(2)}) collective-permute-start(f32[8,24]{1,0:T(8,128)S(1)} %bitcast_reduce_fusion), channel_id=1, source_target_pairs={{0,1},{1,0},{2,3},{3,2},{4,5},{5,4},{6,7},{7,6},{8,9},{9,8},{10,11... | collective-permute-start | bytes 2312 | tf_op jit(solution)/shard_map/ppermute | solution.py:149
  143.8 2.2 %collective-permute-start.16 = (f32[8,24]{1,0:T(8,128)S(1)}, f32[8,24]{1,0:T(8,128)S(1)}, u32[]{:S(2)}, u32[]{:S(2)}) collective-permute-start(f32[8,24]{1,0:T(8,128)S(1)} %add.53), channel_id=1, source_target_pairs={{0,2},{1,7},{2,0},{3,5},{4,6},{5,3},{6,4},{7,1},{8,10},{9,15},{10,... | collective-permute-start | bytes 2312 | tf_op jit(solution)/shard_map/ppermute | solution.py:158
  147.7 4.4 %collective-permute-start.12 = (bf16[288,512]{1,0:T(8,128)(2,1)}, bf16[288,512]{1,0:T(8,128)(2,1)S(1)}, u32[]{:S(2)}, u32[]{:S(2)}) collective-permute-start(bf16[288,512]{1,0:T(8,128)(2,1)} %copy-done.30), channel_id=1, source_target_pairs={{0,2},{1,7},{2,0},{3,5},{4,6},{5,3},{6,4},{7,1},{8,10},{9,15},{10,... | collective-permute-start | bytes 884744 | tf_op jit(solution)/shard_map/ppermute | solution.py:158
  158.9 3.5 %collective-permute-start.13 = (bf16[288,256]{1,0:T(8,128)(2,1)S(1)}, bf16[288,256]{1,0:T(8,128)(2,1)S(1)}, u32[]{:S(2)}, u32[]{:S(2)}) collective-permute-start(bf16[288,256]{1,0:T(8,128)(2,1)S(1)} %slice.147), channel_id=1, source_target_pairs={{0,6},{1,3},{2,4},{3,1},{4,2},{5,7},{6,0},{7,5},{8,14},{9,11},{10,... | collective-permute-start | bytes 442376 | tf_op jit(solution)/shard_map/ppermute | solution.py:158
  163.0 1.9 %collective-permute-done.13 = bf16[288,256]{1,0:T(8,128)(2,1)S(1)} collective-permute-done((bf16[288,256]{1,0:T(8,128)(2,1)S(1)}, bf16[288,256]{1,0:T(8,128)(2,1)S(1)}, u32[]{:S(2)}, u32[]{:S(2)}) %collective-permute-start.13) | collective-permute-done | bytes 147488 | tf_op jit(solution)/shard_map/ppermute | solution.py:158
  165.0 4.9 %collective-permute-start.14 = (bf16[768,128]{1,0:T(8,128)(2,1)S(1)}, bf16[768,128]{1,0:T(8,128)(2,1)S(1)}, u32[]{:S(2)}, u32[]{:S(2)}) collective-permute-start(bf16[768,128]{1,0:T(8,128)(2,1)S(1)} %select_convert_fusion), channel_id=1, source_target_pairs={{0,1},{1,0},{2,3},{3,2},{4,5},{5,4},{6,7},{7,6},{8,9},{9,8},{10,11... | collective-permute-start | bytes 589832 | tf_op jit(solution)/shard_map/ppermute | solution.py:149
  170.0 5.2 %shard_map.97 = bf16[1024,768]{1,0:T(8,128)(2,1)} custom-call(s32[3]{0:T(128)S(1)} %pad_add_fusion.table.refs_0_, bf16[2,96,768]{2,1,0:T(8,128)(2,1)S(1)} %get-tuple-element.29.refs_1_.refs_0_, bf16[2,96,768]{2,1,0:T(8,128)(2,1)S(1)} %copy-done.13, bf16[2,96,768]{2,1,0:T(8,128)(2,1)S(1)} %copy-done.16, bf16[2,96,768]{2,1,0:T(8,128)(2,1)S(1)} %copy-done.20, ...), custom_call_target="tpu_custom_call" | custom-call | flops 2415919104 | bytes 9000000 | tf_op jit(solution)/shard_map/pallas_call | solution.py:26
  (136 shorter events, 48.7 us)
Async XLA Ops:
  7.2 62.9 %all-gather.3.cloned.1.call-start = ((), (), s32[]{:S(2)}) async-start(), calls=%async_computation.2 | async-start | bytes 3538944 | tf_op jit(solution)/shard_map/all_gather | solution.py:174
  10.9 39.0 %copy-start.2 = (bf16[1024,768]{1,0:T(8,128)(2,1)S(1)}, bf16[1024,768]{1,0:T(8,128)(2,1)}, u32[]{:S(2)}) copy-start(bf16[1024,768]{1,0:T(8,128)(2,1)} %refs_4_.1) | copy-start | bytes 4718596
  29.0 6.4 %collective-permute-start = (bf16[192,768]{1,0:T(8,128)(2,1)S(1)}, bf16[192,768]{1,0:T(8,128)(2,1)S(1)}, u32[]{:S(2)}, u32[]{:S(2)}) collective-permute-start(bf16[192,768]{1,0:T(8,128)(2,1)S(1)} %bitcast.67), channel_id=1, source_target_pairs={{0,1},{1,0},{2,3},{3,2},{4,5},{5,4},{6,7},{7,6},{8,9},{9,8},{10,11... | collective-permute-start | bytes 884744 | tf_op jit(solution)/shard_map/ppermute | solution.py:149
  35.5 14.3 %collective-permute-start.1 = (bf16[2,96,768]{2,1,0:T(8,128)(2,1)S(1)}, bf16[2,96,768]{2,1,0:T(8,128)(2,1)S(1)}, u32[]{:S(2)}, u32[]{:S(2)}) collective-permute-start(bf16[2,96,768]{2,1,0:T(8,128)(2,1)S(1)} %get-tuple-element.29.refs_1_.refs_0_), channel_id=1, source_target_pairs={{0,8},{1,57},{8,16},{9,1},{16,24},{17,9},{24,32},{25,17},{32,40},{... | collective-permute-start | bytes 884744 | tf_op jit(solution)/shard_map/ppermute | solution.py:152
  49.8 20.3 %collective-permute-start.7 = (bf16[1024,768]{1,0:T(8,128)(2,1)S(1)}, bf16[1024,768]{1,0:T(8,128)(2,1)S(1)}, u32[]{:S(2)}, u32[]{:S(2)}) collective-permute-start(bf16[1024,768]{1,0:T(8,128)(2,1)S(1)} %copy-done.2), channel_id=1, source_target_pairs={{0,1},{1,0},{2,3},{3,2},{4,5},{5,4},{6,7},{7,6},{8,9},{9,8},{10,11... | collective-permute-start | bytes 4718600 | tf_op jit(solution)/shard_map/ppermute | solution.py:149
  53.4 7.8 %collective-permute-start.2 = (bf16[2,96,768]{2,1,0:T(8,128)(2,1)S(1)}, bf16[2,96,768]{2,1,0:T(8,128)(2,1)S(1)}, u32[]{:S(2)}, u32[]{:S(2)}) collective-permute-start(bf16[2,96,768]{2,1,0:T(8,128)(2,1)S(1)} %get-tuple-element.28.refs_8_), channel_id=1, source_target_pairs={{0,8},{1,57},{8,16},{9,1},{16,24},{17,9},{24,32},{25,17},{32,40},{... | collective-permute-start | bytes 884744 | tf_op jit(solution)/shard_map/ppermute | solution.py:152
  57.8 8.7 %collective-permute-start.3 = (bf16[2,96,768]{2,1,0:T(8,128)(2,1)S(1)}, bf16[2,96,768]{2,1,0:T(8,128)(2,1)S(1)}, u32[]{:S(2)}, u32[]{:S(2)}) collective-permute-start(bf16[2,96,768]{2,1,0:T(8,128)(2,1)S(1)} %collective-permute-done.1.refs_2_.refs_1_), channel_id=1, source_target_pairs={{0,8},{1,57},{8,16},{9,1},{16,24},{17,9},{24,32},{25,17},{32,40},{... | collective-permute-start | bytes 884744 | tf_op jit(solution)/shard_map/ppermute | solution.py:152
  61.2 8.2 %collective-permute-start.4 = (bf16[2,96,768]{2,1,0:T(8,128)(2,1)S(1)}, bf16[2,96,768]{2,1,0:T(8,128)(2,1)S(1)}, u32[]{:S(2)}, u32[]{:S(2)}) collective-permute-start(bf16[2,96,768]{2,1,0:T(8,128)(2,1)S(1)} %collective-permute-done.2.refs_3_.refs_2_), channel_id=1, source_target_pairs={{0,8},{1,57},{8,16},{9,1},{16,24},{17,9},{24,32},{25,17},{32,40},{... | collective-permute-start | bytes 884744 | tf_op jit(solution)/shard_map/ppermute | solution.py:152
  80.5 13.4 %collective-permute-start.10 = (bf16[480,512]{1,0:T(8,128)(2,1)}, bf16[480,512]{1,0:T(8,128)(2,1)S(1)}, u32[]{:S(2)}, u32[]{:S(2)}) collective-permute-start(bf16[480,512]{1,0:T(8,128)(2,1)} %get-tuple-element.17), channel_id=1, source_target_pairs={{0,2},{1,7},{2,0},{3,5},{4,6},{5,3},{6,4},{7,1},{8,10},{9,15},{10,... | collective-permute-start | bytes 1474568 | tf_op jit(solution)/shard_map/ppermute | solution.py:158
  86.0 13.1 %copy-start.19 = (bf16[2,96,768]{2,1,0:T(8,128)(2,1)S(1)}, bf16[2,96,768]{2,1,0:T(8,128)(2,1)}, u32[]{:S(2)}) copy-start(bf16[2,96,768]{2,1,0:T(8,128)(2,1)} %copy-done.17) | copy-start | bytes 884740
  87.0 12.2 %collective-permute-start.5 = (bf16[2,96,768]{2,1,0:T(8,128)(2,1)}, bf16[2,96,768]{2,1,0:T(8,128)(2,1)}, u32[]{:S(2)}, u32[]{:S(2)}) collective-permute-start(bf16[2,96,768]{2,1,0:T(8,128)(2,1)} %copy-done.17), channel_id=1, source_target_pairs={{0,8},{1,57},{8,16},{9,1},{16,24},{17,9},{24,32},{25,17},{32,40},{... | collective-permute-start | bytes 884744 | tf_op jit(solution)/shard_map/ppermute | solution.py:152
  92.0 15.9 %collective-permute-start.6 = (bf16[2,96,768]{2,1,0:T(8,128)(2,1)}, bf16[2,96,768]{2,1,0:T(8,128)(2,1)}, u32[]{:S(2)}, u32[]{:S(2)}) collective-permute-start(bf16[2,96,768]{2,1,0:T(8,128)(2,1)} %copy-done.21), channel_id=1, source_target_pairs={{0,8},{1,57},{8,16},{9,1},{16,24},{17,9},{24,32},{25,17},{32,40},{... | collective-permute-start | bytes 884744 | tf_op jit(solution)/shard_map/ppermute | solution.py:152
  94.7 13.2 %copy-start.1 = (bf16[16,768,128]{2,1,0:T(8,128)(2,1)S(1)}, bf16[16,768,128]{2,1,0:T(8,128)(2,1)}, u32[]{:S(2)}) copy-start(bf16[16,768,128]{2,1,0:T(8,128)(2,1)} %all-gather.3.cloned.1.call-done) | copy-start | bytes 9437188
  97.2 7.2 %collective-permute-start.11 = (bf16[480,256]{1,0:T(8,128)(2,1)}, bf16[480,256]{1,0:T(8,128)(2,1)}, u32[]{:S(2)}, u32[]{:S(2)}) collective-permute-start(bf16[480,256]{1,0:T(8,128)(2,1)} %slice.146), channel_id=1, source_target_pairs={{0,6},{1,3},{2,4},{3,1},{4,2},{5,7},{6,0},{7,5},{8,14},{9,11},{10,... | collective-permute-start | bytes 737288 | tf_op jit(solution)/shard_map/ppermute | solution.py:158
  100.1 7.8 %collective-permute-start.8 = (bf16[2,96,768]{2,1,0:T(8,128)(2,1)}, bf16[2,96,768]{2,1,0:T(8,128)(2,1)}, u32[]{:S(2)}, u32[]{:S(2)}) collective-permute-start(bf16[2,96,768]{2,1,0:T(8,128)(2,1)} %collective-permute-done.5.refs_1_.refs_5_), channel_id=1, source_target_pairs={{0,8},{1,57},{8,16},{9,1},{16,24},{17,9},{24,32},{25,17},{32,40},{... | collective-permute-start | bytes 884744 | tf_op jit(solution)/shard_map/ppermute | solution.py:152
  116.1 15.4 %all-to-all-start.1 = ((f32[64,1,24]{2,1,0:T(1,128)}), f32[64,1,24]{2,1,0:T(1,128)S(1)}, u32[]{:S(2)}, u32[]{:S(2)}) async-start(f32[64,1,24]{2,1,0:T(1,128)} %bitcast.25), calls=%async_computation.1 | async-start | bytes 65536 | tf_op jit(solution)/shard_map/all_to_all | solution.py:224
  131.6 12.2 %collective-permute-start.15 = (f32[8,24]{1,0:T(8,128)S(1)}, f32[8,24]{1,0:T(8,128)S(1)}, u32[]{:S(2)}, u32[]{:S(2)}) collective-permute-start(f32[8,24]{1,0:T(8,128)S(1)} %bitcast_reduce_fusion), channel_id=1, source_target_pairs={{0,1},{1,0},{2,3},{3,2},{4,5},{5,4},{6,7},{7,6},{8,9},{9,8},{10,11... | collective-permute-start | bytes 2312 | tf_op jit(solution)/shard_map/ppermute | solution.py:149
  143.8 21.1 %copy-start.31 = (f32[480,256]{1,0:T(8,128)S(1)}, f32[480,256]{1,0:T(8,128)}, u32[]{:S(2)}) copy-start(f32[480,256]{1,0:T(8,128)} %slice_add_fusion) | copy-start | bytes 1474564
  143.8 8.2 %collective-permute-start.16 = (f32[8,24]{1,0:T(8,128)S(1)}, f32[8,24]{1,0:T(8,128)S(1)}, u32[]{:S(2)}, u32[]{:S(2)}) collective-permute-start(f32[8,24]{1,0:T(8,128)S(1)} %add.53), channel_id=1, source_target_pairs={{0,2},{1,7},{2,0},{3,5},{4,6},{5,3},{6,4},{7,1},{8,10},{9,15},{10,... | collective-permute-start | bytes 2312 | tf_op jit(solution)/shard_map/ppermute | solution.py:158
  147.7 10.0 %collective-permute-start.12 = (bf16[288,512]{1,0:T(8,128)(2,1)}, bf16[288,512]{1,0:T(8,128)(2,1)S(1)}, u32[]{:S(2)}, u32[]{:S(2)}) collective-permute-start(bf16[288,512]{1,0:T(8,128)(2,1)} %copy-done.30), channel_id=1, source_target_pairs={{0,2},{1,7},{2,0},{3,5},{4,6},{5,3},{6,4},{7,1},{8,10},{9,15},{10,... | collective-permute-start | bytes 884744 | tf_op jit(solution)/shard_map/ppermute | solution.py:158
  152.1 5.4 %collective-permute-start.17 = (f32[8,24]{1,0:T(8,128)S(1)}, f32[8,24]{1,0:T(8,128)S(1)}, u32[]{:S(2)}, u32[]{:S(2)}) collective-permute-start(f32[8,24]{1,0:T(8,128)S(1)} %add.54), channel_id=1, source_target_pairs={{0,6},{1,3},{2,4},{3,1},{4,2},{5,7},{6,0},{7,5},{8,14},{9,11},{10,... | collective-permute-start | bytes 2312 | tf_op jit(solution)/shard_map/ppermute | solution.py:158
  155.6 14.4 %collective-permute-start.9 = (bf16[672,768]{1,0:T(8,128)(2,1)}, bf16[672,768]{1,0:T(8,128)(2,1)S(1)}, u32[]{:S(2)}, u32[]{:S(2)}) collective-permute-start(bf16[672,768]{1,0:T(8,128)(2,1)} %fusion.3), channel_id=1, source_target_pairs={{0,1},{1,0},{2,3},{3,2},{4,5},{5,4},{6,7},{7,6},{8,9},{9,8},{10,11... | collective-permute-start | bytes 3096584 | tf_op jit(solution)/shard_map/ppermute | solution.py:149
  158.9 6.0 %collective-permute-start.13 = (bf16[288,256]{1,0:T(8,128)(2,1)S(1)}, bf16[288,256]{1,0:T(8,128)(2,1)S(1)}, u32[]{:S(2)}, u32[]{:S(2)}) collective-permute-start(bf16[288,256]{1,0:T(8,128)(2,1)S(1)} %slice.147), channel_id=1, source_target_pairs={{0,6},{1,3},{2,4},{3,1},{4,2},{5,7},{6,0},{7,5},{8,14},{9,11},{10,... | collective-permute-start | bytes 442376 | tf_op jit(solution)/shard_map/ppermute | solution.py:158
  165.0 10.3 %collective-permute-start.14 = (bf16[768,128]{1,0:T(8,128)(2,1)S(1)}, bf16[768,128]{1,0:T(8,128)(2,1)S(1)}, u32[]{:S(2)}, u32[]{:S(2)}) collective-permute-start(bf16[768,128]{1,0:T(8,128)(2,1)S(1)} %select_convert_fusion), channel_id=1, source_target_pairs={{0,1},{1,0},{2,3},{3,2},{4,5},{5,4},{6,7},{7,6},{8,9},{9,8},{10,11... | collective-permute-start | bytes 589832 | tf_op jit(solution)/shard_map/ppermute | solution.py:149
  (31 other events, 106.9 us)
Sparse Core Ops, SparseCore 0:
  11.0 38.9 all-gather.2

commit v5 on v4

v5 whole, which is shorter than its diff:
```python
import jax
import jax.numpy as jnp
from jax import lax
from jax.experimental import pallas as pl
from jax.experimental.pallas import tpu as pltpu
from jax.sharding import Mesh
from jax.sharding import PartitionSpec as P

EXPERTS = 8
CAP = 24
NZ = 8
NX = 4
BLOCK = EXPERTS * CAP
SLOTS = NZ * BLOCK
PART = SLOTS // 2
BF = jnp.bfloat16
F32 = jnp.float32
WHOLE = pl.BlockSpec()
SM = pl.BlockSpec(memory_space=pltpu.SMEM)


def call(body, outs, ins, cost, scratch=()):
    specs = [SM if a.dtype == jnp.int32 and a.shape == (2,) else WHOLE for a in ins]
    return pl.pallas_call(
        body,
        out_shape=[jax.ShapeDtypeStruct(s, d) for s, d in outs],
        in_specs=specs,
        out_specs=[WHOLE] * len(outs),
        scratch_shapes=scratch,
        compiler_params=pltpu.CompilerParams(vmem_limit_bytes=40 * 2**20),
        cost_estimate=pl.CostEstimate(flops=cost[0], bytes_accessed=cost[1], transcendentals=0),
    )(*ins)


def dot(a, b, da, db):
    return lax.dot_general(a, b, (((da,), (db,)), ((), ())), preferred_element_type=F32)


def pack_body(routes, gates_ref, rows, out):
    gates = gates_ref[...].astype(F32)
    tokens = rows.shape[0]
    expert = lax.broadcasted_iota(jnp.int32, (EXPERTS, tokens), 0)
    first, second = routes[0:1, :] == expert, routes[1:2, :] == expert
    weight = jnp.where(first, gates[0:1, :], 0.0) + jnp.where(second, gates[1:2, :], 0.0)
    member = jnp.where(first | second, 1.0, 0.0)
    at = lax.broadcasted_iota(jnp.int32, (tokens, tokens), 0)
    to = lax.broadcasted_iota(jnp.int32, (tokens, tokens), 1)
    earlier = jnp.where(at < to, 1.0, 0.0).astype(BF)
    rank = dot(member.astype(BF), earlier, 1, 0)
    rank = jnp.where(member > 0.0, rank, -1.0).astype(jnp.int32)
    place = lax.broadcasted_iota(jnp.int32, (CAP, tokens), 0)
    chosen = [
        jnp.where(rank[e : e + 1] == place, weight[e : e + 1], 0.0) for e in range(EXPERTS)
    ]
    out[...] = dot(jnp.concatenate(chosen, axis=0).astype(BF), rows[...], 1, 0).astype(BF)


def act_body(gate, up, hidden):
    for z in range(NZ):
        a = gate[:, z].astype(F32).reshape(BLOCK, 128)
        b = up[:, z].astype(F32).reshape(BLOCK, 128)
        sig = 1.0 / (1.0 + jnp.exp(-a))
        hidden[z // 4, pl.ds(z % 4 * BLOCK, BLOCK), :] = (a * sig * b).astype(BF)


def product_body(rows, w, out):
    part = dot(rows[...], w[...], 1, 1).astype(BF)
    out[0] = part[:, :128]
    out[1] = part[:, 128:]


def hidden_blocks(place, refs):
    masks = (0, 3 - 2 * place[1], 1 + 2 * place[1], 2)
    lent = refs[4]
    for label in range(4):
        yield place[0] ^ masks[label], refs[label], lent[(0, 2, 1, 3)[label]]


def slots_of(core):
    return pl.ds(pl.multiple_of(core * PART, PART), PART)


def dots_body(place, parts, h0, h1, h2, h3, lent, dots, total):
    core = place[1]
    mine, others = slots_of(core), slots_of(1 - core)
    total[...] = jnp.zeros_like(total)
    for x, own, got in hidden_blocks(place, (h0, h1, h2, h3, lent)):
        for i in range(2):
            total[mine, :] += parts[2 * x + i, mine, :].astype(F32) * own[i].astype(F32)
            total[others, :] += parts[2 * x + i, others, :].astype(F32) * got[i].astype(F32)
    dots[...] = lax.dot_general(
        jnp.ones((8, 128), F32), total[...], (((1,), (1,)), ((), ())),
        precision=lax.Precision.HIGHEST, preferred_element_type=F32,
    )


def weight_body(place, rows, h0, h1, h2, h3, lent, out, units):
    core = place[1]
    mine, others = slots_of(core), slots_of(1 - core)
    for x, own, got in hidden_blocks(place, (h0, h1, h2, h3, lent)):
        for i in range(2):
            units[mine, pl.ds(i * 128, 128)] = own[i]
            units[others, pl.ds(i * 128, 128)] = got[i]
        at = pl.ds(pl.multiple_of(x * 256, 256), 256)
        out[at, :] = dot(units[...], rows[...], 0, 0).astype(BF)


def grad_body(hidden_grad, gate, up, gate_out, up_out):
    for z in range(NZ):
        src = hidden_grad[pl.ds(z * BLOCK, BLOCK), :].astype(F32).reshape(EXPERTS, CAP, 128)
        a, b = gate[:, z].astype(F32), up[:, z].astype(F32)
        sig = 1.0 / (1.0 + jnp.exp(-a))
        gate_out[:, z] = (src * b * sig * (1.0 + a * (1.0 - sig))).astype(BF)
        up_out[:, z] = (src * (a * sig)).astype(BF)


def per_device(grad_out, routes, gates, w_down, gate_pre, up_pre):
    xi, ci = lax.axis_index("x"), lax.axis_index("c")
    tokens, width = grad_out.shape
    ff = w_down.shape[0]
    place = jnp.stack([xi, ci]).astype(jnp.int32)

    def swap_core(x):
        return lax.ppermute(x, "c", [(0, 1), (1, 0)])

    def swap_x(x, first):
        masks = (1, 3) if first else (3, 1)
        return lax.ppermute(
            x, ("x", "c"), [(i * 2 + c, (i ^ masks[c]) * 2 + c) for i in range(NX) for c in range(2)]
        )

    routes_t, gates_t = routes.T, gates.T
    (packed,) = call(
        pack_body, [((BLOCK, width), BF)], (routes_t, gates_t, grad_out), (2 * BLOCK * tokens * width, 400000)
    )
    own = lax.all_to_all(
        packed.reshape(EXPERTS, CAP, width), "y", split_axis=0, concat_axis=0, tiled=True
    ).reshape(BLOCK, width)
    rows = lax.all_gather(own, "z", axis=0, tiled=True)

    view = (EXPERTS, NZ, CAP, 128)
    gate_late, up_late, _ = lax.optimization_barrier((gate_pre, up_pre, own))
    gate_view, up_view = gate_late.reshape(view), up_late.reshape(view)
    (hid,) = call(
        act_body, [((2, PART, 128), BF)], (gate_view, up_view), (20 * SLOTS * 128, 2000000)
    )
    keep = lax.dynamic_index_in_dim(hid, ci, 0, keepdims=False)
    got = swap_core(lax.dynamic_index_in_dim(hid, 1 - ci, 0, keepdims=False))
    h0 = jnp.stack([jnp.where(ci == 0, keep, got), jnp.where(ci == 0, got, keep)])
    h2 = swap_x(h0, True)
    h1 = swap_x(h0, False)
    h3 = swap_x(h2, False)
    lent = swap_core(jnp.stack([h0, h1, h2, h3]))
    rows, lent = lax.optimization_barrier((rows, lent))
    hiddens = (h0, h1, h2, h3, lent)

    parts = pl.pallas_call(
        product_body,
        grid=(NX,),
        out_shape=jax.ShapeDtypeStruct((2 * NX, SLOTS, 128), BF),
        in_specs=[
            pl.BlockSpec((SLOTS, width), lambda i: (0, 0)),
            pl.BlockSpec((ff // NX, width), lambda i: (i, 0)),
        ],
        out_specs=pl.BlockSpec((2, SLOTS, 128), lambda i: (i, 0, 0)),
        compiler_params=pltpu.CompilerParams(vmem_limit_bytes=40 * 2**20),
        cost_estimate=pl.CostEstimate(
            flops=2 * SLOTS * ff * width, bytes_accessed=8000000, transcendentals=0
        ),
    )(rows, w_down)
    hidden_grad = lax.psum_scatter(parts, ("x", "c"), scatter_dimension=0)
    gate_pre_grad, up_pre_grad = call(
        grad_body, [(view, BF), (view, BF)], (hidden_grad, gate_view, up_view), (4 * SLOTS * 128, 3000000)
    )

    (dots,) = call(
        dots_body,
        [((8, SLOTS), F32)],
        (place, parts, *hiddens),
        (2 * SLOTS * ff, 6000000),
        (pltpu.VMEM((SLOTS, 128), F32),),
    )
    back = lax.all_to_all(
        dots[0].reshape(NZ * EXPERTS, CAP), ("z", "y"), split_axis=0, concat_axis=0, tiled=True
    )
    totals = jnp.sum(back.reshape(NZ, EXPERTS, CAP), axis=0)
    totals = totals + swap_core(totals)
    totals = totals + swap_x(totals, True)
    totals = totals + swap_x(totals, False)

    named = routes_t[:, None, :] == jnp.arange(EXPERTS, dtype=jnp.int32)[None, :, None]
    member = jnp.any(named, axis=0)
    order = jnp.arange(tokens, dtype=jnp.int32)
    earlier = (order[:, None] < order[None, :]).astype(BF)
    rank = jnp.dot(member.astype(BF), earlier, preferred_element_type=F32).astype(jnp.int32)
    chosen = member[:, None, :] & (rank[:, None, :] == jnp.arange(CAP, dtype=jnp.int32)[None, :, None])
    by_token = jnp.sum(jnp.where(chosen, totals[:, :, None], 0.0), axis=1)
    gate_grad = jnp.sum(jnp.where(named, by_token[None], 0.0), axis=1) / gates_t.astype(F32)

    (w_down_grad,) = call(
        weight_body,
        [((ff, width), BF)],
        (place, rows, *hiddens),
        (2 * SLOTS * ff * width, 9000000),
        (pltpu.VMEM((SLOTS, 256), BF),),
    )
    flat = (EXPERTS * NZ * CAP, 128)
    return (w_down_grad, gate_pre_grad.reshape(flat), up_pre_grad.reshape(flat), gate_grad.T)


def solution(mesh):
    fine = Mesh(mesh.devices.reshape(EXPERTS, NZ, NX, 2), ("y", "z", "x", "c"))
    e, t = ("y", "z"), ("x", "c")
    return jax.shard_map(
        per_device,
        mesh=fine,
        in_specs=(P(e, t), P(e, None), P(e, None), P(e, t), P(None, e + t), P(None, e + t)),
        out_specs=(P(e, t), P(None, e + t), P(None, e + t), P(e, None)),
        check_vma=False,
    )
```

time: 185 us -> 139 us (0.75)
  starting transfers between devices: 80.2 us -> 36.6 us
  local copies, waits for them, and re-layouts: 29.3 us -> 9.78 us
  blocking collectives: 17.8 us -> 37.3 us
  other arithmetic: 5.77 us -> 1.09 us
  waiting for transfers between devices: 21.5 us -> 24 us
    ppermute x7 -> x0, starting transfers between devices: 31 us -> none  [ring(): lax.ppermute(x, ('z', 'c'), [(z * 2 + c, (z + 1 - 2 * c) % NZ * 2 + c) fo...]
    all_to_all x0 -> x1, blocking collectives: none -> 19.9 us  [per_device(): lax.all_to_all(dots[0].reshape(NZ * EXPERTS, CAP), ('z', 'y'), split_axis...]
    unnamed x76 -> x24, local copies, waits for them, and re-layouts: 25.7 us -> 9.02 us
    all_to_all x1 -> x0, waiting for transfers between devices: 9.26 us -> none  [per_device(): lax.all_to_all(by_source.reshape(EXPERTS * NZ, CAP), ('y', 'z'), split_ax...]
    all_gather x1, waiting for transfers between devices: 0.01 us -> 8.88 us  [per_device(): rows = lax.all_gather(own, 'z', axis=0, tiled=True)]
    ppermute x7 -> x0, waiting for transfers between devices: 7.9 us -> none  [ring(): lax.ppermute(x, ('z', 'c'), [(z * 2 + c, (z + 1 - 2 * c) % NZ * 2 + c) fo...]
    ppermute x6 -> x5, waiting for transfers between devices: 3.14 us -> 10.3 us  [swap_x(): lax.ppermute(x, ('x', 'c'), [(i * 2 + c, (i ^ masks[c]) * 2 + c) for i in...]
    ppermute x5 -> x3, starting transfers between devices: 26.3 us -> 20.1 us  [swap_core(): return lax.ppermute(x, 'c', [(0, 1), (1, 0)])]
  transfers between devices with their start and end apart: 20 -> 10, of which waited for: 8 -> 8; matrix products, arithmetic and copies ran while one was open for 8% -> 1% of each run, Pallas kernels for 3% -> 7%
where the time goes in v5:
time: 139 us; the launch traced here: 138 us
  blocking collectives  37.3 us (27%)
  starting transfers between devices  36.6 us (26%)
  waiting for transfers between devices  24 us (17%)
  Pallas kernels  15.3 us (11%)
  between operations  14.3 us (10%)
  local copies, waits for them, and re-layouts  9.78 us (7%)
    ppermute x3, starting transfers between devices, swap_core(): return lax.ppermute(x, 'c', [(0, 1), (1, 0)])  20.1 us
    all_to_all x1, blocking collectives, per_device(): lax.all_to_all(dots[0].reshape(NZ * EXPERTS, CAP), ('z', 'y'), split_axis...  19.9 us
    all_to_all x1, blocking collectives, per_device(): lax.all_to_all(packed.reshape(EXPERTS, CAP, width), 'y', split_axis=0, co...  17.4 us
    ppermute x5, starting transfers between devices, swap_x(): lax.ppermute(x, ('x', 'c'), [(i * 2 + c, (i ^ masks[c]) * 2 + c) for i in...  16.4 us
    pallas_call x5, Pallas kernels, call(): pl.pallas_call(body, out_shape=[jax.ShapeDtypeStruct(s, d) for s, d in ou...  11 us
    ppermute x5, waiting for transfers between devices, swap_x(): lax.ppermute(x, ('x', 'c'), [(i * 2 + c, (i ^ masks[c]) * 2 + c) for i in...  10.3 us
    unnamed x24, local copies, waits for them, and re-layouts  9.02 us
    all_gather x1, waiting for transfers between devices, per_device(): rows = lax.all_gather(own, 'z', axis=0, tiled=True)  8.88 us
  transfers between devices with their start and end apart: 10, of which 8 were waited for; matrix products, arithmetic and copies ran while one was open for 1% of the time, Pallas kernels for 7%

profile of v5, /device:TPU:1, one launch (start us, length us, event | category | flops | bytes accessed | tf_op | source)
XLA Modules:
  0.0 138.4 jit_solution(6386555257527806195)
XLA Ops:
  9.9 17.4 %all_to_all.14 = bf16[8,24,768]{2,1,0:T(8,128)(2,1)} all-to-all(bf16[8,24,768]{2,1,0:T(8,128)(2,1)S(1)} %bitcast.43), channel_id=1, replica_groups=mesh['y'=8,'z'=8,'x'=4,'c'=2] {'y'}, dimensions={0} | all-to-all | bytes 589824 | tf_op jit(solution)/shard_map/all_to_all | solution.py:136
  27.6 5.6 %collective-permute-start = (bf16[768,128]{1,0:T(8,128)(2,1)S(1)}, bf16[768,128]{1,0:T(8,128)(2,1)S(1)}, u32[]{:S(2)}, u32[]{:S(2)}) collective-permute-start(bf16[768,128]{1,0:T(8,128)(2,1)S(1)} %dynamic-slice_bitcast_fusion), channel_id=1, source_target_pairs={{0,1},{1,0},{2,3},{3,2},{4,5},{5,4},{6,7},{7,6},{8,9},{9,8},{10,11... | collective-permute-start | bytes 589832 | tf_op jit(solution)/shard_map/ppermute | solution.py:124
  33.3 1.0 collective-permute-done
  34.4 4.4 %collective-permute-start.2 = (bf16[2,768,128]{2,1,0:T(8,128)(2,1)S(1)}, bf16[2,768,128]{2,1,0:T(8,128)(2,1)S(1)}, u32[]{:S(2)}, u32[]{:S(2)}) collective-permute-start(bf16[2,768,128]{2,1,0:T(8,128)(2,1)S(1)} %get-tuple-element.19.h0), channel_id=1, source_target_pairs={{0,2},{1,7},{2,0},{3,5},{4,6},{5,3},{6,4},{7,1},{8,10},{9,15},{10,... | collective-permute-start | bytes 1179656 | tf_op jit(solution)/shard_map/ppermute | solution.py:128
  38.8 1.9 %collective-permute-start.1 = (bf16[2,768,128]{2,1,0:T(8,128)(2,1)S(1)}, bf16[2,768,128]{2,1,0:T(8,128)(2,1)S(1)}, u32[]{:S(2)}, u32[]{:S(2)}) collective-permute-start(bf16[2,768,128]{2,1,0:T(8,128)(2,1)S(1)} %get-tuple-element.19.h0), channel_id=1, source_target_pairs={{0,6},{1,3},{2,4},{3,1},{4,2},{5,7},{6,0},{7,5},{8,14},{9,11},{10,... | collective-permute-start | bytes 1179656 | tf_op jit(solution)/shard_map/ppermute | solution.py:128
  40.7 3.4 %collective-permute-done.2.h2 = bf16[2,768,128]{2,1,0:T(8,128)(2,1)S(1)} collective-permute-done((bf16[2,768,128]{2,1,0:T(8,128)(2,1)S(1)}, bf16[2,768,128]{2,1,0:T(8,128)(2,1)S(1)}, u32[]{:S(2)}, u32[]{:S(2)}) %collective-permute-start.2) | collective-permute-done | bytes 393248 | tf_op jit(solution)/shard_map/ppermute | solution.py:128
  44.1 2.9 %collective-permute-start.3 = (bf16[2,768,128]{2,1,0:T(8,128)(2,1)S(1)}, bf16[2,768,128]{2,1,0:T(8,128)(2,1)S(1)}, u32[]{:S(2)}, u32[]{:S(2)}) collective-permute-start(bf16[2,768,128]{2,1,0:T(8,128)(2,1)S(1)} %collective-permute-done.2.h2), channel_id=1, source_target_pairs={{0,6},{1,3},{2,4},{3,1},{4,2},{5,7},{6,0},{7,5},{8,14},{9,11},{10,... | collective-permute-start | bytes 1179656 | tf_op jit(solution)/shard_map/ppermute | solution.py:128
  47.0 1.3 collective-permute-done.1.h1
  48.4 4.7 %collective-permute-done.3.h3 = bf16[2,768,128]{2,1,0:T(8,128)(2,1)S(1)} collective-permute-done((bf16[2,768,128]{2,1,0:T(8,128)(2,1)S(1)}, bf16[2,768,128]{2,1,0:T(8,128)(2,1)S(1)}, u32[]{:S(2)}, u32[]{:S(2)}) %collective-permute-start.3) | collective-permute-done | bytes 393248 | tf_op jit(solution)/shard_map/ppermute | solution.py:128
  53.2 6.6 %collective-permute-start.4 = (bf16[4,2,768,128]{3,2,1,0:T(8,128)(2,1)S(1)}, bf16[4,2,768,128]{3,2,1,0:T(8,128)(2,1)S(1)}, u32[]{:S(2)}, u32[]{:S(2)}) collective-permute-start(bf16[4,2,768,128]{3,2,1,0:T(8,128)(2,1)S(1)} %pad_maximum_fusion), channel_id=1, source_target_pairs={{0,1},{1,0},{2,3},{3,2},{4,5},{5,4},{6,7},{7,6},{8,9},{9,8},{10,11... | collective-permute-start | bytes 4718600 | tf_op jit(solution)/shard_map/ppermute | solution.py:124
  59.9 3.0 %collective-permute-done.4.lent = bf16[4,2,768,128]{3,2,1,0:T(8,128)(2,1)S(1)} collective-permute-done((bf16[4,2,768,128]{3,2,1,0:T(8,128)(2,1)S(1)}, bf16[4,2,768,128]{3,2,1,0:T(8,128)(2,1)S(1)}, u32[]{:S(2)}, u32[]{:S(2)}) %collective-permute-start.4) | collective-permute-done | bytes 1572896 | tf_op jit(solution)/shard_map/ppermute | solution.py:124
  62.9 8.9 %all-gather.2.cloned.1.call-done.rows = bf16[1536,768]{1,0:T(8,128)(2,1)} async-done(((bf16[192,768]{1,0:T(8,128)(2,1)}), bf16[1536,768]{1,0:T(8,128)(2,1)}) %all-gather.2.cloned.1.call-update) | async-done | bytes 2359312 | tf_op jit(solution)/shard_map/all_gather | solution.py:139
  71.8 1.7 %copy-done.9 = bf16[1536,768]{1,0:T(8,128)(2,1)S(1)} copy-done((bf16[1536,768]{1,0:T(8,128)(2,1)S(1)}, bf16[1536,768]{1,0:T(8,128)(2,1)}, u32[]{:S(2)}) %copy-start.9) | copy-done | bytes 2359320
  73.4 1.4 %copy-done.11 = bf16[1024,768]{1,0:T(8,128)(2,1)S(1)} copy-done((bf16[1024,768]{1,0:T(8,128)(2,1)S(1)}, bf16[1024,768]{1,0:T(8,128)(2,1)}, u32[]{:S(2)}) %copy-start.11) | copy-done | bytes 1572888
  74.8 4.3 %shard_map.96.parts = bf16[8,1536,128]{2,1,0:T(8,128)(2,1)} custom-call(bf16[1536,768]{1,0:T(8,128)(2,1)S(1)} %copy-done.9, bf16[1024,768]{1,0:T(8,128)(2,1)S(1)} %copy-done.11), custom_call_target="tpu_custom_call" | custom-call | flops 2415919104 | bytes 8000000 | tf_op jit(solution)/shard_map/pallas_call | solution.py:157
  79.2 4.2 %shard_map.98 = f32[8,1536]{1,0:T(8,128)S(1)} custom-call(s32[2]{0:T(128)S(1)} %pad_add_fusion.place, bf16[8,1536,128]{2,1,0:T(8,128)(2,1)} %shard_map.96.parts, bf16[2,768,128]{2,1,0:T(8,128)(2,1)S(1)} %get-tuple-element.19.h0, bf16[2,768,128]{2,1,0:T(8,128)(2,1)S(1)} %collective-permute-done.1.h1, bf16[2,768,128]{2,1,0:T(8,128)(2,1)S(1)} %collective-permute-done.2.h2, ...), custom_call_target="tpu_custom_call" | custom-call | flops 3145728 | bytes 6000000 | tf_op jit(solution)/shard_map/pallas_call | solution.py:24
  84.1 19.9 %all_to_all.15 = f32[64,1,24]{2,1,0:T(1,128)S(1)} all-to-all(f32[64,1,24]{2,1,0:T(1,128)} %bitcast.50), channel_id=1, replica_groups=mesh['y'=8,'z'=8,'x'=4,'c'=2] {'z','y'}, dimensions={0} | all-to-all | bytes 12288 | tf_op jit(solution)/shard_map/all_to_all | solution.py:183
  104.0 7.9 %collective-permute-start.5 = (f32[8,24]{1,0:T(8,128)S(1)}, f32[8,24]{1,0:T(8,128)S(1)}, u32[]{:S(2)}, u32[]{:S(2)}) collective-permute-start(f32[8,24]{1,0:T(8,128)S(1)} %bitcast_reduce_fusion), channel_id=1, source_target_pairs={{0,1},{1,0},{2,3},{3,2},{4,5},{5,4},{6,7},{7,6},{8,9},{9,8},{10,11... | collective-permute-start | bytes 2312 | tf_op jit(solution)/shard_map/ppermute | solution.py:124
  112.7 4.5 %collective-permute-start.6 = (f32[8,24]{1,0:T(8,128)S(1)}, f32[8,24]{1,0:T(8,128)S(1)}, u32[]{:S(2)}, u32[]{:S(2)}) collective-permute-start(f32[8,24]{1,0:T(8,128)S(1)} %add.21), channel_id=1, source_target_pairs={{0,2},{1,7},{2,0},{3,5},{4,6},{5,3},{6,4},{7,1},{8,10},{9,15},{10,... | collective-permute-start | bytes 2312 | tf_op jit(solution)/shard_map/ppermute | solution.py:128
  118.2 2.6 %collective-permute-start.7 = (f32[8,24]{1,0:T(8,128)S(1)}, f32[8,24]{1,0:T(8,128)S(1)}, u32[]{:S(2)}, u32[]{:S(2)}) collective-permute-start(f32[8,24]{1,0:T(8,128)S(1)} %add.22), channel_id=1, source_target_pairs={{0,6},{1,3},{2,4},{3,1},{4,2},{5,7},{6,0},{7,5},{8,14},{9,11},{10,... | collective-permute-start | bytes 2312 | tf_op jit(solution)/shard_map/ppermute | solution.py:128
  120.9 1.7 %copy-done.10 = bf16[1536,768]{1,0:T(8,128)(2,1)S(1)} copy-done((bf16[1536,768]{1,0:T(8,128)(2,1)S(1)}, bf16[1536,768]{1,0:T(8,128)(2,1)}, u32[]{:S(2)}) %copy-start.10) | copy-done | bytes 2359320
  122.5 4.9 %shard_map.95 = bf16[1024,768]{1,0:T(8,128)(2,1)} custom-call(s32[2]{0:T(128)S(1)} %pad_add_fusion.place, bf16[1536,768]{1,0:T(8,128)(2,1)S(1)} %copy-done.10, bf16[2,768,128]{2,1,0:T(8,128)(2,1)S(1)} %get-tuple-element.19.h0, bf16[2,768,128]{2,1,0:T(8,128)(2,1)S(1)} %collective-permute-done.1.h1, bf16[2,768,128]{2,1,0:T(8,128)(2,1)S(1)} %collective-permute-done.2.h2, ...), custom_call_target="tpu_custom_call" | custom-call | flops 2415919104 | bytes 9000000 | tf_op jit(solution)/shard_map/pallas_call | solution.py:24
  128.2 1.0 copy-done.2
  130.2 1.3 shard_map.97
  (46 shorter events, 7.6 us)
Async XLA Ops:
  7.2 20.1 %copy-start = (bf16[1536,128]{1,0:T(8,128)(2,1)S(1)}, bf16[1536,128]{1,0:T(8,128)(2,1)}, u32[]{:S(2)}) copy-start(bf16[1536,128]{1,0:T(8,128)(2,1)} %param.10) | copy-start | bytes 1179652
  7.2 20.1 %copy-start.1 = (bf16[1536,128]{1,0:T(8,128)(2,1)S(1)}, bf16[1536,128]{1,0:T(8,128)(2,1)}, u32[]{:S(2)}) copy-start(bf16[1536,128]{1,0:T(8,128)(2,1)} %param.11) | copy-start | bytes 1179652
  7.2 64.6 %all-gather.2.cloned.1.call-start = ((), (), s32[]{:S(2)}) async-start(), calls=%async_computation.3 | async-start | bytes 2654208 | tf_op jit(solution)/shard_map/all_gather | solution.py:139
  7.2 1.0 copy-start.4
  8.2 0.7 copy-start.5
  8.9 0.7 copy-start.7
  27.2 100.9 %reduce-scatter.2.cloned.1.call-start = ((), (), s32[]{:S(2)}) async-start(), calls=%async_computation.4 | async-start | bytes 3538944 | tf_op jit(solution)/shard_map/reduce_scatter | solution.py:171
  27.6 6.7 %collective-permute-start = (bf16[768,128]{1,0:T(8,128)(2,1)S(1)}, bf16[768,128]{1,0:T(8,128)(2,1)S(1)}, u32[]{:S(2)}, u32[]{:S(2)}) collective-permute-start(bf16[768,128]{1,0:T(8,128)(2,1)S(1)} %dynamic-slice_bitcast_fusion), channel_id=1, source_target_pairs={{0,1},{1,0},{2,3},{3,2},{4,5},{5,4},{6,7},{7,6},{8,9},{9,8},{10,11... | collective-permute-start | bytes 589832 | tf_op jit(solution)/shard_map/ppermute | solution.py:124
  34.4 9.7 %collective-permute-start.2 = (bf16[2,768,128]{2,1,0:T(8,128)(2,1)S(1)}, bf16[2,768,128]{2,1,0:T(8,128)(2,1)S(1)}, u32[]{:S(2)}, u32[]{:S(2)}) collective-permute-start(bf16[2,768,128]{2,1,0:T(8,128)(2,1)S(1)} %get-tuple-element.19.h0), channel_id=1, source_target_pairs={{0,2},{1,7},{2,0},{3,5},{4,6},{5,3},{6,4},{7,1},{8,10},{9,15},{10,... | collective-permute-start | bytes 1179656 | tf_op jit(solution)/shard_map/ppermute | solution.py:128
  38.8 9.6 %collective-permute-start.1 = (bf16[2,768,128]{2,1,0:T(8,128)(2,1)S(1)}, bf16[2,768,128]{2,1,0:T(8,128)(2,1)S(1)}, u32[]{:S(2)}, u32[]{:S(2)}) collective-permute-start(bf16[2,768,128]{2,1,0:T(8,128)(2,1)S(1)} %get-tuple-element.19.h0), channel_id=1, source_target_pairs={{0,6},{1,3},{2,4},{3,1},{4,2},{5,7},{6,0},{7,5},{8,14},{9,11},{10,... | collective-permute-start | bytes 1179656 | tf_op jit(solution)/shard_map/ppermute | solution.py:128
  44.1 8.9 %collective-permute-start.3 = (bf16[2,768,128]{2,1,0:T(8,128)(2,1)S(1)}, bf16[2,768,128]{2,1,0:T(8,128)(2,1)S(1)}, u32[]{:S(2)}, u32[]{:S(2)}) collective-permute-start(bf16[2,768,128]{2,1,0:T(8,128)(2,1)S(1)} %collective-permute-done.2.h2), channel_id=1, source_target_pairs={{0,6},{1,3},{2,4},{3,1},{4,2},{5,7},{6,0},{7,5},{8,14},{9,11},{10,... | collective-permute-start | bytes 1179656 | tf_op jit(solution)/shard_map/ppermute | solution.py:128
  53.2 9.6 %collective-permute-start.4 = (bf16[4,2,768,128]{3,2,1,0:T(8,128)(2,1)S(1)}, bf16[4,2,768,128]{3,2,1,0:T(8,128)(2,1)S(1)}, u32[]{:S(2)}, u32[]{:S(2)}) collective-permute-start(bf16[4,2,768,128]{3,2,1,0:T(8,128)(2,1)S(1)} %pad_maximum_fusion), channel_id=1, source_target_pairs={{0,1},{1,0},{2,3},{3,2},{4,5},{5,4},{6,7},{7,6},{8,9},{9,8},{10,11... | collective-permute-start | bytes 4718600 | tf_op jit(solution)/shard_map/ppermute | solution.py:124
  71.8 1.7 %copy-start.9 = (bf16[1536,768]{1,0:T(8,128)(2,1)S(1)}, bf16[1536,768]{1,0:T(8,128)(2,1)}, u32[]{:S(2)}) copy-start(bf16[1536,768]{1,0:T(8,128)(2,1)} %all-gather.2.cloned.1.call-done.rows) | copy-start | bytes 7077892
  73.4 1.4 %copy-start.11 = (bf16[1024,768]{1,0:T(8,128)(2,1)S(1)}, bf16[1024,768]{1,0:T(8,128)(2,1)}, u32[]{:S(2)}) copy-start(bf16[1024,768]{1,0:T(8,128)(2,1)} %w.1) | copy-start | bytes 4718596
  79.2 32.7 %copy-start.6 = (s32[64,2]{0,1:T(2,128)S(1)}, s32[64,2]{0,1:T(2,128)}, u32[]{:S(2)}) copy-start(s32[64,2]{0,1:T(2,128)} %param.7) | copy-start | bytes 1540
  104.0 8.7 %collective-permute-start.5 = (f32[8,24]{1,0:T(8,128)S(1)}, f32[8,24]{1,0:T(8,128)S(1)}, u32[]{:S(2)}, u32[]{:S(2)}) collective-permute-start(f32[8,24]{1,0:T(8,128)S(1)} %bitcast_reduce_fusion), channel_id=1, source_target_pairs={{0,1},{1,0},{2,3},{3,2},{4,5},{5,4},{6,7},{7,6},{8,9},{9,8},{10,11... | collective-permute-start | bytes 2312 | tf_op jit(solution)/shard_map/ppermute | solution.py:124
  112.7 5.5 %collective-permute-start.6 = (f32[8,24]{1,0:T(8,128)S(1)}, f32[8,24]{1,0:T(8,128)S(1)}, u32[]{:S(2)}, u32[]{:S(2)}) collective-permute-start(f32[8,24]{1,0:T(8,128)S(1)} %add.21), channel_id=1, source_target_pairs={{0,2},{1,7},{2,0},{3,5},{4,6},{5,3},{6,4},{7,1},{8,10},{9,15},{10,... | collective-permute-start | bytes 2312 | tf_op jit(solution)/shard_map/ppermute | solution.py:128
  118.2 9.4 %copy-start.8 = (bf16[64,2]{0,1:T(2,128)(2,1)S(1)}, bf16[64,2]{0,1:T(2,128)(2,1)}, u32[]{:S(2)}) copy-start(bf16[64,2]{0,1:T(2,128)(2,1)} %param.8) | copy-start | bytes 772
  118.2 9.2 %collective-permute-start.7 = (f32[8,24]{1,0:T(8,128)S(1)}, f32[8,24]{1,0:T(8,128)S(1)}, u32[]{:S(2)}, u32[]{:S(2)}) collective-permute-start(f32[8,24]{1,0:T(8,128)S(1)} %add.22), channel_id=1, source_target_pairs={{0,6},{1,3},{2,4},{3,1},{4,2},{5,7},{6,0},{7,5},{8,14},{9,11},{10,... | collective-permute-start | bytes 2312 | tf_op jit(solution)/shard_map/ppermute | solution.py:128
  120.9 1.7 %copy-start.10 = (bf16[1536,768]{1,0:T(8,128)(2,1)S(1)}, bf16[1536,768]{1,0:T(8,128)(2,1)}, u32[]{:S(2)}) copy-start(bf16[1536,768]{1,0:T(8,128)(2,1)} %all-gather.2.cloned.1.call-done.rows) | copy-start | bytes 7077892
  128.2 1.0 copy-start.2
  129.2 1.0 copy-start.3
Sparse Core Ops, SparseCore 0:
  27.4 44.3 all-gather.1
  79.2 40.9 reduce-scatter.1

commit v6 on v5

--- a/solution.py
+++ b/solution.py
@@ -15,19 +15,18 @@
 PART = SLOTS // 2
 BF = jnp.bfloat16
 F32 = jnp.float32
+LIMIT = 52 * 2**20
 WHOLE = pl.BlockSpec()
-SM = pl.BlockSpec(memory_space=pltpu.SMEM)
-
-
-def call(body, outs, ins, cost, scratch=()):
-    specs = [SM if a.dtype == jnp.int32 and a.shape == (2,) else WHOLE for a in ins]
+CHUNK = SLOTS // 4
+
+
+def call(body, outs, ins, cost):
     return pl.pallas_call(
         body,
         out_shape=[jax.ShapeDtypeStruct(s, d) for s, d in outs],
-        in_specs=specs,
+        in_specs=[WHOLE] * len(ins),
         out_specs=[WHOLE] * len(outs),
-        scratch_shapes=scratch,
-        compiler_params=pltpu.CompilerParams(vmem_limit_bytes=40 * 2**20),
+        compiler_params=pltpu.CompilerParams(vmem_limit_bytes=LIMIT),
         cost_estimate=pl.CostEstimate(flops=cost[0], bytes_accessed=cost[1], transcendentals=0),
     )(*ins)
 
@@ -63,46 +62,46 @@
         hidden[z // 4, pl.ds(z % 4 * BLOCK, BLOCK), :] = (a * sig * b).astype(BF)
 
 
-def product_body(rows, w, out):
-    part = dot(rows[...], w[...], 1, 1).astype(BF)
-    out[0] = part[:, :128]
-    out[1] = part[:, 128:]
-
-
-def hidden_blocks(place, refs):
-    masks = (0, 3 - 2 * place[1], 1 + 2 * place[1], 2)
-    lent = refs[4]
-    for label in range(4):
-        yield place[0] ^ masks[label], refs[label], lent[(0, 2, 1, 3)[label]]
-
-
-def slots_of(core):
-    return pl.ds(pl.multiple_of(core * PART, PART), PART)
-
-
-def dots_body(place, parts, h0, h1, h2, h3, lent, dots, total):
-    core = place[1]
-    mine, others = slots_of(core), slots_of(1 - core)
-    total[...] = jnp.zeros_like(total)
-    for x, own, got in hidden_blocks(place, (h0, h1, h2, h3, lent)):
+def x_of(label, place):
+    mask = jnp.where(label == 1, 3 - 2 * place[1], jnp.where(label == 2, 1 + 2 * place[1], label - label // 3))
+    return place[0] ^ mask
+
+
+def swapped(label):
+    return jnp.where(label == 1, 2, jnp.where(label == 2, 1, label))
+
+
+def product_body(place, rows, w, mine, lent, parts, dots, total):
+    label = pl.program_id(0)
+
+    @pl.when(label == 0)
+    def _():
+        total[...] = jnp.zeros_like(total)
+
+    for k in range(4):
+        at = pl.ds(k * CHUNK, CHUNK)
+        part = dot(rows[at, :], w[...], 1, 1)
+        here = pl.ds(k % 2 * CHUNK, CHUNK)
         for i in range(2):
-            total[mine, :] += parts[2 * x + i, mine, :].astype(F32) * own[i].astype(F32)
-            total[others, :] += parts[2 * x + i, others, :].astype(F32) * got[i].astype(F32)
-    dots[...] = lax.dot_general(
-        jnp.ones((8, 128), F32), total[...], (((1,), (1,)), ((), ())),
-        precision=lax.Precision.HIGHEST, preferred_element_type=F32,
-    )
-
-
-def weight_body(place, rows, h0, h1, h2, h3, lent, out, units):
-    core = place[1]
-    mine, others = slots_of(core), slots_of(1 - core)
-    for x, own, got in hidden_blocks(place, (h0, h1, h2, h3, lent)):
+            unit = part[:, i * 128 : i * 128 + 128]
+            parts[i, at, :] = unit.astype(BF)
+            hidden = jnp.where(place[1] == k // 2, mine[0, i, here, :], lent[0, i, here, :])
+            total[at, :] += unit * hidden.astype(F32)
+
+    @pl.when(label == NX - 1)
+    def _():
+        dots[...] = lax.dot_general(
+            jnp.ones((8, 128), F32), total[...], (((1,), (1,)), ((), ())),
+            precision=lax.Precision.HIGHEST, preferred_element_type=F32,
+        )
+
+
+def weight_body(place, rows, mine, lent, out, units):
+    for half in range(2):
         for i in range(2):
-            units[mine, pl.ds(i * 128, 128)] = own[i]
-            units[others, pl.ds(i * 128, 128)] = got[i]
-        at = pl.ds(pl.multiple_of(x * 256, 256), 256)
-        out[at, :] = dot(units[...], rows[...], 0, 0).astype(BF)
+            hidden = jnp.where(place[1] == half, mine[0, i], lent[0, i])
+            units[pl.ds(half * PART, PART), pl.ds(i * 128, 128)] = hidden
+    out[...] = dot(units[...], rows[...], 0, 0).astype(BF)
 
 
 def grad_body(hidden_grad, gate, up, gate_out, up_out):
@@ -150,36 +149,42 @@
     h2 = swap_x(h0, True)
     h1 = swap_x(h0, False)
     h3 = swap_x(h2, False)
-    lent = swap_core(jnp.stack([h0, h1, h2, h3]))
+    mine = jnp.stack([h0, h1, h2, h3])
+    lent = swap_core(mine)
     rows, lent = lax.optimization_barrier((rows, lent))
-    hiddens = (h0, h1, h2, h3, lent)
-
-    parts = pl.pallas_call(
+
+    hidden_specs = [
+        pl.BlockSpec((1, 2, PART, 128), lambda i, place: (i, 0, 0, 0)),
+        pl.BlockSpec((1, 2, PART, 128), lambda i, place: (swapped(i), 0, 0, 0)),
+    ]
+    rows_spec = pl.BlockSpec((SLOTS, width), lambda i, place: (0, 0))
+    units_spec = pl.BlockSpec((ff // NX, width), lambda i, place: (x_of(i, place), 0))
+    parts, dots = pl.pallas_call(
         product_body,
-        grid=(NX,),
-        out_shape=jax.ShapeDtypeStruct((2 * NX, SLOTS, 128), BF),
-        in_specs=[
-            pl.BlockSpec((SLOTS, width), lambda i: (0, 0)),
-            pl.BlockSpec((ff // NX, width), lambda i: (i, 0)),
+        out_shape=[
+            jax.ShapeDtypeStruct((2 * NX, SLOTS, 128), BF),
+            jax.ShapeDtypeStruct((8, SLOTS), F32),
         ],
-        out_specs=pl.BlockSpec((2, SLOTS, 128), lambda i: (i, 0, 0)),
-        compiler_params=pltpu.CompilerParams(vmem_limit_bytes=40 * 2**20),
+        grid_spec=pltpu.PrefetchScalarGridSpec(
+            num_scalar_prefetch=1,
+            grid=(NX,),
+            in_specs=[rows_spec, units_spec, *hidden_specs],
+            out_specs=[
+                pl.BlockSpec((2, SLOTS, 128), lambda i, place: (x_of(i, place), 0, 0)),
+                pl.BlockSpec((8, SLOTS), lambda i, place: (0, 0)),
+            ],
+            scratch_shapes=[pltpu.VMEM((SLOTS, 128), F32)],
+        ),
+        compiler_params=pltpu.CompilerParams(vmem_limit_bytes=LIMIT),
         cost_estimate=pl.CostEstimate(
-            flops=2 * SLOTS * ff * width, bytes_accessed=8000000, transcendentals=0
-        ),
-    )(rows, w_down)
+            flops=2 * SLOTS * ff * width, bytes_accessed=11000000, transcendentals=0
+        ),
+    )(place, rows, w_down, mine, lent)
     hidden_grad = lax.psum_scatter(parts, ("x", "c"), scatter_dimension=0)
     gate_pre_grad, up_pre_grad = call(
         grad_body, [(view, BF), (view, BF)], (hidden_grad, gate_view, up_view), (4 * SLOTS * 128, 3000000)
     )
 
-    (dots,) = call(
-        dots_body,
-        [((8, SLOTS), F32)],
-        (place, parts, *hiddens),
-        (2 * SLOTS * ff, 6000000),
-        (pltpu.VMEM((SLOTS, 128), F32),),
-    )
     back = lax.all_to_all(
         dots[0].reshape(NZ * EXPERTS, CAP), ("z", "y"), split_axis=0, concat_axis=0, tiled=True
     )
@@ -197,13 +202,21 @@
     by_token = jnp.sum(jnp.where(chosen, totals[:, :, None], 0.0), axis=1)
     gate_grad = jnp.sum(jnp.where(named, by_token[None], 0.0), axis=1) / gates_t.astype(F32)
 
-    (w_down_grad,) = call(
+    w_down_grad = pl.pallas_call(
         weight_body,
-        [((ff, width), BF)],
-        (place, rows, *hiddens),
-        (2 * SLOTS * ff * width, 9000000),
-        (pltpu.VMEM((SLOTS, 256), BF),),
-    )
+        out_shape=jax.ShapeDtypeStruct((ff, width), BF),
+        grid_spec=pltpu.PrefetchScalarGridSpec(
+            num_scalar_prefetch=1,
+            grid=(NX,),
+            in_specs=[rows_spec, *hidden_specs],
+            out_specs=units_spec,
+            scratch_shapes=[pltpu.VMEM((SLOTS, 256), BF)],
+        ),
+        compiler_params=pltpu.CompilerParams(vmem_limit_bytes=LIMIT),
+        cost_estimate=pl.CostEstimate(
+            flops=2 * SLOTS * ff * width, bytes_accessed=8000000, transcendentals=0
+        ),
+    )(place, rows, mine, lent)
     flat = (EXPERTS * NZ * CAP, 128)
     return (w_down_grad, gate_pre_grad.reshape(flat), up_pre_grad.reshape(flat), gate_grad.T)
 

time: 139 us -> 136 us (0.978)
  local copies, waits for them, and re-layouts: 9.78 us -> 4.84 us
  Pallas kernels: 15.3 us -> 17.2 us
    pallas_call x1 -> x2, Pallas kernels: 4.25 us -> 15.3 us  [the longest x1 8.25 us: per_device(): pl.pallas_call(product_body, out_shape=[jax.ShapeDtypeStruct((2 * NX, SLO...]
    pallas_call x5 -> x3, Pallas kernels: 11 us -> 1.93 us  [call(): pl.pallas_call(body, out_shape=[jax.ShapeDtypeStruct(s, d) for s, d in ou...]
    unnamed x24 -> x22, local copies, waits for them, and re-layouts: 9.02 us -> 4.71 us
  transfers between devices with their start and end apart: 10 -> 10, of which waited for: 8 -> 8; matrix products, arithmetic and copies ran while one was open for 1% -> 1% of each run, Pallas kernels for 7% -> 5%
where the time goes in v6:
time: 136 us; the launch traced here: 135 us
  blocking collectives  37.3 us (27%)
  starting transfers between devices  36.2 us (27%)
  waiting for transfers between devices  24.3 us (18%)
  Pallas kernels  17.2 us (13%)
  between operations  14.3 us (11%)
  local copies, waits for them, and re-layouts  4.84 us (4%)
    ppermute x3, starting transfers between devices, swap_core(): return lax.ppermute(x, 'c', [(0, 1), (1, 0)])  20.1 us
    all_to_all x1, blocking collectives, per_device(): lax.all_to_all(dots[0].reshape(NZ * EXPERTS, CAP), ('z', 'y'), split_axis...  19.9 us
    all_to_all x1, blocking collectives, per_device(): lax.all_to_all(packed.reshape(EXPERTS, CAP, width), 'y', split_axis=0, co...  17.4 us
    ppermute x5, starting transfers between devices, swap_x(): lax.ppermute(x, ('x', 'c'), [(i * 2 + c, (i ^ masks[c]) * 2 + c) for i in...  16 us
    ppermute x5, waiting for transfers between devices, swap_x(): lax.ppermute(x, ('x', 'c'), [(i * 2 + c, (i ^ masks[c]) * 2 + c) for i in...  10.7 us
    all_gather x1, waiting for transfers between devices, per_device(): rows = lax.all_gather(own, 'z', axis=0, tiled=True)  8.74 us
    pallas_call x1, Pallas kernels, per_device(): pl.pallas_call(product_body, out_shape=[jax.ShapeDtypeStruct((2 * NX, SLO...  8.25 us
    pallas_call x1, Pallas kernels, per_device(): pl.pallas_call(weight_body, out_shape=jax.ShapeDtypeStruct((ff, width), B...  7.05 us
  transfers between devices with their start and end apart: 10, of which 8 were waited for; matrix products, arithmetic and copies ran while one was open for 1% of the time, Pallas kernels for 5%

profile of v6, /device:TPU:1, one launch (start us, length us, event | category | flops | bytes accessed | tf_op | source)
XLA Modules:
  0.0 135.3 jit_solution(7349573912177148885)
XLA Ops:
  7.2 0.9 copy-done.5
  9.9 17.4 %all_to_all.14 = bf16[8,24,768]{2,1,0:T(8,128)(2,1)} all-to-all(bf16[8,24,768]{2,1,0:T(8,128)(2,1)S(1)} %bitcast.40), channel_id=1, replica_groups=mesh['y'=8,'z'=8,'x'=4,'c'=2] {'y'}, dimensions={0} | all-to-all | bytes 589824 | tf_op jit(solution)/shard_map/all_to_all | solution.py:135
  27.6 5.6 %collective-permute-start = (bf16[768,128]{1,0:T(8,128)(2,1)S(1)}, bf16[768,128]{1,0:T(8,128)(2,1)S(1)}, u32[]{:S(2)}, u32[]{:S(2)}) collective-permute-start(bf16[768,128]{1,0:T(8,128)(2,1)S(1)} %dynamic-slice_bitcast_fusion), channel_id=1, source_target_pairs={{0,1},{1,0},{2,3},{3,2},{4,5},{5,4},{6,7},{7,6},{8,9},{9,8},{10,11... | collective-permute-start | bytes 589832 | tf_op jit(solution)/shard_map/ppermute | solution.py:123
  33.3 1.0 collective-permute-done
  34.4 4.4 %collective-permute-start.2 = (bf16[2,768,128]{2,1,0:T(8,128)(2,1)S(1)}, bf16[2,768,128]{2,1,0:T(8,128)(2,1)S(1)}, u32[]{:S(2)}, u32[]{:S(2)}) collective-permute-start(bf16[2,768,128]{2,1,0:T(8,128)(2,1)S(1)} %get-tuple-element.23), channel_id=1, source_target_pairs={{0,2},{1,7},{2,0},{3,5},{4,6},{5,3},{6,4},{7,1},{8,10},{9,15},{10,... | collective-permute-start | bytes 1179656 | tf_op jit(solution)/shard_map/ppermute | solution.py:127
  38.8 1.9 %collective-permute-start.1 = (bf16[2,768,128]{2,1,0:T(8,128)(2,1)S(1)}, bf16[2,768,128]{2,1,0:T(8,128)(2,1)S(1)}, u32[]{:S(2)}, u32[]{:S(2)}) collective-permute-start(bf16[2,768,128]{2,1,0:T(8,128)(2,1)S(1)} %get-tuple-element.23), channel_id=1, source_target_pairs={{0,6},{1,3},{2,4},{3,1},{4,2},{5,7},{6,0},{7,5},{8,14},{9,11},{10,... | collective-permute-start | bytes 1179656 | tf_op jit(solution)/shard_map/ppermute | solution.py:127
  40.7 3.4 %collective-permute-done.2 = bf16[2,768,128]{2,1,0:T(8,128)(2,1)S(1)} collective-permute-done((bf16[2,768,128]{2,1,0:T(8,128)(2,1)S(1)}, bf16[2,768,128]{2,1,0:T(8,128)(2,1)S(1)}, u32[]{:S(2)}, u32[]{:S(2)}) %collective-permute-start.2) | collective-permute-done | bytes 393248 | tf_op jit(solution)/shard_map/ppermute | solution.py:127
  44.1 2.9 %collective-permute-start.3 = (bf16[2,768,128]{2,1,0:T(8,128)(2,1)S(1)}, bf16[2,768,128]{2,1,0:T(8,128)(2,1)S(1)}, u32[]{:S(2)}, u32[]{:S(2)}) collective-permute-start(bf16[2,768,128]{2,1,0:T(8,128)(2,1)S(1)} %collective-permute-done.2), channel_id=1, source_target_pairs={{0,6},{1,3},{2,4},{3,1},{4,2},{5,7},{6,0},{7,5},{8,14},{9,11},{10,... | collective-permute-start | bytes 1179656 | tf_op jit(solution)/shard_map/ppermute | solution.py:127
  47.0 1.3 collective-permute-done.1
  48.4 4.7 %collective-permute-done.3 = bf16[2,768,128]{2,1,0:T(8,128)(2,1)S(1)} collective-permute-done((bf16[2,768,128]{2,1,0:T(8,128)(2,1)S(1)}, bf16[2,768,128]{2,1,0:T(8,128)(2,1)S(1)}, u32[]{:S(2)}, u32[]{:S(2)}) %collective-permute-start.3) | collective-permute-done | bytes 393248 | tf_op jit(solution)/shard_map/ppermute | solution.py:127
  53.3 6.6 %collective-permute-start.4 = (bf16[4,2,768,128]{3,2,1,0:T(8,128)(2,1)S(1)}, bf16[4,2,768,128]{3,2,1,0:T(8,128)(2,1)}, u32[]{:S(2)}, u32[]{:S(2)}) collective-permute-start(bf16[4,2,768,128]{3,2,1,0:T(8,128)(2,1)S(1)} %pad_maximum_fusion.mine), channel_id=1, source_target_pairs={{0,1},{1,0},{2,3},{3,2},{4,5},{5,4},{6,7},{7,6},{8,9},{9,8},{10,11... | collective-permute-start | bytes 4718600 | tf_op jit(solution)/shard_map/ppermute | solution.py:123
  60.0 3.1 %collective-permute-done.4.lent = bf16[4,2,768,128]{3,2,1,0:T(8,128)(2,1)} collective-permute-done((bf16[4,2,768,128]{3,2,1,0:T(8,128)(2,1)S(1)}, bf16[4,2,768,128]{3,2,1,0:T(8,128)(2,1)}, u32[]{:S(2)}, u32[]{:S(2)}) %collective-permute-start.4) | collective-permute-done | bytes 1572896 | tf_op jit(solution)/shard_map/ppermute | solution.py:123
  63.0 8.7 %all-gather.2.cloned.1.call-done.rows = bf16[1536,768]{1,0:T(8,128)(2,1)} async-done(((bf16[192,768]{1,0:T(8,128)(2,1)}), bf16[1536,768]{1,0:T(8,128)(2,1)}) %all-gather.2.cloned.1.call-update) | async-done | bytes 2359312 | tf_op jit(solution)/shard_map/all_gather | solution.py:138
  71.8 1.4 %copy-done.10 = bf16[1024,768]{1,0:T(8,128)(2,1)S(1)} copy-done((bf16[1024,768]{1,0:T(8,128)(2,1)S(1)}, bf16[1024,768]{1,0:T(8,128)(2,1)}, u32[]{:S(2)}) %copy-start.10) | copy-done | bytes 1572888
  73.2 8.3 %shard_map.96 = (bf16[8,1536,128]{2,1,0:T(8,128)(2,1)}, f32[8,1536]{1,0:T(8,128)S(1)}) custom-call(s32[2]{0:T(128)S(1)} %pad_add_fusion.place, bf16[1536,768]{1,0:T(8,128)(2,1)} %all-gather.2.cloned.1.call-done.rows, bf16[1024,768]{1,0:T(8,128)(2,1)S(1)} %copy-done.10, bf16[4,2,768,128]{3,2,1,0:T(8,128)(2,1)} %copy-done, ...), custom_call_target="tpu_custom_call" | custom-call | flops 2415919104 | bytes 11000000 | tf_op jit(solution)/shard_map/pallas_call | solution.py:162
  81.6 19.9 %all_to_all.15 = f32[64,1,24]{2,1,0:T(1,128)S(1)} all-to-all(f32[64,1,24]{2,1,0:T(1,128)S(1)} %bitcast.50), channel_id=1, replica_groups=mesh['y'=8,'z'=8,'x'=4,'c'=2] {'z','y'}, dimensions={0} | all-to-all | bytes 12288 | tf_op jit(solution)/shard_map/all_to_all | solution.py:188
  101.5 7.9 %collective-permute-start.5 = (f32[8,24]{1,0:T(8,128)S(1)}, f32[8,24]{1,0:T(8,128)S(1)}, u32[]{:S(2)}, u32[]{:S(2)}) collective-permute-start(f32[8,24]{1,0:T(8,128)S(1)} %bitcast_reduce_fusion), channel_id=1, source_target_pairs={{0,1},{1,0},{2,3},{3,2},{4,5},{5,4},{6,7},{7,6},{8,9},{9,8},{10,11... | collective-permute-start | bytes 2312 | tf_op jit(solution)/shard_map/ppermute | solution.py:123
  109.4 0.8 collective-permute-done.5
  110.2 4.6 %collective-permute-start.6 = (f32[8,24]{1,0:T(8,128)S(1)}, f32[8,24]{1,0:T(8,128)S(1)}, u32[]{:S(2)}, u32[]{:S(2)}) collective-permute-start(f32[8,24]{1,0:T(8,128)S(1)} %add.21), channel_id=1, source_target_pairs={{0,2},{1,7},{2,0},{3,5},{4,6},{5,3},{6,4},{7,1},{8,10},{9,15},{10,... | collective-permute-start | bytes 2312 | tf_op jit(solution)/shard_map/ppermute | solution.py:127
  114.9 1.3 collective-permute-done.6
  116.1 2.2 %collective-permute-start.7 = (f32[8,24]{1,0:T(8,128)S(1)}, f32[8,24]{1,0:T(8,128)S(1)}, u32[]{:S(2)}, u32[]{:S(2)}) collective-permute-start(f32[8,24]{1,0:T(8,128)S(1)} %add.22), channel_id=1, source_target_pairs={{0,6},{1,3},{2,4},{3,1},{4,2},{5,7},{6,0},{7,5},{8,14},{9,11},{10,... | collective-permute-start | bytes 2312 | tf_op jit(solution)/shard_map/ppermute | solution.py:127
  118.4 7.0 %shard_map.95 = bf16[1024,768]{1,0:T(8,128)(2,1)} custom-call(s32[2]{0:T(128)S(1)} %pad_add_fusion.place, bf16[1536,768]{1,0:T(8,128)(2,1)} %all-gather.2.cloned.1.call-done.rows, bf16[4,2,768,128]{3,2,1,0:T(8,128)(2,1)S(1)} %copy-done.1, bf16[4,2,768,128]{3,2,1,0:T(8,128)(2,1)} %collective-permute-done.4.lent), custom_call_target="tpu_custom_call" | custom-call | flops 2415919104 | bytes 8000000 | tf_op jit(solution)/shard_map/pallas_call | solution.py:205
  126.2 1.0 copy-done.4
  127.1 1.3 shard_map.97
  (43 shorter events, 3.4 us)
Async XLA Ops:
  7.2 20.1 %copy-start.2 = (bf16[1536,128]{1,0:T(8,128)(2,1)S(1)}, bf16[1536,128]{1,0:T(8,128)(2,1)}, u32[]{:S(2)}) copy-start(bf16[1536,128]{1,0:T(8,128)(2,1)} %param.10) | copy-start | bytes 1179652
  7.2 20.1 %copy-start.3 = (bf16[1536,128]{1,0:T(8,128)(2,1)S(1)}, bf16[1536,128]{1,0:T(8,128)(2,1)}, u32[]{:S(2)}) copy-start(bf16[1536,128]{1,0:T(8,128)(2,1)} %param.11) | copy-start | bytes 1179652
  7.2 64.6 %all-gather.2.cloned.1.call-start = ((), (), s32[]{:S(2)}) async-start(), calls=%async_computation.3 | async-start | bytes 2654208 | tf_op jit(solution)/shard_map/all_gather | solution.py:138
  7.2 1.0 copy-start.5
  8.2 0.7 copy-start.6
  8.9 0.7 copy-start.8
  27.2 98.9 %reduce-scatter.2.cloned.1.call-start = ((), (), s32[]{:S(2)}) async-start(), calls=%async_computation.4 | async-start | bytes 3538944 | tf_op jit(solution)/shard_map/reduce_scatter | solution.py:183
  27.6 6.7 %collective-permute-start = (bf16[768,128]{1,0:T(8,128)(2,1)S(1)}, bf16[768,128]{1,0:T(8,128)(2,1)S(1)}, u32[]{:S(2)}, u32[]{:S(2)}) collective-permute-start(bf16[768,128]{1,0:T(8,128)(2,1)S(1)} %dynamic-slice_bitcast_fusion), channel_id=1, source_target_pairs={{0,1},{1,0},{2,3},{3,2},{4,5},{5,4},{6,7},{7,6},{8,9},{9,8},{10,11... | collective-permute-start | bytes 589832 | tf_op jit(solution)/shard_map/ppermute | solution.py:123
  34.4 9.7 %collective-permute-start.2 = (bf16[2,768,128]{2,1,0:T(8,128)(2,1)S(1)}, bf16[2,768,128]{2,1,0:T(8,128)(2,1)S(1)}, u32[]{:S(2)}, u32[]{:S(2)}) collective-permute-start(bf16[2,768,128]{2,1,0:T(8,128)(2,1)S(1)} %get-tuple-element.23), channel_id=1, source_target_pairs={{0,2},{1,7},{2,0},{3,5},{4,6},{5,3},{6,4},{7,1},{8,10},{9,15},{10,... | collective-permute-start | bytes 1179656 | tf_op jit(solution)/shard_map/ppermute | solution.py:127
  38.8 9.6 %collective-permute-start.1 = (bf16[2,768,128]{2,1,0:T(8,128)(2,1)S(1)}, bf16[2,768,128]{2,1,0:T(8,128)(2,1)S(1)}, u32[]{:S(2)}, u32[]{:S(2)}) collective-permute-start(bf16[2,768,128]{2,1,0:T(8,128)(2,1)S(1)} %get-tuple-element.23), channel_id=1, source_target_pairs={{0,6},{1,3},{2,4},{3,1},{4,2},{5,7},{6,0},{7,5},{8,14},{9,11},{10,... | collective-permute-start | bytes 1179656 | tf_op jit(solution)/shard_map/ppermute | solution.py:127
  44.1 8.9 %collective-permute-start.3 = (bf16[2,768,128]{2,1,0:T(8,128)(2,1)S(1)}, bf16[2,768,128]{2,1,0:T(8,128)(2,1)S(1)}, u32[]{:S(2)}, u32[]{:S(2)}) collective-permute-start(bf16[2,768,128]{2,1,0:T(8,128)(2,1)S(1)} %collective-permute-done.2), channel_id=1, source_target_pairs={{0,6},{1,3},{2,4},{3,1},{4,2},{5,7},{6,0},{7,5},{8,14},{9,11},{10,... | collective-permute-start | bytes 1179656 | tf_op jit(solution)/shard_map/ppermute | solution.py:127
  53.2 18.5 %copy-start = (bf16[4,2,768,128]{3,2,1,0:T(8,128)(2,1)}, bf16[4,2,768,128]{3,2,1,0:T(8,128)(2,1)S(1)}, u32[]{:S(2)}) copy-start(bf16[4,2,768,128]{3,2,1,0:T(8,128)(2,1)S(1)} %pad_maximum_fusion.mine) | copy-start | bytes 4718596
  53.3 9.8 %collective-permute-start.4 = (bf16[4,2,768,128]{3,2,1,0:T(8,128)(2,1)S(1)}, bf16[4,2,768,128]{3,2,1,0:T(8,128)(2,1)}, u32[]{:S(2)}, u32[]{:S(2)}) collective-permute-start(bf16[4,2,768,128]{3,2,1,0:T(8,128)(2,1)S(1)} %pad_maximum_fusion.mine), channel_id=1, source_target_pairs={{0,1},{1,0},{2,3},{3,2},{4,5},{5,4},{6,7},{7,6},{8,9},{9,8},{10,11... | collective-permute-start | bytes 4718600 | tf_op jit(solution)/shard_map/ppermute | solution.py:123
  71.8 1.4 %copy-start.10 = (bf16[1024,768]{1,0:T(8,128)(2,1)S(1)}, bf16[1024,768]{1,0:T(8,128)(2,1)}, u32[]{:S(2)}) copy-start(bf16[1024,768]{1,0:T(8,128)(2,1)} %w.1) | copy-start | bytes 4718596
  81.4 27.9 %copy-start.7 = (s32[64,2]{0,1:T(2,128)S(1)}, s32[64,2]{0,1:T(2,128)}, u32[]{:S(2)}) copy-start(s32[64,2]{0,1:T(2,128)} %param.7) | copy-start | bytes 1540
  81.4 36.9 %copy-start.1 = (bf16[4,2,768,128]{3,2,1,0:T(8,128)(2,1)S(1)}, bf16[4,2,768,128]{3,2,1,0:T(8,128)(2,1)}, u32[]{:S(2)}) copy-start(bf16[4,2,768,128]{3,2,1,0:T(8,128)(2,1)} %copy-done) | copy-start | bytes 4718596
  101.5 8.7 %collective-permute-start.5 = (f32[8,24]{1,0:T(8,128)S(1)}, f32[8,24]{1,0:T(8,128)S(1)}, u32[]{:S(2)}, u32[]{:S(2)}) collective-permute-start(f32[8,24]{1,0:T(8,128)S(1)} %bitcast_reduce_fusion), channel_id=1, source_target_pairs={{0,1},{1,0},{2,3},{3,2},{4,5},{5,4},{6,7},{7,6},{8,9},{9,8},{10,11... | collective-permute-start | bytes 2312 | tf_op jit(solution)/shard_map/ppermute | solution.py:123
  110.2 6.0 %collective-permute-start.6 = (f32[8,24]{1,0:T(8,128)S(1)}, f32[8,24]{1,0:T(8,128)S(1)}, u32[]{:S(2)}, u32[]{:S(2)}) collective-permute-start(f32[8,24]{1,0:T(8,128)S(1)} %add.21), channel_id=1, source_target_pairs={{0,2},{1,7},{2,0},{3,5},{4,6},{5,3},{6,4},{7,1},{8,10},{9,15},{10,... | collective-permute-start | bytes 2312 | tf_op jit(solution)/shard_map/ppermute | solution.py:127
  116.1 9.4 %copy-start.9 = (bf16[64,2]{0,1:T(2,128)(2,1)S(1)}, bf16[64,2]{0,1:T(2,128)(2,1)}, u32[]{:S(2)}) copy-start(bf16[64,2]{0,1:T(2,128)(2,1)} %param.8) | copy-start | bytes 772
  116.1 9.3 %collective-permute-start.7 = (f32[8,24]{1,0:T(8,128)S(1)}, f32[8,24]{1,0:T(8,128)S(1)}, u32[]{:S(2)}, u32[]{:S(2)}) collective-permute-start(f32[8,24]{1,0:T(8,128)S(1)} %add.22), channel_id=1, source_target_pairs={{0,6},{1,3},{2,4},{3,1},{4,2},{5,7},{6,0},{7,5},{8,14},{9,11},{10,... | collective-permute-start | bytes 2312 | tf_op jit(solution)/shard_map/ppermute | solution.py:127
  126.1 1.0 copy-start.4
Sparse Core Ops, SparseCore 0:
  27.4 44.3 all-gather.1
  81.6 40.8 reduce-scatter.1

commit v7 on v6

--- a/solution.py
+++ b/solution.py
@@ -16,7 +16,11 @@
 BF = jnp.bfloat16
 F32 = jnp.float32
 LIMIT = 52 * 2**20
+STREAM_LIMIT = 56 * 2**20
 WHOLE = pl.BlockSpec()
+SCALARS = pl.BlockSpec(memory_space=pltpu.SMEM)
+LOCAL = pl.BlockSpec(memory_space=pltpu.VMEM)
+REMOTE = pl.BlockSpec(memory_space=pl.ANY)
 CHUNK = SLOTS // 4
 
 
@@ -63,45 +67,92 @@
 
 
 def x_of(label, place):
-    mask = jnp.where(label == 1, 3 - 2 * place[1], jnp.where(label == 2, 1 + 2 * place[1], label - label // 3))
-    return place[0] ^ mask
-
-
-def swapped(label):
-    return jnp.where(label == 1, 2, jnp.where(label == 2, 1, label))
-
-
-def product_body(place, rows, w, mine, lent, parts, dots, total):
-    label = pl.program_id(0)
-
-    @pl.when(label == 0)
-    def _():
-        total[...] = jnp.zeros_like(total)
-
+    return place[0] ^ (0, 3 - 2 * place[1], 1 + 2 * place[1], 2)[label]
+
+
+def hidden_of(place, mine, lent, label, half, i, at):
+    return jnp.where(place[1] == half, mine[label, i, at, :], lent[OTHERS[label], i, at, :])
+
+
+OTHERS = (0, 2, 1, 3)
+
+
+def fetch(source, target, sems, size):
+    copies = []
+    for k in range(4):
+        at = pl.ds(k * size, size)
+        copies.append(pltpu.make_async_copy(source.at[at], target.at[at], sems.at[k]))
+        copies[-1].start()
+    return copies
+
+
+def product_body(
+    place, rows_in, w_in, mine_in, lent_in, parts_out, dots, rows, w, mine, lent, parts,
+    in_sems, w_sems, mine_sems, lent_sems, out_sems,
+):
+    arriving = fetch(rows_in, rows, in_sems, CHUNK)
+    units = fetch(w_in, w, w_sems, w.shape[0] // 4)
+    ours = fetch(mine_in, mine, mine_sems, 1)
+    coming = fetch(lent_in, lent, lent_sems, 1)
+    for copy in units:
+        copy.wait()
+    leaving = []
     for k in range(4):
         at = pl.ds(k * CHUNK, CHUNK)
-        part = dot(rows[at, :], w[...], 1, 1)
         here = pl.ds(k % 2 * CHUNK, CHUNK)
-        for i in range(2):
-            unit = part[:, i * 128 : i * 128 + 128]
-            parts[i, at, :] = unit.astype(BF)
-            hidden = jnp.where(place[1] == k // 2, mine[0, i, here, :], lent[0, i, here, :])
-            total[at, :] += unit * hidden.astype(F32)
-
-    @pl.when(label == NX - 1)
-    def _():
-        dots[...] = lax.dot_general(
-            jnp.ones((8, 128), F32), total[...], (((1,), (1,)), ((), ())),
+        arriving[k].wait()
+        total = None
+        for label in range(NX):
+            x = x_of(label, place)
+            part = dot(rows[at, :], w[pl.ds(pl.multiple_of(x * 256, 256), 256), :], 1, 1)
+            if k == 0:
+                ours[label].wait()
+                coming[OTHERS[label]].wait()
+            for i in range(2):
+                unit = part[:, i * 128 : i * 128 + 128]
+                slot = 2 * label + i
+                parts[slot, at, :] = unit.astype(BF)
+                copy = pltpu.make_async_copy(
+                    parts.at[slot, at], parts_out.at[2 * x + i, at], out_sems.at[k, slot]
+                )
+                copy.start()
+                leaving.append(copy)
+                term = unit * hidden_of(place, mine, lent, label, k // 2, i, here).astype(F32)
+                total = term if total is None else total + term
+        dots[:, at] = lax.dot_general(
+            jnp.ones((8, 128), F32), total, (((1,), (1,)), ((), ())),
             precision=lax.Precision.HIGHEST, preferred_element_type=F32,
         )
-
-
-def weight_body(place, rows, mine, lent, out, units):
-    for half in range(2):
-        for i in range(2):
-            hidden = jnp.where(place[1] == half, mine[0, i], lent[0, i])
-            units[pl.ds(half * PART, PART), pl.ds(i * 128, 128)] = hidden
-    out[...] = dot(units[...], rows[...], 0, 0).astype(BF)
+    for copy in leaving:
+        copy.wait()
+
+
+def weight_body(
+    place, rows_in, mine_in, lent_in, out, rows, mine, lent, units, blocks,
+    in_sems, mine_sems, lent_sems, out_sems,
+):
+    ours = fetch(mine_in, mine, mine_sems, 1)
+    coming = fetch(lent_in, lent, lent_sems, 1)
+    arriving = fetch(rows_in, rows, in_sems, CHUNK)
+    leaving = []
+    whole = pl.ds(0, PART)
+    for label in range(NX):
+        ours[label].wait()
+        coming[OTHERS[label]].wait()
+        for half in range(2):
+            for i in range(2):
+                units[label % 2, pl.ds(half * PART, PART), pl.ds(i * 128, 128)] = hidden_of(
+                    place, mine, lent, label, half, i, whole
+                )
+        if label == 0:
+            for copy in arriving:
+                copy.wait()
+        blocks[label] = dot(units[label % 2], rows[...], 0, 0).astype(BF)
+        at = pl.ds(pl.multiple_of(x_of(label, place) * 256, 256), 256)
+        leaving.append(pltpu.make_async_copy(blocks.at[label], out.at[at], out_sems.at[label]))
+        leaving[-1].start()
+    for copy in leaving:
+        copy.wait()
 
 
 def grad_body(hidden_grad, gate, up, gate_out, up_out):
@@ -153,29 +204,27 @@
     lent = swap_core(mine)
     rows, lent = lax.optimization_barrier((rows, lent))
 
-    hidden_specs = [
-        pl.BlockSpec((1, 2, PART, 128), lambda i, place: (i, 0, 0, 0)),
-        pl.BlockSpec((1, 2, PART, 128), lambda i, place: (swapped(i), 0, 0, 0)),
-    ]
-    rows_spec = pl.BlockSpec((SLOTS, width), lambda i, place: (0, 0))
-    units_spec = pl.BlockSpec((ff // NX, width), lambda i, place: (x_of(i, place), 0))
     parts, dots = pl.pallas_call(
         product_body,
         out_shape=[
             jax.ShapeDtypeStruct((2 * NX, SLOTS, 128), BF),
             jax.ShapeDtypeStruct((8, SLOTS), F32),
         ],
-        grid_spec=pltpu.PrefetchScalarGridSpec(
-            num_scalar_prefetch=1,
-            grid=(NX,),
-            in_specs=[rows_spec, units_spec, *hidden_specs],
-            out_specs=[
-                pl.BlockSpec((2, SLOTS, 128), lambda i, place: (x_of(i, place), 0, 0)),
-                pl.BlockSpec((8, SLOTS), lambda i, place: (0, 0)),
-            ],
-            scratch_shapes=[pltpu.VMEM((SLOTS, 128), F32)],
-        ),
-        compiler_params=pltpu.CompilerParams(vmem_limit_bytes=LIMIT),
+        in_specs=[SCALARS, REMOTE, REMOTE, REMOTE, REMOTE],
+        out_specs=[REMOTE, LOCAL],
+        scratch_shapes=[
+            pltpu.VMEM((SLOTS, width), BF),
+            pltpu.VMEM((ff, width), BF),
+            pltpu.VMEM((NX, 2, PART, 128), BF),
+            pltpu.VMEM((NX, 2, PART, 128), BF),
+            pltpu.VMEM((2 * NX, SLOTS, 128), BF),
+            pltpu.SemaphoreType.DMA((4,)),
+            pltpu.SemaphoreType.DMA((4,)),
+            pltpu.SemaphoreType.DMA((4,)),
+            pltpu.SemaphoreType.DMA((4,)),
+            pltpu.SemaphoreType.DMA((4, 2 * NX)),
+        ],
+        compiler_params=pltpu.CompilerParams(vmem_limit_bytes=STREAM_LIMIT),
         cost_estimate=pl.CostEstimate(
             flops=2 * SLOTS * ff * width, bytes_accessed=11000000, transcendentals=0
         ),
@@ -205,14 +254,20 @@
     w_down_grad = pl.pallas_call(
         weight_body,
         out_shape=jax.ShapeDtypeStruct((ff, width), BF),
-        grid_spec=pltpu.PrefetchScalarGridSpec(
-            num_scalar_prefetch=1,
-            grid=(NX,),
-            in_specs=[rows_spec, *hidden_specs],
-            out_specs=units_spec,
-            scratch_shapes=[pltpu.VMEM((SLOTS, 256), BF)],
-        ),
-        compiler_params=pltpu.CompilerParams(vmem_limit_bytes=LIMIT),
+        in_specs=[SCALARS, REMOTE, REMOTE, REMOTE],
+        out_specs=REMOTE,
+        scratch_shapes=[
+            pltpu.VMEM((SLOTS, width), BF),
+            pltpu.VMEM((NX, 2, PART, 128), BF),
+            pltpu.VMEM((NX, 2, PART, 128), BF),
+            pltpu.VMEM((2, SLOTS, 256), BF),
+            pltpu.VMEM((NX, 256, width), BF),
+            pltpu.SemaphoreType.DMA((4,)),
+            pltpu.SemaphoreType.DMA((4,)),
+            pltpu.SemaphoreType.DMA((4,)),
+            pltpu.SemaphoreType.DMA((NX,)),
+        ],
+        compiler_params=pltpu.CompilerParams(vmem_limit_bytes=STREAM_LIMIT),
         cost_estimate=pl.CostEstimate(
             flops=2 * SLOTS * ff * width, bytes_accessed=8000000, transcendentals=0
         ),

time: 136 us -> 139 us (1.022)
  Pallas kernels: 17.2 us -> 21.4 us
    pallas_call x1, Pallas kernels: 8.25 us -> 11 us  [per_device(): pl.pallas_call(product_body, out_shape=[jax.ShapeDtypeStruct((2 * NX, SLO...]
    unnamed x22 -> x18, local copies, waits for them, and re-layouts: 4.71 us -> 3.3 us
  transfers between devices with their start and end apart: 10 -> 10, of which waited for: 8 -> 8; matrix products, arithmetic and copies ran while one was open for 1% -> 2% of each run, Pallas kernels for 5% -> 6%
where the time goes in v7:
time: 139 us
  blocking collectives  37.1 us (27%)
  starting transfers between devices  36.2 us (26%)
  waiting for transfers between devices  23.9 us (17%)
  Pallas kernels  21.4 us (15%)
  between operations  14.3 us (10%)
  local copies, waits for them, and re-layouts  4.22 us (3%)
  other arithmetic  1.59 us (1%)
    ppermute x3, starting transfers between devices, swap_core(): return lax.ppermute(x, 'c', [(0, 1), (1, 0)])  20.1 us
    all_to_all x1, blocking collectives, per_device(): lax.all_to_all(dots[0].reshape(NZ * EXPERTS, CAP), ('z', 'y'), split_axis...  19.8 us
    all_to_all x1, blocking collectives, per_device(): lax.all_to_all(packed.reshape(EXPERTS, CAP, width), 'y', split_axis=0, co...  17.4 us
    ppermute x5, starting transfers between devices, swap_x(): lax.ppermute(x, ('x', 'c'), [(i * 2 + c, (i ^ masks[c]) * 2 + c) for i in...  16 us
    pallas_call x1, Pallas kernels, per_device(): pl.pallas_call(product_body, out_shape=[jax.ShapeDtypeStruct((2 * NX, SLO...  11 us
    ppermute x5, waiting for transfers between devices, swap_x(): lax.ppermute(x, ('x', 'c'), [(i * 2 + c, (i ^ masks[c]) * 2 + c) for i in...  10.7 us
    all_gather x1, waiting for transfers between devices, per_device(): rows = lax.all_gather(own, 'z', axis=0, tiled=True)  8.74 us
    pallas_call x1, Pallas kernels, per_device(): pl.pallas_call(weight_body, out_shape=jax.ShapeDtypeStruct((ff, width), B...  8.41 us
  transfers between devices with their start and end apart: 10, of which 8 were waited for; matrix products, arithmetic and copies ran while one was open for 2% of the time, Pallas kernels for 6%

profile of v7, /device:TPU:1, one launch (start us, length us, event | category | flops | bytes accessed | tf_op | source)
XLA Modules:
  0.0 138.7 jit_solution(16843439744584261618)
XLA Ops:
  7.2 0.9 copy-done.3
  9.9 17.4 %all_to_all.14 = bf16[8,24,768]{2,1,0:T(8,128)(2,1)} all-to-all(bf16[8,24,768]{2,1,0:T(8,128)(2,1)S(1)} %bitcast.40), channel_id=1, replica_groups=mesh['y'=8,'z'=8,'x'=4,'c'=2] {'y'}, dimensions={0} | all-to-all | bytes 589824 | tf_op jit(solution)/shard_map/all_to_all | solution.py:186
  27.6 5.6 %collective-permute-start = (bf16[768,128]{1,0:T(8,128)(2,1)S(1)}, bf16[768,128]{1,0:T(8,128)(2,1)S(1)}, u32[]{:S(2)}, u32[]{:S(2)}) collective-permute-start(bf16[768,128]{1,0:T(8,128)(2,1)S(1)} %dynamic-slice_bitcast_fusion), channel_id=1, source_target_pairs={{0,1},{1,0},{2,3},{3,2},{4,5},{5,4},{6,7},{7,6},{8,9},{9,8},{10,11... | collective-permute-start | bytes 589832 | tf_op jit(solution)/shard_map/ppermute | solution.py:174
  33.3 1.0 collective-permute-done
  34.4 4.4 %collective-permute-start.2 = (bf16[2,768,128]{2,1,0:T(8,128)(2,1)S(1)}, bf16[2,768,128]{2,1,0:T(8,128)(2,1)S(1)}, u32[]{:S(2)}, u32[]{:S(2)}) collective-permute-start(bf16[2,768,128]{2,1,0:T(8,128)(2,1)S(1)} %get-tuple-element.23), channel_id=1, source_target_pairs={{0,2},{1,7},{2,0},{3,5},{4,6},{5,3},{6,4},{7,1},{8,10},{9,15},{10,... | collective-permute-start | bytes 1179656 | tf_op jit(solution)/shard_map/ppermute | solution.py:178
  38.8 1.9 %collective-permute-start.1 = (bf16[2,768,128]{2,1,0:T(8,128)(2,1)S(1)}, bf16[2,768,128]{2,1,0:T(8,128)(2,1)S(1)}, u32[]{:S(2)}, u32[]{:S(2)}) collective-permute-start(bf16[2,768,128]{2,1,0:T(8,128)(2,1)S(1)} %get-tuple-element.23), channel_id=1, source_target_pairs={{0,6},{1,3},{2,4},{3,1},{4,2},{5,7},{6,0},{7,5},{8,14},{9,11},{10,... | collective-permute-start | bytes 1179656 | tf_op jit(solution)/shard_map/ppermute | solution.py:178
  40.7 3.4 %collective-permute-done.2 = bf16[2,768,128]{2,1,0:T(8,128)(2,1)S(1)} collective-permute-done((bf16[2,768,128]{2,1,0:T(8,128)(2,1)S(1)}, bf16[2,768,128]{2,1,0:T(8,128)(2,1)S(1)}, u32[]{:S(2)}, u32[]{:S(2)}) %collective-permute-start.2) | collective-permute-done | bytes 393248 | tf_op jit(solution)/shard_map/ppermute | solution.py:178
  44.1 2.9 %collective-permute-start.3 = (bf16[2,768,128]{2,1,0:T(8,128)(2,1)S(1)}, bf16[2,768,128]{2,1,0:T(8,128)(2,1)S(1)}, u32[]{:S(2)}, u32[]{:S(2)}) collective-permute-start(bf16[2,768,128]{2,1,0:T(8,128)(2,1)S(1)} %collective-permute-done.2), channel_id=1, source_target_pairs={{0,6},{1,3},{2,4},{3,1},{4,2},{5,7},{6,0},{7,5},{8,14},{9,11},{10,... | collective-permute-start | bytes 1179656 | tf_op jit(solution)/shard_map/ppermute | solution.py:178
  47.0 1.3 collective-permute-done.1
  48.4 4.7 %collective-permute-done.3 = bf16[2,768,128]{2,1,0:T(8,128)(2,1)S(1)} collective-permute-done((bf16[2,768,128]{2,1,0:T(8,128)(2,1)S(1)}, bf16[2,768,128]{2,1,0:T(8,128)(2,1)S(1)}, u32[]{:S(2)}, u32[]{:S(2)}) %collective-permute-start.3) | collective-permute-done | bytes 393248 | tf_op jit(solution)/shard_map/ppermute | solution.py:178
  53.3 6.6 %collective-permute-start.4 = (bf16[4,2,768,128]{3,2,1,0:T(8,128)(2,1)S(1)}, bf16[4,2,768,128]{3,2,1,0:T(8,128)(2,1)}, u32[]{:S(2)}, u32[]{:S(2)}) collective-permute-start(bf16[4,2,768,128]{3,2,1,0:T(8,128)(2,1)S(1)} %pad_maximum_fusion.mine_in), channel_id=1, source_target_pairs={{0,1},{1,0},{2,3},{3,2},{4,5},{5,4},{6,7},{7,6},{8,9},{9,8},{10,11... | collective-permute-start | bytes 4718600 | tf_op jit(solution)/shard_map/ppermute | solution.py:174
  60.5 2.6 %collective-permute-done.4.lent_in = bf16[4,2,768,128]{3,2,1,0:T(8,128)(2,1)} collective-permute-done((bf16[4,2,768,128]{3,2,1,0:T(8,128)(2,1)S(1)}, bf16[4,2,768,128]{3,2,1,0:T(8,128)(2,1)}, u32[]{:S(2)}, u32[]{:S(2)}) %collective-permute-start.4) | collective-permute-done | bytes 1572896 | tf_op jit(solution)/shard_map/ppermute | solution.py:174
  63.0 8.7 %all-gather.2.cloned.1.call-done.rows_in = bf16[1536,768]{1,0:T(8,128)(2,1)} async-done(((bf16[192,768]{1,0:T(8,128)(2,1)}), bf16[1536,768]{1,0:T(8,128)(2,1)}) %all-gather.2.cloned.1.call-update) | async-done | bytes 2359312 | tf_op jit(solution)/shard_map/all_gather | solution.py:189
  71.8 11.0 %shard_map.96 = (bf16[8,1536,128]{2,1,0:T(8,128)(2,1)}, f32[8,1536]{1,0:T(8,128)}) custom-call(s32[2]{0:T(128)} %pad_add_fusion.place, bf16[1536,768]{1,0:T(8,128)(2,1)} %all-gather.2.cloned.1.call-done.rows_in, bf16[1024,768]{1,0:T(8,128)(2,1)} %w_in.1, bf16[4,2,768,128]{3,2,1,0:T(8,128)(2,1)} %copy-done.8, ...), custom_call_target="tpu_custom_call" | custom-call | flops 2415919104 | bytes 11000000 | tf_op jit(solution)/shard_map/pallas_call | solution.py:207
  82.8 0.8 slice_reduce_fusion
  83.7 19.8 %all_to_all.15 = f32[64,1,24]{2,1,0:T(1,128)S(1)} all-to-all(f32[64,1,24]{2,1,0:T(1,128)S(1)} %bitcast.50), channel_id=1, replica_groups=mesh['y'=8,'z'=8,'x'=4,'c'=2] {'z','y'}, dimensions={0} | all-to-all | bytes 12288 | tf_op jit(solution)/shard_map/all_to_all | solution.py:237
  103.5 7.9 %collective-permute-start.5 = (f32[8,24]{1,0:T(8,128)S(1)}, f32[8,24]{1,0:T(8,128)S(1)}, u32[]{:S(2)}, u32[]{:S(2)}) collective-permute-start(f32[8,24]{1,0:T(8,128)S(1)} %bitcast_reduce_fusion), channel_id=1, source_target_pairs={{0,1},{1,0},{2,3},{3,2},{4,5},{5,4},{6,7},{7,6},{8,9},{9,8},{10,11... | collective-permute-start | bytes 2312 | tf_op jit(solution)/shard_map/ppermute | solution.py:174
  111.4 0.8 collective-permute-done.5
  112.2 4.5 %collective-permute-start.6 = (f32[8,24]{1,0:T(8,128)S(1)}, f32[8,24]{1,0:T(8,128)S(1)}, u32[]{:S(2)}, u32[]{:S(2)}) collective-permute-start(f32[8,24]{1,0:T(8,128)S(1)} %add.21), channel_id=1, source_target_pairs={{0,2},{1,7},{2,0},{3,5},{4,6},{5,3},{6,4},{7,1},{8,10},{9,15},{10,... | collective-permute-start | bytes 2312 | tf_op jit(solution)/shard_map/ppermute | solution.py:178
  116.9 1.3 collective-permute-done.6
  118.2 2.2 %collective-permute-start.7 = (f32[8,24]{1,0:T(8,128)S(1)}, f32[8,24]{1,0:T(8,128)S(1)}, u32[]{:S(2)}, u32[]{:S(2)}) collective-permute-start(f32[8,24]{1,0:T(8,128)S(1)} %add.22), channel_id=1, source_target_pairs={{0,6},{1,3},{2,4},{3,1},{4,2},{5,7},{6,0},{7,5},{8,14},{9,11},{10,... | collective-permute-start | bytes 2312 | tf_op jit(solution)/shard_map/ppermute | solution.py:178
  120.4 8.4 %shard_map.95 = bf16[1024,768]{1,0:T(8,128)(2,1)} custom-call(s32[2]{0:T(128)} %pad_add_fusion.place, bf16[1536,768]{1,0:T(8,128)(2,1)} %all-gather.2.cloned.1.call-done.rows_in, bf16[4,2,768,128]{3,2,1,0:T(8,128)(2,1)} %copy-done.8, bf16[4,2,768,128]{3,2,1,0:T(8,128)(2,1)} %collective-permute-done.4.lent_in), custom_call_target="tpu_custom_call" | custom-call | flops 2415919104 | bytes 8000000 | tf_op jit(solution)/shard_map/pallas_call | solution.py:254
  129.6 1.0 copy-done.2
  130.6 1.3 shard_map.97
  (39 shorter events, 3.9 us)
Async XLA Ops:
  7.2 20.1 %copy-start = (bf16[1536,128]{1,0:T(8,128)(2,1)S(1)}, bf16[1536,128]{1,0:T(8,128)(2,1)}, u32[]{:S(2)}) copy-start(bf16[1536,128]{1,0:T(8,128)(2,1)} %param.10) | copy-start | bytes 1179652
  7.2 20.1 %copy-start.1 = (bf16[1536,128]{1,0:T(8,128)(2,1)S(1)}, bf16[1536,128]{1,0:T(8,128)(2,1)}, u32[]{:S(2)}) copy-start(bf16[1536,128]{1,0:T(8,128)(2,1)} %param.11) | copy-start | bytes 1179652
  7.2 64.6 %all-gather.2.cloned.1.call-start = ((), (), s32[]{:S(2)}) async-start(), calls=%async_computation.3 | async-start | bytes 2654208 | tf_op jit(solution)/shard_map/all_gather | solution.py:189
  7.2 1.0 copy-start.3
  8.2 0.7 copy-start.4
  8.9 0.7 copy-start.6
  27.2 102.3 %reduce-scatter.2.cloned.1.call-start = ((), (), s32[]{:S(2)}) async-start(), calls=%async_computation.4 | async-start | bytes 3538944 | tf_op jit(solution)/shard_map/reduce_scatter | solution.py:232
  27.6 6.7 %collective-permute-start = (bf16[768,128]{1,0:T(8,128)(2,1)S(1)}, bf16[768,128]{1,0:T(8,128)(2,1)S(1)}, u32[]{:S(2)}, u32[]{:S(2)}) collective-permute-start(bf16[768,128]{1,0:T(8,128)(2,1)S(1)} %dynamic-slice_bitcast_fusion), channel_id=1, source_target_pairs={{0,1},{1,0},{2,3},{3,2},{4,5},{5,4},{6,7},{7,6},{8,9},{9,8},{10,11... | collective-permute-start | bytes 589832 | tf_op jit(solution)/shard_map/ppermute | solution.py:174
  34.4 9.7 %collective-permute-start.2 = (bf16[2,768,128]{2,1,0:T(8,128)(2,1)S(1)}, bf16[2,768,128]{2,1,0:T(8,128)(2,1)S(1)}, u32[]{:S(2)}, u32[]{:S(2)}) collective-permute-start(bf16[2,768,128]{2,1,0:T(8,128)(2,1)S(1)} %get-tuple-element.23), channel_id=1, source_target_pairs={{0,2},{1,7},{2,0},{3,5},{4,6},{5,3},{6,4},{7,1},{8,10},{9,15},{10,... | collective-permute-start | bytes 1179656 | tf_op jit(solution)/shard_map/ppermute | solution.py:178
  38.8 9.6 %collective-permute-start.1 = (bf16[2,768,128]{2,1,0:T(8,128)(2,1)S(1)}, bf16[2,768,128]{2,1,0:T(8,128)(2,1)S(1)}, u32[]{:S(2)}, u32[]{:S(2)}) collective-permute-start(bf16[2,768,128]{2,1,0:T(8,128)(2,1)S(1)} %get-tuple-element.23), channel_id=1, source_target_pairs={{0,6},{1,3},{2,4},{3,1},{4,2},{5,7},{6,0},{7,5},{8,14},{9,11},{10,... | collective-permute-start | bytes 1179656 | tf_op jit(solution)/shard_map/ppermute | solution.py:178
  44.1 8.9 %collective-permute-start.3 = (bf16[2,768,128]{2,1,0:T(8,128)(2,1)S(1)}, bf16[2,768,128]{2,1,0:T(8,128)(2,1)S(1)}, u32[]{:S(2)}, u32[]{:S(2)}) collective-permute-start(bf16[2,768,128]{2,1,0:T(8,128)(2,1)S(1)} %collective-permute-done.2), channel_id=1, source_target_pairs={{0,6},{1,3},{2,4},{3,1},{4,2},{5,7},{6,0},{7,5},{8,14},{9,11},{10,... | collective-permute-start | bytes 1179656 | tf_op jit(solution)/shard_map/ppermute | solution.py:178
  53.2 18.5 %copy-start.8 = (bf16[4,2,768,128]{3,2,1,0:T(8,128)(2,1)}, bf16[4,2,768,128]{3,2,1,0:T(8,128)(2,1)S(1)}, u32[]{:S(2)}) copy-start(bf16[4,2,768,128]{3,2,1,0:T(8,128)(2,1)S(1)} %pad_maximum_fusion.mine_in) | copy-start | bytes 4718596
  53.3 9.8 %collective-permute-start.4 = (bf16[4,2,768,128]{3,2,1,0:T(8,128)(2,1)S(1)}, bf16[4,2,768,128]{3,2,1,0:T(8,128)(2,1)}, u32[]{:S(2)}, u32[]{:S(2)}) collective-permute-start(bf16[4,2,768,128]{3,2,1,0:T(8,128)(2,1)S(1)} %pad_maximum_fusion.mine_in), channel_id=1, source_target_pairs={{0,1},{1,0},{2,3},{3,2},{4,5},{5,4},{6,7},{7,6},{8,9},{9,8},{10,11... | collective-permute-start | bytes 4718600 | tf_op jit(solution)/shard_map/ppermute | solution.py:174
  82.8 28.6 %copy-start.5 = (s32[64,2]{0,1:T(2,128)S(1)}, s32[64,2]{0,1:T(2,128)}, u32[]{:S(2)}) copy-start(s32[64,2]{0,1:T(2,128)} %param.7) | copy-start | bytes 1540
  103.5 8.7 %collective-permute-start.5 = (f32[8,24]{1,0:T(8,128)S(1)}, f32[8,24]{1,0:T(8,128)S(1)}, u32[]{:S(2)}, u32[]{:S(2)}) collective-permute-start(f32[8,24]{1,0:T(8,128)S(1)} %bitcast_reduce_fusion), channel_id=1, source_target_pairs={{0,1},{1,0},{2,3},{3,2},{4,5},{5,4},{6,7},{7,6},{8,9},{9,8},{10,11... | collective-permute-start | bytes 2312 | tf_op jit(solution)/shard_map/ppermute | solution.py:174
  112.2 6.0 %collective-permute-start.6 = (f32[8,24]{1,0:T(8,128)S(1)}, f32[8,24]{1,0:T(8,128)S(1)}, u32[]{:S(2)}, u32[]{:S(2)}) collective-permute-start(f32[8,24]{1,0:T(8,128)S(1)} %add.21), channel_id=1, source_target_pairs={{0,2},{1,7},{2,0},{3,5},{4,6},{5,3},{6,4},{7,1},{8,10},{9,15},{10,... | collective-permute-start | bytes 2312 | tf_op jit(solution)/shard_map/ppermute | solution.py:178
  118.2 10.8 %copy-start.7 = (bf16[64,2]{0,1:T(2,128)(2,1)S(1)}, bf16[64,2]{0,1:T(2,128)(2,1)}, u32[]{:S(2)}) copy-start(bf16[64,2]{0,1:T(2,128)(2,1)} %param.8) | copy-start | bytes 772
  118.2 10.7 %collective-permute-start.7 = (f32[8,24]{1,0:T(8,128)S(1)}, f32[8,24]{1,0:T(8,128)S(1)}, u32[]{:S(2)}, u32[]{:S(2)}) collective-permute-start(f32[8,24]{1,0:T(8,128)S(1)} %add.22), channel_id=1, source_target_pairs={{0,6},{1,3},{2,4},{3,1},{4,2},{5,7},{6,0},{7,5},{8,14},{9,11},{10,... | collective-permute-start | bytes 2312 | tf_op jit(solution)/shard_map/ppermute | solution.py:178
  129.6 1.0 copy-start.2
Sparse Core Ops, SparseCore 0:
  27.4 44.3 all-gather.1
  82.9 40.9 reduce-scatter.1

commit v8 on v6

--- a/solution.py
+++ b/solution.py
@@ -15,7 +15,7 @@
 PART = SLOTS // 2
 BF = jnp.bfloat16
 F32 = jnp.float32
-LIMIT = 52 * 2**20
+LIMIT = 24 * 2**20
 WHOLE = pl.BlockSpec()
 CHUNK = SLOTS // 4
 

time: 136 us -> 138 us (1.015)
  local copies, waits for them, and re-layouts: 4.84 us -> 8.17 us
  Pallas kernels: 17.2 us -> 15.4 us
    unnamed x22, local copies, waits for them, and re-layouts: 4.71 us -> 8.04 us
where the time goes in v8:
time: 138 us; the launch traced here: 137 us
  blocking collectives  37.1 us (27%)
  starting transfers between devices  36.2 us (26%)
  waiting for transfers between devices  24.3 us (18%)
  Pallas kernels  15.4 us (11%)
  between operations  14.3 us (10%)
  local copies, waits for them, and re-layouts  8.17 us (6%)
    ppermute x3, starting transfers between devices, swap_core(): return lax.ppermute(x, 'c', [(0, 1), (1, 0)])  20.1 us
    all_to_all x1, blocking collectives, per_device(): lax.all_to_all(dots[0].reshape(NZ * EXPERTS, CAP), ('z', 'y'), split_axis...  19.8 us
    all_to_all x1, blocking collectives, per_device(): lax.all_to_all(packed.reshape(EXPERTS, CAP, width), 'y', split_axis=0, co...  17.4 us
    ppermute x5, starting transfers between devices, swap_x(): lax.ppermute(x, ('x', 'c'), [(i * 2 + c, (i ^ masks[c]) * 2 + c) for i in...  16 us
    ppermute x5, waiting for transfers between devices, swap_x(): lax.ppermute(x, ('x', 'c'), [(i * 2 + c, (i ^ masks[c]) * 2 + c) for i in...  10.7 us
    all_gather x1, waiting for transfers between devices, per_device(): rows = lax.all_gather(own, 'z', axis=0, tiled=True)  8.75 us
    unnamed x22, local copies, waits for them, and re-layouts  8.04 us
    pallas_call x1, Pallas kernels, per_device(): pl.pallas_call(product_body, out_shape=[jax.ShapeDtypeStruct((2 * NX, SLO...  7.2 us
  transfers between devices with their start and end apart: 10, of which 8 were waited for; matrix products, arithmetic and copies ran while one was open for 1% of the time, Pallas kernels for 5%

profile of v8, /device:TPU:1, one launch (start us, length us, event | category | flops | bytes accessed | tf_op | source)
XLA Modules:
  0.0 136.7 jit_solution(12443906432365489381)
XLA Ops:
  9.9 17.4 %all_to_all.14 = bf16[8,24,768]{2,1,0:T(8,128)(2,1)} all-to-all(bf16[8,24,768]{2,1,0:T(8,128)(2,1)S(1)} %bitcast.40), channel_id=1, replica_groups=mesh['y'=8,'z'=8,'x'=4,'c'=2] {'y'}, dimensions={0} | all-to-all | bytes 589824 | tf_op jit(solution)/shard_map/all_to_all | solution.py:135
  27.6 5.6 %collective-permute-start = (bf16[768,128]{1,0:T(8,128)(2,1)S(1)}, bf16[768,128]{1,0:T(8,128)(2,1)S(1)}, u32[]{:S(2)}, u32[]{:S(2)}) collective-permute-start(bf16[768,128]{1,0:T(8,128)(2,1)S(1)} %dynamic-slice_bitcast_fusion), channel_id=1, source_target_pairs={{0,1},{1,0},{2,3},{3,2},{4,5},{5,4},{6,7},{7,6},{8,9},{9,8},{10,11... | collective-permute-start | bytes 589832 | tf_op jit(solution)/shard_map/ppermute | solution.py:123
  33.3 1.0 collective-permute-done
  34.4 4.4 %collective-permute-start.2 = (bf16[2,768,128]{2,1,0:T(8,128)(2,1)S(1)}, bf16[2,768,128]{2,1,0:T(8,128)(2,1)S(1)}, u32[]{:S(2)}, u32[]{:S(2)}) collective-permute-start(bf16[2,768,128]{2,1,0:T(8,128)(2,1)S(1)} %get-tuple-element.23), channel_id=1, source_target_pairs={{0,2},{1,7},{2,0},{3,5},{4,6},{5,3},{6,4},{7,1},{8,10},{9,15},{10,... | collective-permute-start | bytes 1179656 | tf_op jit(solution)/shard_map/ppermute | solution.py:127
  38.8 1.9 %collective-permute-start.1 = (bf16[2,768,128]{2,1,0:T(8,128)(2,1)S(1)}, bf16[2,768,128]{2,1,0:T(8,128)(2,1)S(1)}, u32[]{:S(2)}, u32[]{:S(2)}) collective-permute-start(bf16[2,768,128]{2,1,0:T(8,128)(2,1)S(1)} %get-tuple-element.23), channel_id=1, source_target_pairs={{0,6},{1,3},{2,4},{3,1},{4,2},{5,7},{6,0},{7,5},{8,14},{9,11},{10,... | collective-permute-start | bytes 1179656 | tf_op jit(solution)/shard_map/ppermute | solution.py:127
  40.7 3.4 %collective-permute-done.2 = bf16[2,768,128]{2,1,0:T(8,128)(2,1)S(1)} collective-permute-done((bf16[2,768,128]{2,1,0:T(8,128)(2,1)S(1)}, bf16[2,768,128]{2,1,0:T(8,128)(2,1)S(1)}, u32[]{:S(2)}, u32[]{:S(2)}) %collective-permute-start.2) | collective-permute-done | bytes 393248 | tf_op jit(solution)/shard_map/ppermute | solution.py:127
  44.1 2.9 %collective-permute-start.3 = (bf16[2,768,128]{2,1,0:T(8,128)(2,1)S(1)}, bf16[2,768,128]{2,1,0:T(8,128)(2,1)S(1)}, u32[]{:S(2)}, u32[]{:S(2)}) collective-permute-start(bf16[2,768,128]{2,1,0:T(8,128)(2,1)S(1)} %collective-permute-done.2), channel_id=1, source_target_pairs={{0,6},{1,3},{2,4},{3,1},{4,2},{5,7},{6,0},{7,5},{8,14},{9,11},{10,... | collective-permute-start | bytes 1179656 | tf_op jit(solution)/shard_map/ppermute | solution.py:127
  47.0 1.3 collective-permute-done.1
  48.4 4.7 %collective-permute-done.3 = bf16[2,768,128]{2,1,0:T(8,128)(2,1)S(1)} collective-permute-done((bf16[2,768,128]{2,1,0:T(8,128)(2,1)S(1)}, bf16[2,768,128]{2,1,0:T(8,128)(2,1)S(1)}, u32[]{:S(2)}, u32[]{:S(2)}) %collective-permute-start.3) | collective-permute-done | bytes 393248 | tf_op jit(solution)/shard_map/ppermute | solution.py:127
  53.2 6.6 %collective-permute-start.4 = (bf16[4,2,768,128]{3,2,1,0:T(8,128)(2,1)S(1)}, bf16[4,2,768,128]{3,2,1,0:T(8,128)(2,1)}, u32[]{:S(2)}, u32[]{:S(2)}) collective-permute-start(bf16[4,2,768,128]{3,2,1,0:T(8,128)(2,1)S(1)} %pad_maximum_fusion.mine), channel_id=1, source_target_pairs={{0,1},{1,0},{2,3},{3,2},{4,5},{5,4},{6,7},{7,6},{8,9},{9,8},{10,11... | collective-permute-start | bytes 4718600 | tf_op jit(solution)/shard_map/ppermute | solution.py:123
  59.9 3.1 %collective-permute-done.4.lent = bf16[4,2,768,128]{3,2,1,0:T(8,128)(2,1)} collective-permute-done((bf16[4,2,768,128]{3,2,1,0:T(8,128)(2,1)S(1)}, bf16[4,2,768,128]{3,2,1,0:T(8,128)(2,1)}, u32[]{:S(2)}, u32[]{:S(2)}) %collective-permute-start.4) | collective-permute-done | bytes 1572896 | tf_op jit(solution)/shard_map/ppermute | solution.py:123
  63.0 8.7 %all-gather.2.cloned.1.call-done.rows = bf16[1536,768]{1,0:T(8,128)(2,1)} async-done(((bf16[192,768]{1,0:T(8,128)(2,1)}), bf16[1536,768]{1,0:T(8,128)(2,1)}) %all-gather.2.cloned.1.call-update) | async-done | bytes 2359312 | tf_op jit(solution)/shard_map/all_gather | solution.py:138
  71.8 1.7 %copy-done.8 = bf16[1536,768]{1,0:T(8,128)(2,1)S(1)} copy-done((bf16[1536,768]{1,0:T(8,128)(2,1)S(1)}, bf16[1536,768]{1,0:T(8,128)(2,1)}, u32[]{:S(2)}) %copy-start.8) | copy-done | bytes 2359320
  73.4 1.4 %copy-done.10 = bf16[1024,768]{1,0:T(8,128)(2,1)S(1)} copy-done((bf16[1024,768]{1,0:T(8,128)(2,1)S(1)}, bf16[1024,768]{1,0:T(8,128)(2,1)}, u32[]{:S(2)}) %copy-start.10) | copy-done | bytes 1572888
  74.8 7.2 %shard_map.96 = (bf16[8,1536,128]{2,1,0:T(8,128)(2,1)}, f32[8,1536]{1,0:T(8,128)S(1)}) custom-call(s32[2]{0:T(128)S(1)} %pad_add_fusion.place, bf16[1536,768]{1,0:T(8,128)(2,1)S(1)} %copy-done.8, bf16[1024,768]{1,0:T(8,128)(2,1)S(1)} %copy-done.10, bf16[4,2,768,128]{3,2,1,0:T(8,128)(2,1)S(1)} %pad_maximum_fusion.mine, ...), custom_call_target="tpu_custom_call" | custom-call | flops 2415919104 | bytes 11000000 | tf_op jit(solution)/shard_map/pallas_call | solution.py:162
  82.2 19.8 %all_to_all.15 = f32[64,1,24]{2,1,0:T(1,128)S(1)} all-to-all(f32[64,1,24]{2,1,0:T(1,128)S(1)} %bitcast.50), channel_id=1, replica_groups=mesh['y'=8,'z'=8,'x'=4,'c'=2] {'z','y'}, dimensions={0} | all-to-all | bytes 12288 | tf_op jit(solution)/shard_map/all_to_all | solution.py:188
  102.0 7.9 %collective-permute-start.5 = (f32[8,24]{1,0:T(8,128)S(1)}, f32[8,24]{1,0:T(8,128)S(1)}, u32[]{:S(2)}, u32[]{:S(2)}) collective-permute-start(f32[8,24]{1,0:T(8,128)S(1)} %bitcast_reduce_fusion), channel_id=1, source_target_pairs={{0,1},{1,0},{2,3},{3,2},{4,5},{5,4},{6,7},{7,6},{8,9},{9,8},{10,11... | collective-permute-start | bytes 2312 | tf_op jit(solution)/shard_map/ppermute | solution.py:123
  110.6 4.6 %collective-permute-start.6 = (f32[8,24]{1,0:T(8,128)S(1)}, f32[8,24]{1,0:T(8,128)S(1)}, u32[]{:S(2)}, u32[]{:S(2)}) collective-permute-start(f32[8,24]{1,0:T(8,128)S(1)} %add.21), channel_id=1, source_target_pairs={{0,2},{1,7},{2,0},{3,5},{4,6},{5,3},{6,4},{7,1},{8,10},{9,15},{10,... | collective-permute-start | bytes 2312 | tf_op jit(solution)/shard_map/ppermute | solution.py:127
  115.3 1.3 collective-permute-done.6
  116.6 2.2 %collective-permute-start.7 = (f32[8,24]{1,0:T(8,128)S(1)}, f32[8,24]{1,0:T(8,128)S(1)}, u32[]{:S(2)}, u32[]{:S(2)}) collective-permute-start(f32[8,24]{1,0:T(8,128)S(1)} %add.22), channel_id=1, source_target_pairs={{0,6},{1,3},{2,4},{3,1},{4,2},{5,7},{6,0},{7,5},{8,14},{9,11},{10,... | collective-permute-start | bytes 2312 | tf_op jit(solution)/shard_map/ppermute | solution.py:127
  118.9 1.7 %copy-done.9 = bf16[1536,768]{1,0:T(8,128)(2,1)S(1)} copy-done((bf16[1536,768]{1,0:T(8,128)(2,1)S(1)}, bf16[1536,768]{1,0:T(8,128)(2,1)}, u32[]{:S(2)}) %copy-start.9) | copy-done | bytes 2359320
  120.5 6.2 %shard_map.95 = bf16[1024,768]{1,0:T(8,128)(2,1)} custom-call(s32[2]{0:T(128)S(1)} %pad_add_fusion.place, bf16[1536,768]{1,0:T(8,128)(2,1)S(1)} %copy-done.9, bf16[4,2,768,128]{3,2,1,0:T(8,128)(2,1)S(1)} %pad_maximum_fusion.mine, bf16[4,2,768,128]{3,2,1,0:T(8,128)(2,1)} %collective-permute-done.4.lent), custom_call_target="tpu_custom_call" | custom-call | flops 2415919104 | bytes 8000000 | tf_op jit(solution)/shard_map/pallas_call | solution.py:205
  127.5 1.0 copy-done.2
  128.5 1.3 shard_map.97
  (43 shorter events, 5.1 us)
Async XLA Ops:
  7.2 20.1 %copy-start = (bf16[1536,128]{1,0:T(8,128)(2,1)S(1)}, bf16[1536,128]{1,0:T(8,128)(2,1)}, u32[]{:S(2)}) copy-start(bf16[1536,128]{1,0:T(8,128)(2,1)} %param.10) | copy-start | bytes 1179652
  7.2 20.1 %copy-start.1 = (bf16[1536,128]{1,0:T(8,128)(2,1)S(1)}, bf16[1536,128]{1,0:T(8,128)(2,1)}, u32[]{:S(2)}) copy-start(bf16[1536,128]{1,0:T(8,128)(2,1)} %param.11) | copy-start | bytes 1179652
  7.2 64.6 %all-gather.2.cloned.1.call-start = ((), (), s32[]{:S(2)}) async-start(), calls=%async_computation.3 | async-start | bytes 2654208 | tf_op jit(solution)/shard_map/all_gather | solution.py:138
  7.2 1.0 copy-start.3
  8.2 0.7 copy-start.4
  8.9 0.7 copy-start.6
  27.2 100.3 %reduce-scatter.2.cloned.1.call-start = ((), (), s32[]{:S(2)}) async-start(), calls=%async_computation.4 | async-start | bytes 3538944 | tf_op jit(solution)/shard_map/reduce_scatter | solution.py:183
  27.6 6.7 %collective-permute-start = (bf16[768,128]{1,0:T(8,128)(2,1)S(1)}, bf16[768,128]{1,0:T(8,128)(2,1)S(1)}, u32[]{:S(2)}, u32[]{:S(2)}) collective-permute-start(bf16[768,128]{1,0:T(8,128)(2,1)S(1)} %dynamic-slice_bitcast_fusion), channel_id=1, source_target_pairs={{0,1},{1,0},{2,3},{3,2},{4,5},{5,4},{6,7},{7,6},{8,9},{9,8},{10,11... | collective-permute-start | bytes 589832 | tf_op jit(solution)/shard_map/ppermute | solution.py:123
  34.4 9.7 %collective-permute-start.2 = (bf16[2,768,128]{2,1,0:T(8,128)(2,1)S(1)}, bf16[2,768,128]{2,1,0:T(8,128)(2,1)S(1)}, u32[]{:S(2)}, u32[]{:S(2)}) collective-permute-start(bf16[2,768,128]{2,1,0:T(8,128)(2,1)S(1)} %get-tuple-element.23), channel_id=1, source_target_pairs={{0,2},{1,7},{2,0},{3,5},{4,6},{5,3},{6,4},{7,1},{8,10},{9,15},{10,... | collective-permute-start | bytes 1179656 | tf_op jit(solution)/shard_map/ppermute | solution.py:127
  38.8 9.6 %collective-permute-start.1 = (bf16[2,768,128]{2,1,0:T(8,128)(2,1)S(1)}, bf16[2,768,128]{2,1,0:T(8,128)(2,1)S(1)}, u32[]{:S(2)}, u32[]{:S(2)}) collective-permute-start(bf16[2,768,128]{2,1,0:T(8,128)(2,1)S(1)} %get-tuple-element.23), channel_id=1, source_target_pairs={{0,6},{1,3},{2,4},{3,1},{4,2},{5,7},{6,0},{7,5},{8,14},{9,11},{10,... | collective-permute-start | bytes 1179656 | tf_op jit(solution)/shard_map/ppermute | solution.py:127
  44.1 8.9 %collective-permute-start.3 = (bf16[2,768,128]{2,1,0:T(8,128)(2,1)S(1)}, bf16[2,768,128]{2,1,0:T(8,128)(2,1)S(1)}, u32[]{:S(2)}, u32[]{:S(2)}) collective-permute-start(bf16[2,768,128]{2,1,0:T(8,128)(2,1)S(1)} %collective-permute-done.2), channel_id=1, source_target_pairs={{0,6},{1,3},{2,4},{3,1},{4,2},{5,7},{6,0},{7,5},{8,14},{9,11},{10,... | collective-permute-start | bytes 1179656 | tf_op jit(solution)/shard_map/ppermute | solution.py:127
  53.2 9.8 %collective-permute-start.4 = (bf16[4,2,768,128]{3,2,1,0:T(8,128)(2,1)S(1)}, bf16[4,2,768,128]{3,2,1,0:T(8,128)(2,1)}, u32[]{:S(2)}, u32[]{:S(2)}) collective-permute-start(bf16[4,2,768,128]{3,2,1,0:T(8,128)(2,1)S(1)} %pad_maximum_fusion.mine), channel_id=1, source_target_pairs={{0,1},{1,0},{2,3},{3,2},{4,5},{5,4},{6,7},{7,6},{8,9},{9,8},{10,11... | collective-permute-start | bytes 4718600 | tf_op jit(solution)/shard_map/ppermute | solution.py:123
  71.8 1.7 %copy-start.8 = (bf16[1536,768]{1,0:T(8,128)(2,1)S(1)}, bf16[1536,768]{1,0:T(8,128)(2,1)}, u32[]{:S(2)}) copy-start(bf16[1536,768]{1,0:T(8,128)(2,1)} %all-gather.2.cloned.1.call-done.rows) | copy-start | bytes 7077892
  73.4 1.4 %copy-start.10 = (bf16[1024,768]{1,0:T(8,128)(2,1)S(1)}, bf16[1024,768]{1,0:T(8,128)(2,1)}, u32[]{:S(2)}) copy-start(bf16[1024,768]{1,0:T(8,128)(2,1)} %w.1) | copy-start | bytes 4718596
  82.0 27.8 %copy-start.5 = (s32[64,2]{0,1:T(2,128)S(1)}, s32[64,2]{0,1:T(2,128)}, u32[]{:S(2)}) copy-start(s32[64,2]{0,1:T(2,128)} %param.7) | copy-start | bytes 1540
  102.0 8.7 %collective-permute-start.5 = (f32[8,24]{1,0:T(8,128)S(1)}, f32[8,24]{1,0:T(8,128)S(1)}, u32[]{:S(2)}, u32[]{:S(2)}) collective-permute-start(f32[8,24]{1,0:T(8,128)S(1)} %bitcast_reduce_fusion), channel_id=1, source_target_pairs={{0,1},{1,0},{2,3},{3,2},{4,5},{5,4},{6,7},{7,6},{8,9},{9,8},{10,11... | collective-permute-start | bytes 2312 | tf_op jit(solution)/shard_map/ppermute | solution.py:123
  110.6 6.0 %collective-permute-start.6 = (f32[8,24]{1,0:T(8,128)S(1)}, f32[8,24]{1,0:T(8,128)S(1)}, u32[]{:S(2)}, u32[]{:S(2)}) collective-permute-start(f32[8,24]{1,0:T(8,128)S(1)} %add.21), channel_id=1, source_target_pairs={{0,2},{1,7},{2,0},{3,5},{4,6},{5,3},{6,4},{7,1},{8,10},{9,15},{10,... | collective-permute-start | bytes 2312 | tf_op jit(solution)/shard_map/ppermute | solution.py:127
  116.6 10.3 %copy-start.7 = (bf16[64,2]{0,1:T(2,128)(2,1)S(1)}, bf16[64,2]{0,1:T(2,128)(2,1)}, u32[]{:S(2)}) copy-start(bf16[64,2]{0,1:T(2,128)(2,1)} %param.8) | copy-start | bytes 772
  116.6 10.2 %collective-permute-start.7 = (f32[8,24]{1,0:T(8,128)S(1)}, f32[8,24]{1,0:T(8,128)S(1)}, u32[]{:S(2)}, u32[]{:S(2)}) collective-permute-start(f32[8,24]{1,0:T(8,128)S(1)} %add.22), channel_id=1, source_target_pairs={{0,6},{1,3},{2,4},{3,1},{4,2},{5,7},{6,0},{7,5},{8,14},{9,11},{10,... | collective-permute-start | bytes 2312 | tf_op jit(solution)/shard_map/ppermute | solution.py:127
  118.9 1.7 %copy-start.9 = (bf16[1536,768]{1,0:T(8,128)(2,1)S(1)}, bf16[1536,768]{1,0:T(8,128)(2,1)}, u32[]{:S(2)}) copy-start(bf16[1536,768]{1,0:T(8,128)(2,1)} %all-gather.2.cloned.1.call-done.rows) | copy-start | bytes 7077892
  127.5 1.0 copy-start.2
Sparse Core Ops, SparseCore 0:
  27.4 44.3 all-gather.1
  82.2 40.7 reduce-scatter.1

commit v9 on v6

--- a/solution.py
+++ b/solution.py
@@ -186,9 +186,10 @@
     )
 
     back = lax.all_to_all(
-        dots[0].reshape(NZ * EXPERTS, CAP), ("z", "y"), split_axis=0, concat_axis=0, tiled=True
-    )
-    totals = jnp.sum(back.reshape(NZ, EXPERTS, CAP), axis=0)
+        dots[0].reshape(NZ, EXPERTS, CAP).transpose(1, 0, 2).reshape(EXPERTS * NZ, CAP),
+        ("y", "z"), split_axis=0, concat_axis=0, tiled=True,
+    )
+    totals = jnp.sum(back.reshape(EXPERTS, NZ, CAP), axis=1)
     totals = totals + swap_core(totals)
     totals = totals + swap_x(totals, True)
     totals = totals + swap_x(totals, False)

time: 136 us -> 136 us (level)
  no operation moved by 1% of the time
where the time goes in v9:
time: 136 us; the launch traced here: 135 us
  blocking collectives  37.3 us (27%)
  starting transfers between devices  36.2 us (27%)
  waiting for transfers between devices  24.3 us (18%)
  Pallas kernels  17.2 us (13%)
  between operations  14.3 us (11%)
  local copies, waits for them, and re-layouts  4.84 us (4%)
    ppermute x3, starting transfers between devices, swap_core(): return lax.ppermute(x, 'c', [(0, 1), (1, 0)])  20.1 us
    all_to_all x1, blocking collectives, per_device(): lax.all_to_all(dots[0].reshape(NZ, EXPERTS, CAP).transpose(1, 0, 2).resha...  19.9 us
    all_to_all x1, blocking collectives, per_device(): lax.all_to_all(packed.reshape(EXPERTS, CAP, width), 'y', split_axis=0, co...  17.4 us
    ppermute x5, starting transfers between devices, swap_x(): lax.ppermute(x, ('x', 'c'), [(i * 2 + c, (i ^ masks[c]) * 2 + c) for i in...  16 us
    ppermute x5, waiting for transfers between devices, swap_x(): lax.ppermute(x, ('x', 'c'), [(i * 2 + c, (i ^ masks[c]) * 2 + c) for i in...  10.7 us
    all_gather x1, waiting for transfers between devices, per_device(): rows = lax.all_gather(own, 'z', axis=0, tiled=True)  8.74 us
    pallas_call x1, Pallas kernels, per_device(): pl.pallas_call(product_body, out_shape=[jax.ShapeDtypeStruct((2 * NX, SLO...  8.25 us
    pallas_call x1, Pallas kernels, per_device(): pl.pallas_call(weight_body, out_shape=jax.ShapeDtypeStruct((ff, width), B...  7.05 us
  transfers between devices with their start and end apart: 10, of which 8 were waited for; matrix products, arithmetic and copies ran while one was open for 1% of the time, Pallas kernels for 5%

profile of v9, /device:TPU:1, one launch (start us, length us, event | category | flops | bytes accessed | tf_op | source)
XLA Modules:
  0.0 135.4 jit_solution(5543070113282963641)
XLA Ops:
  7.2 0.9 copy-done.5
  9.9 17.4 %all_to_all.14 = bf16[8,24,768]{2,1,0:T(8,128)(2,1)} all-to-all(bf16[8,24,768]{2,1,0:T(8,128)(2,1)S(1)} %bitcast.44), channel_id=1, replica_groups=mesh['y'=8,'z'=8,'x'=4,'c'=2] {'y'}, dimensions={0} | all-to-all | bytes 589824 | tf_op jit(solution)/shard_map/all_to_all | solution.py:135
  27.6 5.6 %collective-permute-start = (bf16[768,128]{1,0:T(8,128)(2,1)S(1)}, bf16[768,128]{1,0:T(8,128)(2,1)S(1)}, u32[]{:S(2)}, u32[]{:S(2)}) collective-permute-start(bf16[768,128]{1,0:T(8,128)(2,1)S(1)} %dynamic-slice_bitcast_fusion), channel_id=1, source_target_pairs={{0,1},{1,0},{2,3},{3,2},{4,5},{5,4},{6,7},{7,6},{8,9},{9,8},{10,11... | collective-permute-start | bytes 589832 | tf_op jit(solution)/shard_map/ppermute | solution.py:123
  33.3 1.0 collective-permute-done
  34.4 4.4 %collective-permute-start.2 = (bf16[2,768,128]{2,1,0:T(8,128)(2,1)S(1)}, bf16[2,768,128]{2,1,0:T(8,128)(2,1)S(1)}, u32[]{:S(2)}, u32[]{:S(2)}) collective-permute-start(bf16[2,768,128]{2,1,0:T(8,128)(2,1)S(1)} %get-tuple-element.23), channel_id=1, source_target_pairs={{0,2},{1,7},{2,0},{3,5},{4,6},{5,3},{6,4},{7,1},{8,10},{9,15},{10,... | collective-permute-start | bytes 1179656 | tf_op jit(solution)/shard_map/ppermute | solution.py:127
  38.8 1.9 %collective-permute-start.1 = (bf16[2,768,128]{2,1,0:T(8,128)(2,1)S(1)}, bf16[2,768,128]{2,1,0:T(8,128)(2,1)S(1)}, u32[]{:S(2)}, u32[]{:S(2)}) collective-permute-start(bf16[2,768,128]{2,1,0:T(8,128)(2,1)S(1)} %get-tuple-element.23), channel_id=1, source_target_pairs={{0,6},{1,3},{2,4},{3,1},{4,2},{5,7},{6,0},{7,5},{8,14},{9,11},{10,... | collective-permute-start | bytes 1179656 | tf_op jit(solution)/shard_map/ppermute | solution.py:127
  40.7 3.4 %collective-permute-done.2 = bf16[2,768,128]{2,1,0:T(8,128)(2,1)S(1)} collective-permute-done((bf16[2,768,128]{2,1,0:T(8,128)(2,1)S(1)}, bf16[2,768,128]{2,1,0:T(8,128)(2,1)S(1)}, u32[]{:S(2)}, u32[]{:S(2)}) %collective-permute-start.2) | collective-permute-done | bytes 393248 | tf_op jit(solution)/shard_map/ppermute | solution.py:127
  44.1 2.9 %collective-permute-start.3 = (bf16[2,768,128]{2,1,0:T(8,128)(2,1)S(1)}, bf16[2,768,128]{2,1,0:T(8,128)(2,1)S(1)}, u32[]{:S(2)}, u32[]{:S(2)}) collective-permute-start(bf16[2,768,128]{2,1,0:T(8,128)(2,1)S(1)} %collective-permute-done.2), channel_id=1, source_target_pairs={{0,6},{1,3},{2,4},{3,1},{4,2},{5,7},{6,0},{7,5},{8,14},{9,11},{10,... | collective-permute-start | bytes 1179656 | tf_op jit(solution)/shard_map/ppermute | solution.py:127
  47.0 1.3 collective-permute-done.1
  48.4 4.7 %collective-permute-done.3 = bf16[2,768,128]{2,1,0:T(8,128)(2,1)S(1)} collective-permute-done((bf16[2,768,128]{2,1,0:T(8,128)(2,1)S(1)}, bf16[2,768,128]{2,1,0:T(8,128)(2,1)S(1)}, u32[]{:S(2)}, u32[]{:S(2)}) %collective-permute-start.3) | collective-permute-done | bytes 393248 | tf_op jit(solution)/shard_map/ppermute | solution.py:127
  53.3 6.6 %collective-permute-start.4 = (bf16[4,2,768,128]{3,2,1,0:T(8,128)(2,1)S(1)}, bf16[4,2,768,128]{3,2,1,0:T(8,128)(2,1)}, u32[]{:S(2)}, u32[]{:S(2)}) collective-permute-start(bf16[4,2,768,128]{3,2,1,0:T(8,128)(2,1)S(1)} %pad_maximum_fusion.mine), channel_id=1, source_target_pairs={{0,1},{1,0},{2,3},{3,2},{4,5},{5,4},{6,7},{7,6},{8,9},{9,8},{10,11... | collective-permute-start | bytes 4718600 | tf_op jit(solution)/shard_map/ppermute | solution.py:123
  60.0 3.1 %collective-permute-done.4.lent = bf16[4,2,768,128]{3,2,1,0:T(8,128)(2,1)} collective-permute-done((bf16[4,2,768,128]{3,2,1,0:T(8,128)(2,1)S(1)}, bf16[4,2,768,128]{3,2,1,0:T(8,128)(2,1)}, u32[]{:S(2)}, u32[]{:S(2)}) %collective-permute-start.4) | collective-permute-done | bytes 1572896 | tf_op jit(solution)/shard_map/ppermute | solution.py:123
  63.0 8.7 %all-gather.2.cloned.1.call-done.rows = bf16[1536,768]{1,0:T(8,128)(2,1)} async-done(((bf16[192,768]{1,0:T(8,128)(2,1)}), bf16[1536,768]{1,0:T(8,128)(2,1)}) %all-gather.2.cloned.1.call-update) | async-done | bytes 2359312 | tf_op jit(solution)/shard_map/all_gather | solution.py:138
  71.8 1.4 %copy-done.10 = bf16[1024,768]{1,0:T(8,128)(2,1)S(1)} copy-done((bf16[1024,768]{1,0:T(8,128)(2,1)S(1)}, bf16[1024,768]{1,0:T(8,128)(2,1)}, u32[]{:S(2)}) %copy-start.10) | copy-done | bytes 1572888
  73.2 8.3 %shard_map.96 = (bf16[8,1536,128]{2,1,0:T(8,128)(2,1)}, f32[8,1536]{1,0:T(8,128)S(1)}) custom-call(s32[2]{0:T(128)S(1)} %pad_add_fusion.place, bf16[1536,768]{1,0:T(8,128)(2,1)} %all-gather.2.cloned.1.call-done.rows, bf16[1024,768]{1,0:T(8,128)(2,1)S(1)} %copy-done.10, bf16[4,2,768,128]{3,2,1,0:T(8,128)(2,1)} %copy-done, ...), custom_call_target="tpu_custom_call" | custom-call | flops 2415919104 | bytes 11000000 | tf_op jit(solution)/shard_map/pallas_call | solution.py:162
  81.6 19.9 %all_to_all.15 = f32[64,1,24]{2,1,0:T(1,128)S(1)} all-to-all(f32[64,1,24]{2,1,0:T(1,128)S(1)} %bitcast.54), channel_id=1, replica_groups=mesh['y'=8,'z'=8,'x'=4,'c'=2] {'y','z'}, dimensions={0} | all-to-all | bytes 12288 | tf_op jit(solution)/shard_map/all_to_all | solution.py:188
  101.5 7.9 %collective-permute-start.5 = (f32[8,24]{1,0:T(8,128)S(1)}, f32[8,24]{1,0:T(8,128)S(1)}, u32[]{:S(2)}, u32[]{:S(2)}) collective-permute-start(f32[8,24]{1,0:T(8,128)S(1)} %bitcast_reduce_fusion), channel_id=1, source_target_pairs={{0,1},{1,0},{2,3},{3,2},{4,5},{5,4},{6,7},{7,6},{8,9},{9,8},{10,11... | collective-permute-start | bytes 2312 | tf_op jit(solution)/shard_map/ppermute | solution.py:123
  109.4 0.8 collective-permute-done.5
  110.2 4.6 %collective-permute-start.6 = (f32[8,24]{1,0:T(8,128)S(1)}, f32[8,24]{1,0:T(8,128)S(1)}, u32[]{:S(2)}, u32[]{:S(2)}) collective-permute-start(f32[8,24]{1,0:T(8,128)S(1)} %add.21), channel_id=1, source_target_pairs={{0,2},{1,7},{2,0},{3,5},{4,6},{5,3},{6,4},{7,1},{8,10},{9,15},{10,... | collective-permute-start | bytes 2312 | tf_op jit(solution)/shard_map/ppermute | solution.py:127
  114.9 1.3 collective-permute-done.6
  116.2 2.3 %collective-permute-start.7 = (f32[8,24]{1,0:T(8,128)S(1)}, f32[8,24]{1,0:T(8,128)S(1)}, u32[]{:S(2)}, u32[]{:S(2)}) collective-permute-start(f32[8,24]{1,0:T(8,128)S(1)} %add.22), channel_id=1, source_target_pairs={{0,6},{1,3},{2,4},{3,1},{4,2},{5,7},{6,0},{7,5},{8,14},{9,11},{10,... | collective-permute-start | bytes 2312 | tf_op jit(solution)/shard_map/ppermute | solution.py:127
  118.4 7.0 %shard_map.95 = bf16[1024,768]{1,0:T(8,128)(2,1)} custom-call(s32[2]{0:T(128)S(1)} %pad_add_fusion.place, bf16[1536,768]{1,0:T(8,128)(2,1)} %all-gather.2.cloned.1.call-done.rows, bf16[4,2,768,128]{3,2,1,0:T(8,128)(2,1)S(1)} %copy-done.1, bf16[4,2,768,128]{3,2,1,0:T(8,128)(2,1)} %collective-permute-done.4.lent), custom_call_target="tpu_custom_call" | custom-call | flops 2415919104 | bytes 8000000 | tf_op jit(solution)/shard_map/pallas_call | solution.py:206
  126.2 1.0 copy-done.4
  127.2 1.3 shard_map.97
  (44 shorter events, 3.4 us)
Async XLA Ops:
  7.2 20.1 %copy-start.2 = (bf16[1536,128]{1,0:T(8,128)(2,1)S(1)}, bf16[1536,128]{1,0:T(8,128)(2,1)}, u32[]{:S(2)}) copy-start(bf16[1536,128]{1,0:T(8,128)(2,1)} %param.10) | copy-start | bytes 1179652
  7.2 20.1 %copy-start.3 = (bf16[1536,128]{1,0:T(8,128)(2,1)S(1)}, bf16[1536,128]{1,0:T(8,128)(2,1)}, u32[]{:S(2)}) copy-start(bf16[1536,128]{1,0:T(8,128)(2,1)} %param.11) | copy-start | bytes 1179652
  7.2 64.6 %all-gather.2.cloned.1.call-start = ((), (), s32[]{:S(2)}) async-start(), calls=%async_computation.3 | async-start | bytes 2654208 | tf_op jit(solution)/shard_map/all_gather | solution.py:138
  7.2 1.0 copy-start.5
  8.2 0.7 copy-start.6
  8.9 0.7 copy-start.8
  27.2 98.9 %reduce-scatter.2.cloned.1.call-start = ((), (), s32[]{:S(2)}) async-start(), calls=%async_computation.4 | async-start | bytes 3538944 | tf_op jit(solution)/shard_map/reduce_scatter | solution.py:183
  27.6 6.7 %collective-permute-start = (bf16[768,128]{1,0:T(8,128)(2,1)S(1)}, bf16[768,128]{1,0:T(8,128)(2,1)S(1)}, u32[]{:S(2)}, u32[]{:S(2)}) collective-permute-start(bf16[768,128]{1,0:T(8,128)(2,1)S(1)} %dynamic-slice_bitcast_fusion), channel_id=1, source_target_pairs={{0,1},{1,0},{2,3},{3,2},{4,5},{5,4},{6,7},{7,6},{8,9},{9,8},{10,11... | collective-permute-start | bytes 589832 | tf_op jit(solution)/shard_map/ppermute | solution.py:123
  34.4 9.7 %collective-permute-start.2 = (bf16[2,768,128]{2,1,0:T(8,128)(2,1)S(1)}, bf16[2,768,128]{2,1,0:T(8,128)(2,1)S(1)}, u32[]{:S(2)}, u32[]{:S(2)}) collective-permute-start(bf16[2,768,128]{2,1,0:T(8,128)(2,1)S(1)} %get-tuple-element.23), channel_id=1, source_target_pairs={{0,2},{1,7},{2,0},{3,5},{4,6},{5,3},{6,4},{7,1},{8,10},{9,15},{10,... | collective-permute-start | bytes 1179656 | tf_op jit(solution)/shard_map/ppermute | solution.py:127
  38.8 9.6 %collective-permute-start.1 = (bf16[2,768,128]{2,1,0:T(8,128)(2,1)S(1)}, bf16[2,768,128]{2,1,0:T(8,128)(2,1)S(1)}, u32[]{:S(2)}, u32[]{:S(2)}) collective-permute-start(bf16[2,768,128]{2,1,0:T(8,128)(2,1)S(1)} %get-tuple-element.23), channel_id=1, source_target_pairs={{0,6},{1,3},{2,4},{3,1},{4,2},{5,7},{6,0},{7,5},{8,14},{9,11},{10,... | collective-permute-start | bytes 1179656 | tf_op jit(solution)/shard_map/ppermute | solution.py:127
  44.1 8.9 %collective-permute-start.3 = (bf16[2,768,128]{2,1,0:T(8,128)(2,1)S(1)}, bf16[2,768,128]{2,1,0:T(8,128)(2,1)S(1)}, u32[]{:S(2)}, u32[]{:S(2)}) collective-permute-start(bf16[2,768,128]{2,1,0:T(8,128)(2,1)S(1)} %collective-permute-done.2), channel_id=1, source_target_pairs={{0,6},{1,3},{2,4},{3,1},{4,2},{5,7},{6,0},{7,5},{8,14},{9,11},{10,... | collective-permute-start | bytes 1179656 | tf_op jit(solution)/shard_map/ppermute | solution.py:127
  53.2 18.5 %copy-start = (bf16[4,2,768,128]{3,2,1,0:T(8,128)(2,1)}, bf16[4,2,768,128]{3,2,1,0:T(8,128)(2,1)S(1)}, u32[]{:S(2)}) copy-start(bf16[4,2,768,128]{3,2,1,0:T(8,128)(2,1)S(1)} %pad_maximum_fusion.mine) | copy-start | bytes 4718596
  53.3 9.8 %collective-permute-start.4 = (bf16[4,2,768,128]{3,2,1,0:T(8,128)(2,1)S(1)}, bf16[4,2,768,128]{3,2,1,0:T(8,128)(2,1)}, u32[]{:S(2)}, u32[]{:S(2)}) collective-permute-start(bf16[4,2,768,128]{3,2,1,0:T(8,128)(2,1)S(1)} %pad_maximum_fusion.mine), channel_id=1, source_target_pairs={{0,1},{1,0},{2,3},{3,2},{4,5},{5,4},{6,7},{7,6},{8,9},{9,8},{10,11... | collective-permute-start | bytes 4718600 | tf_op jit(solution)/shard_map/ppermute | solution.py:123
  71.8 1.4 %copy-start.10 = (bf16[1024,768]{1,0:T(8,128)(2,1)S(1)}, bf16[1024,768]{1,0:T(8,128)(2,1)}, u32[]{:S(2)}) copy-start(bf16[1024,768]{1,0:T(8,128)(2,1)} %w.1) | copy-start | bytes 4718596
  81.4 27.9 %copy-start.7 = (s32[64,2]{0,1:T(2,128)S(1)}, s32[64,2]{0,1:T(2,128)}, u32[]{:S(2)}) copy-start(s32[64,2]{0,1:T(2,128)} %param.7) | copy-start | bytes 1540
  81.4 37.0 %copy-start.1 = (bf16[4,2,768,128]{3,2,1,0:T(8,128)(2,1)S(1)}, bf16[4,2,768,128]{3,2,1,0:T(8,128)(2,1)}, u32[]{:S(2)}) copy-start(bf16[4,2,768,128]{3,2,1,0:T(8,128)(2,1)} %copy-done) | copy-start | bytes 4718596
  101.5 8.7 %collective-permute-start.5 = (f32[8,24]{1,0:T(8,128)S(1)}, f32[8,24]{1,0:T(8,128)S(1)}, u32[]{:S(2)}, u32[]{:S(2)}) collective-permute-start(f32[8,24]{1,0:T(8,128)S(1)} %bitcast_reduce_fusion), channel_id=1, source_target_pairs={{0,1},{1,0},{2,3},{3,2},{4,5},{5,4},{6,7},{7,6},{8,9},{9,8},{10,11... | collective-permute-start | bytes 2312 | tf_op jit(solution)/shard_map/ppermute | solution.py:123
  110.2 6.0 %collective-permute-start.6 = (f32[8,24]{1,0:T(8,128)S(1)}, f32[8,24]{1,0:T(8,128)S(1)}, u32[]{:S(2)}, u32[]{:S(2)}) collective-permute-start(f32[8,24]{1,0:T(8,128)S(1)} %add.21), channel_id=1, source_target_pairs={{0,2},{1,7},{2,0},{3,5},{4,6},{5,3},{6,4},{7,1},{8,10},{9,15},{10,... | collective-permute-start | bytes 2312 | tf_op jit(solution)/shard_map/ppermute | solution.py:127
  116.2 9.5 %copy-start.9 = (bf16[64,2]{0,1:T(2,128)(2,1)S(1)}, bf16[64,2]{0,1:T(2,128)(2,1)}, u32[]{:S(2)}) copy-start(bf16[64,2]{0,1:T(2,128)(2,1)} %param.8) | copy-start | bytes 772
  116.2 9.3 %collective-permute-start.7 = (f32[8,24]{1,0:T(8,128)S(1)}, f32[8,24]{1,0:T(8,128)S(1)}, u32[]{:S(2)}, u32[]{:S(2)}) collective-permute-start(f32[8,24]{1,0:T(8,128)S(1)} %add.22), channel_id=1, source_target_pairs={{0,6},{1,3},{2,4},{3,1},{4,2},{5,7},{6,0},{7,5},{8,14},{9,11},{10,... | collective-permute-start | bytes 2312 | tf_op jit(solution)/shard_map/ppermute | solution.py:127
  126.2 1.0 copy-start.4
Sparse Core Ops, SparseCore 0:
  27.4 44.3 all-gather.1
  81.6 40.8 reduce-scatter.1
